TPU v7x, 32 devices: a whole 2x2x4 slice. The times are simulated.
32 devices in a mesh: groups: 2 (over x), ctx: 16 (over z, y, core).
Axes of the slice: x: 2, y: 2, z: 4, core: 2. Of those that a mesh axis runs over, the one named last changes fastest.
Arguments:
- queries: bfloat16 [2048, 64, 576], P(('groups', 'ctx')), parts along dimension 0, may hold values from -26 to 26
- latent_cache: bfloat16 [8192, 576], P(('groups', 'ctx')), parts along dimension 0, may hold values from -6 to 6
- tile_lists: int32 [32, 32], P(('groups', 'ctx')), parts along dimension 0, may hold values from -1 to 63, as said below
Outputs:
- attended: bfloat16 [2048, 64, 512], P(('groups', 'ctx')), parts along dimension 0
There are 2 independent parts, one for each index of `groups`. A program takes and returns all parts, laid end to end along the dimension named above; each array names one. Nothing has to cross between parts.
Inputs may be any that keep to these rules, and one draw needn't show every extreme that they name: `tile_lists`: each row names distinct tiles that end at or before the block's own last tile 4 * b + 3, which is always named; no row names more than 1 tiles held by one device, and exactly 1 of the block's own device; valid entries come first, then -1; row b has min(32, 1 * (b + 1)) valid entries.
All inputs are finite; a program needn't handle non-finite values.
Results may differ from a plain program's by a relative error of at most 0.0034.
Values may be sent and summed in bfloat16 or wider, within the bound.
No kernel may reach another device: no remote copies, remote signals or barrier semaphores. Data moves between devices by JAX's collectives and lax.ppermute only.
A program may use at most 128 MiB of HBM per device.

v0:
```python
import jax
import jax.numpy as jnp
from jax import lax
from jax.sharding import PartitionSpec as P

LAT = 512
TILE = 64
TOPK = 32
CAP = 1
TILES_DEV = 4


softmax_scale = 192.0 ** (-0.5)


def slot_ranks(holders):
    same = (holders[:, None] == holders[None, :]) & (holders[:, None] >= 0)
    count = holders.shape[0]
    earlier = (
        jnp.arange(count, dtype=jnp.int32)[:, None] < jnp.arange(count, dtype=jnp.int32)[None, :]
    )
    return jnp.sum((same & earlier).astype(jnp.int32), axis=0)


def slot_table(match, ranks, local_tile):
    slots = jnp.arange(CAP, dtype=jnp.int32)
    hits = match[..., None] & (ranks[..., None] == slots)
    return jnp.sum(jnp.where(hits, local_tile[..., None] + 1, 0), axis=-2) - 1


def shards(queries, latent_cache, tile_lists):
    width = latent_cache.shape[1]
    listing = tile_lists[0]
    me = lax.axis_index("ctx")
    valid = listing >= 0
    flat_cache = latent_cache.reshape(TILES_DEV, TILE * width)
    peers = lax.axis_size("ctx")
    holders = jnp.where(valid, listing // TILES_DEV, -1)
    ranks = slot_ranks(holders)
    lists_all = lax.all_gather(tile_lists, "ctx", axis=0, tiled=True)
    holders_all = jnp.where(lists_all >= 0, lists_all // TILES_DEV, -1)
    ranks_all = jax.vmap(slot_ranks)(holders_all)
    wanted = slot_table(holders_all == me, ranks_all, lists_all % TILES_DEV)
    outgoing = jnp.take(flat_cache, jnp.clip(wanted, 0, TILES_DEV - 1), axis=0)
    outgoing = jnp.where((wanted >= 0)[..., None], outgoing, jnp.zeros_like(outgoing))
    incoming = lax.all_to_all(outgoing, "ctx", split_axis=0, concat_axis=0, tiled=True)
    incoming = incoming.reshape(peers * CAP, TILE * width)
    position = jnp.clip(holders, 0, peers - 1) * CAP + jnp.clip(ranks, 0, CAP - 1)
    keys = jnp.take(incoming, position, axis=0)
    keys = keys.reshape(TOPK * TILE, width)
    safe = jnp.clip(listing, 0, None)
    offsets = jnp.arange(TILE, dtype=jnp.int32)
    key_pos = (safe[:, None] * TILE + offsets[None, :]).reshape(-1)
    key_ok = jnp.repeat(valid, TILE)
    q_count = queries.shape[0]
    context_dev = TILES_DEV * TILE
    query_pos = me * context_dev + context_dev - q_count + jnp.arange(q_count, dtype=jnp.int32)
    scores = (
        jnp.einsum("qhc,kc->qhk", queries, keys, preferred_element_type=jnp.float32) * softmax_scale
    )
    allowed = (key_ok[None, :] & (key_pos[None, :] <= query_pos[:, None]))[:, None, :]
    scores = jnp.where(allowed, scores, -1e30)
    top = jnp.max(scores, axis=-1, keepdims=True)
    expo = jnp.where(allowed, jnp.exp(scores - top), 0.0)
    total = jnp.sum(expo, axis=-1, keepdims=True)
    weights = expo.astype(jnp.bfloat16)
    summed = jnp.einsum("qhk,kc->qhc", weights, keys[:, :LAT], preferred_element_type=jnp.float32)
    return (summed / total).astype(jnp.bfloat16)


def solution(mesh):
    placed = (
        P(("groups", "ctx"), None, None),
        P(("groups", "ctx"), None),
        P(("groups", "ctx"), None),
    )
    return jax.shard_map(
        shards,
        mesh=mesh,
        in_specs=placed,
        out_specs=P(("groups", "ctx"), None, None),
        check_vma=False,
    )
```

profile of v0, /device:TPU:25, one launch (start us, length us, event | category | flops | bytes accessed | tf_op | source)
XLA Modules:
  0.0 137.3 jit_solution(12244981570889057884)
XLA Ops:
  0.0 17.3 %all-gather = s32[16,1,32]{2,1,0:T(1,128)S(1)} all-gather(s32[1,1,32]{2,1,0:T(1,128)} %bitcast.70), channel_id=1, replica_groups=mesh['groups'=2,'ctx'=16] {'ctx'}, dimensions={0}, use_global_device_ids=true | all-gather | bytes 2176 | tf_op jit(solution)/shard_map/all_gather | solution.py:40
  17.4 0.2 convert_reduce_fusion
  17.6 0.1 fusion.15
  17.8 1.2 copy.14
  18.9 0.4 reshape.335
  19.4 1.3 gather_fusion
  20.7 0.2 fusion.11
  20.9 0.5 broadcast.492
  21.4 1.5 %reduce.2 = bf16[16,36864]{1,0:T(8,128)(2,1)S(1)} reduce(bf16[16,1,36864]{2,0,1:T(8,128)(2,1)S(1)} %fusion.11, bf16[]{:T(256)} %broadcast.492), dimensions={1}, to_apply=%copy.15.reduce_sub_computation | reduce | bytes 2359298 | tf_op jit(solution)/shard_map/jit(_where)/select_n | solution.py:45
  23.0 1.7 %reshape.357 = bf16[16,2,18432]{2,1,0:T(2,128)(2,1)} reshape(bf16[16,36864]{1,0:T(8,128)(2,1)S(1)} %reduce.2) | data formatting | bytes 2359296
  24.7 8.5 %all-to-all-start = ((bf16[16,2,18432]{2,1,0:T(2,128)(2,1)}), bf16[16,2,18432]{2,1,0:T(2,128)(2,1)S(1)}, u32[]{:S(2)}, u32[]{:S(2)}) async-start(bf16[16,2,18432]{2,1,0:T(2,128)(2,1)} %reshape.357), calls=%async_computation | async-start | bytes 2359296 | tf_op jit(solution)/shard_map/all_to_all | solution.py:46
  33.2 0.1 convert_reduce_fusion.1
  33.4 0.1 broadcast_in_dim.86
  33.9 0.8 compare_and_fusion
  34.7 24.1 %all-to-all-done = bf16[16,2,18432]{2,1,0:T(2,128)(2,1)S(1)} async-done(((bf16[16,2,18432]{2,1,0:T(2,128)(2,1)}), bf16[16,2,18432]{2,1,0:T(2,128)(2,1)S(1)}, u32[]{:S(2)}, u32[]{:S(2)}) %all-to-all-start) | async-done | bytes 1179680 | tf_op jit(solution)/shard_map/all_to_all | solution.py:46
  58.8 1.2 reshape.358
  59.9 1.3 copy.21
  61.2 3.5 %gather_fusion.1 = bf16[32,36864]{1,0:T(8,128)(2,1)} fusion(bf16[16,36864]{1,0:T(8,128)(2,1)S(1)} %bitcast.67, s32[1024]{0:T(1024)S(1)} %pad_clamp_fusion), kind=kCustom, calls=%fused_computation.1 | custom fusion | bytes 4718720 | tf_op jit(solution)/shard_map/jit(_take)/gather | solution.py:49
  64.7 4.5 %gather.12 = bf16[2048,576]{1,0:T(8,128)(2,1)S(1)} reshape(bf16[32,36864]{1,0:T(8,128)(2,1)} %gather_fusion.1) | data formatting | bytes 4718592 | tf_op jit(solution)/shard_map/jit(_take)/gather | solution.py:49
  69.3 0.5 broadcast_select_fusion
  69.9 1.5 %copy-done = bf16[2048,576]{1,0:T(8,128)(2,1)} copy-done((bf16[2048,576]{1,0:T(8,128)(2,1)}, bf16[2048,576]{1,0:T(8,128)(2,1)S(1)}, u32[]{:S(2)}) %copy-start) | copy-done | bytes 2359320
  71.3 19.6 %fusion.9 = f32[2048,64,64]{0,2,1:T(8,128)} fusion(bf16[64,64,576]{2,1,0:T(8,128)(2,1)} %param.3, bf16[2048,576]{1,0:T(8,128)(2,1)S(1)} %broadcast_select_fusion), kind=kOutput, calls=%fused_computation.12 | convolution fusion | flops 9663676416 | bytes 40632320 | tf_op jit(solution)/shard_map/qhc,kc->qhk/dot_general | solution.py:59
  91.0 32.5 %fusion.27 = (f32[64,64]{1,0:T(8,128)S(1)}, bf16[64,64,2048]{2,1,0:T(8,128)(2,1)}) fusion(f32[2048,64,64]{0,2,1:T(8,128)} %fusion.9, pred[64,2048]{1,0:T(8,128)(4,1)S(1)} %copy-done.2), kind=kOutput, calls=%fused_computation.76 | output fusion | flops 67110912 | bytes 50479104 | tf_op jit(solution)/shard_map/sub | solution.py:64
  123.5 13.8 %divide_convert_fusion = bf16[64,64,512]{2,1,0:T(8,128)(2,1)} fusion(f32[64,64]{1,0:T(8,128)S(1)} %get-tuple-element.12, bf16[64,64,2048]{2,1,0:T(8,128)(2,1)} %get-tuple-element.13, bf16[2048,576]{1,0:T(8,128)(2,1)S(1)} %copy-done.1), kind=kOutput, calls=%fused_computation.11 | convolution fusion | flops 8594128896 | bytes 23101440 | tf_op jit(solution)/shard_map/qhk,kc->qhc/dot_general | solution.py:67
  (24 shorter events, 0.5 us)
Async XLA Ops:
  20.7 12.5 %copy-start.3 = (s32[1,32]{1,0:T(1,128)S(1)}, s32[1,32]{1,0:T(1,128)}, u32[]{:S(2)}) copy-start(s32[1,32]{1,0:T(1,128)} %param.5) | copy-start | bytes 388
  24.7 34.1 %all-to-all-start = ((bf16[16,2,18432]{2,1,0:T(2,128)(2,1)}), bf16[16,2,18432]{2,1,0:T(2,128)(2,1)S(1)}, u32[]{:S(2)}, u32[]{:S(2)}) async-start(bf16[16,2,18432]{2,1,0:T(2,128)(2,1)} %reshape.357), calls=%async_computation | async-start | bytes 2359296 | tf_op jit(solution)/shard_map/all_to_all | solution.py:46
  69.8 1.5 %copy-start = (bf16[2048,576]{1,0:T(8,128)(2,1)}, bf16[2048,576]{1,0:T(8,128)(2,1)S(1)}, u32[]{:S(2)}) copy-start(bf16[2048,576]{1,0:T(8,128)(2,1)S(1)} %broadcast_select_fusion) | copy-start | bytes 7077892
  71.3 19.7 %copy-start.2 = (pred[64,2048]{1,0:T(8,128)(4,1)S(1)}, pred[64,2048]{1,0:T(8,128)(4,1)}, u32[]{:S(2)}) copy-start(pred[64,2048]{1,0:T(8,128)(4,1)} %compare_and_fusion) | copy-start | bytes 393220
  91.0 32.5 %copy-start.1 = (bf16[2048,576]{1,0:T(8,128)(2,1)S(1)}, bf16[2048,576]{1,0:T(8,128)(2,1)}, u32[]{:S(2)}) copy-start(bf16[2048,576]{1,0:T(8,128)(2,1)} %copy-done) | copy-start | bytes 7077892
where the time goes:
time: 140 us; the launch traced here: 137 us
  other arithmetic  36.2 us (26%)
  matrix products  33.4 us (24%)
  waiting for transfers between devices  24.1 us (17%)
  local copies, waits for them, and re-layouts  17.6 us (13%)
  blocking collectives  17.3 us (12%)
  starting transfers between devices  8.47 us (6%)
    sub x1, other arithmetic, shards(): expo = jnp.where(allowed, jnp.exp(scores - top), 0.0)  32.5 us
    all_to_all x1, waiting for transfers between devices, shards(): lax.all_to_all(outgoing, 'ctx', split_axis=0, concat_axis=0, tiled=True)  24.1 us
    dot_general x1, matrix products, shards(): jnp.einsum('qhc,kc->qhk', queries, keys, preferred_element_type=jnp.float32)  19.6 us
    all_gather x1, blocking collectives, shards(): lists_all = lax.all_gather(tile_lists, 'ctx', axis=0, tiled=True)  17.3 us
    dot_general x1, matrix products, shards(): jnp.einsum('qhk,kc->qhc', weights, keys[:, :LAT], preferred_element_type=...  13.8 us
    all_to_all x1, starting transfers between devices, shards(): lax.all_to_all(outgoing, 'ctx', split_axis=0, concat_axis=0, tiled=True)  8.47 us
    gather x2, local copies, waits for them, and re-layouts, shards(): keys = jnp.take(incoming, position, axis=0)  8.04 us
    unnamed x12, local copies, waits for them, and re-layouts  6.85 us
  transfers between devices with their start and end apart: 1, of which 1 were waited for; matrix products, arithmetic and copies ran while one was open for 1% of the time, Pallas kernels for 0%

commit v1 on v0

--- a/solution.py
+++ b/solution.py
@@ -1,6 +1,11 @@
+import functools
+import math
+
 import jax
 import jax.numpy as jnp
 from jax import lax
+from jax.experimental import pallas as pl
+from jax.experimental.pallas import tpu as pltpu
 from jax.sharding import PartitionSpec as P
 
 LAT = 512
@@ -8,9 +13,12 @@
 TOPK = 32
 CAP = 1
 TILES_DEV = 4
+ROW = 4
 
 
 softmax_scale = 192.0 ** (-0.5)
+LOG2E_SCALE = softmax_scale * math.log2(math.e)
+MASKED = -1e30
 
 
 def slot_ranks(holders):
@@ -28,7 +36,7 @@
     return jnp.sum(jnp.where(hits, local_tile[..., None] + 1, 0), axis=-2) - 1
 
 
-def shards(queries, latent_cache, tile_lists):
+def shards_general(queries, latent_cache, tile_lists):
     width = latent_cache.shape[1]
     listing = tile_lists[0]
     me = lax.axis_index("ctx")
@@ -59,7 +67,7 @@
         jnp.einsum("qhc,kc->qhk", queries, keys, preferred_element_type=jnp.float32) * softmax_scale
     )
     allowed = (key_ok[None, :] & (key_pos[None, :] <= query_pos[:, None]))[:, None, :]
-    scores = jnp.where(allowed, scores, -1e30)
+    scores = jnp.where(allowed, scores, MASKED)
     top = jnp.max(scores, axis=-1, keepdims=True)
     expo = jnp.where(allowed, jnp.exp(scores - top), 0.0)
     total = jnp.sum(expo, axis=-1, keepdims=True)
@@ -68,12 +76,185 @@
     return (summed / total).astype(jnp.bfloat16)
 
 
+def pick_kernel(outs_of, sel_ref, *refs):
+    n_src = 1 + max(src for parts in outs_of for src, _ in parts)
+    sources, outs, sems = refs[:n_src], refs[n_src : n_src + len(outs_of)], refs[-1]
+    copies = []
+    for out, parts in zip(outs, outs_of):
+        for at, (src, entry) in enumerate(parts):
+            tile = pl.multiple_of(sel_ref[entry] * TILE, TILE)
+            copies.append(
+                pltpu.make_async_copy(
+                    sources[src].at[pl.ds(tile, TILE), :],
+                    out.at[pl.ds(at * TILE, TILE), :],
+                    sems.at[len(copies)],
+                )
+            )
+    for copy in copies:
+        copy.start()
+    for copy in copies:
+        copy.wait()
+
+
+def pick_tiles(sel, sources, outs_of):
+    width = sources[0].shape[1]
+    total = sum(len(parts) for parts in outs_of)
+    return pl.pallas_call(
+        functools.partial(pick_kernel, outs_of),
+        in_specs=[pl.BlockSpec(memory_space=pltpu.SMEM)]
+        + [pl.BlockSpec(memory_space=pl.ANY)] * len(sources),
+        out_specs=[pl.BlockSpec(memory_space=pl.ANY)] * len(outs_of),
+        out_shape=[
+            jax.ShapeDtypeStruct((len(parts) * TILE, width), sources[0].dtype) for parts in outs_of
+        ],
+        scratch_shapes=[pltpu.SemaphoreType.DMA((total,))],
+        cost_estimate=pl.CostEstimate(
+            flops=0, transcendentals=0, bytes_accessed=4 * total * TILE * width
+        ),
+        name="pick_tiles",
+    )(sel, *sources)
+
+
+def attend_kernel(heads, parts, sel_ref, bias_ref, q_ref, *refs):
+    n_src = 1 + max(src for src, _, _ in parts)
+    sources, (out_ref, keys_ref, sems) = refs[:n_src], refs[n_src:]
+
+    @pl.when(pl.program_id(0) == 0)
+    def _():
+        copies = []
+        for at, (src, entry, tile) in enumerate(parts):
+            row = tile * TILE if entry is None else pl.multiple_of(sel_ref[entry] * TILE, TILE)
+            copies.append(
+                pltpu.make_async_copy(
+                    sources[src].at[pl.ds(row, TILE), :],
+                    keys_ref.at[pl.ds(at * TILE, TILE), :],
+                    sems.at[at],
+                )
+            )
+        for copy in copies:
+            copy.start()
+        for copy in copies:
+            copy.wait()
+
+    rows = q_ref.shape[0]
+    count = keys_ref.shape[0]
+    scores = lax.dot_general(
+        q_ref[...], keys_ref[...], (((1,), (1,)), ((), ())), preferred_element_type=jnp.float32
+    )
+    scores = scores.reshape(rows // heads, heads, count) + bias_ref[...][:, None, :]
+    scores = scores.reshape(rows, count)
+    top = jnp.max(scores, axis=1, keepdims=True)
+    expo = jnp.exp2(scores * LOG2E_SCALE - top * LOG2E_SCALE)
+    total = jnp.sum(expo, axis=1, keepdims=True)
+    summed = jnp.dot(
+        expo.astype(jnp.bfloat16), keys_ref[:, :LAT], preferred_element_type=jnp.float32
+    )
+    out_ref[...] = (summed * (1.0 / total)).astype(out_ref.dtype)
+
+
+def attend(queries, bias, sel, sources, parts):
+    count, heads, width = queries.shape
+    keys = len(parts) * TILE
+    step = 16
+    rows = step * heads
+    out = pl.pallas_call(
+        functools.partial(attend_kernel, heads, parts),
+        grid=(count // step,),
+        in_specs=[
+            pl.BlockSpec(memory_space=pltpu.SMEM),
+            pl.BlockSpec((step, keys), lambda i: (i, 0)),
+            pl.BlockSpec((rows, width), lambda i: (i, 0)),
+        ]
+        + [pl.BlockSpec(memory_space=pl.ANY)] * len(sources),
+        out_specs=pl.BlockSpec((rows, LAT), lambda i: (i, 0)),
+        out_shape=jax.ShapeDtypeStruct((count * heads, LAT), jnp.bfloat16),
+        scratch_shapes=[
+            pltpu.VMEM((keys, width), jnp.bfloat16),
+            pltpu.SemaphoreType.DMA((len(parts),)),
+        ],
+        compiler_params=pltpu.CompilerParams(
+            vmem_limit_bytes=48 << 20, dimension_semantics=("arbitrary",)
+        ),
+        cost_estimate=pl.CostEstimate(
+            flops=2 * count * heads * keys * (width + LAT),
+            transcendentals=count * heads * keys,
+            bytes_accessed=2 * count * heads * (width + LAT),
+        ),
+        name="attend",
+    )(sel, bias, queries.reshape(count * heads, width), *sources)
+    return out.reshape(count, heads, LAT)
+
+
+def shards_rows(queries, latent_cache, tile_lists):
+    size = lax.axis_size("ctx")
+    depth = size // ROW
+    me = lax.axis_index("ctx")
+    z, r = me // ROW, me % ROW
+    up = [(i, i + ROW) for i in range(size - ROW)]
+    down = [(i + ROW, i) for i in range(size - ROW)]
+    beside = {m: [(i, i ^ m) for i in range(size)] for m in range(1, ROW)}
+
+    above = [latent_cache]
+    if depth > 1:
+        above.append(lax.ppermute(latent_cache, "ctx", up))
+    lists = jnp.concatenate(
+        [tile_lists] + [lax.ppermute(tile_lists, "ctx", beside[m]) for m in range(1, ROW)]
+    )
+    below = lax.ppermute(lists, "ctx", down)
+
+    def local_tile(listing, holder):
+        hit = (listing >= 0) & (listing // TILES_DEV == holder)
+        return jnp.sum(jnp.where(hit, listing % TILES_DEV, 0), axis=1)
+
+    wanted = [local_tile(lists, me - ROW * k) for k in range(depth)]
+    sources, parts = [], {}
+
+    first = range(min(2, depth - 1) if depth > 1 else 1)
+    sel = jnp.concatenate([wanted[k] for k in first])
+    sent = pick_tiles(
+        sel, [above[k] for k in first], [[(k, k * ROW + m) for k in first] for m in range(1, ROW)]
+    )
+    for m in range(1, ROW):
+        for k in first:
+            parts[k, m] = (len(sources), None, k)
+        sources.append(lax.ppermute(sent[m - 1], "ctx", beside[m]))
+    for k in range(2, depth - 1):
+        above.append(lax.ppermute(above[k - 1], "ctx", up))
+        sent = pick_tiles(wanted[k], [above[k]], [[(0, m)] for m in range(1, ROW)])
+        for m in range(1, ROW):
+            parts[k, m] = (len(sources), None, 0)
+            sources.append(lax.ppermute(sent[m - 1], "ctx", beside[m]))
+    if depth > 1:
+        last = depth - 1
+        sel = local_tile(below, me - ROW * (last - 1))
+        sent = pick_tiles(sel, [above[last - 1]], [[(0, m)] for m in range(ROW)])
+        for m in range(ROW):
+            parts[last, m] = (len(sources), None, 0)
+            hop = [(i, (i + ROW) ^ m) for i in range(ROW * (last - 1), ROW * last)]
+            sources.append(lax.ppermute(sent[m], "ctx", hop))
+    for k in range(max(1, depth - 1)):
+        parts[k, 0] = (len(sources), k, 0)
+        sources.append(above[k])
+    order = [(k, m) for k in range(depth) for m in range(ROW)]
+    own = jnp.stack([wanted[k][0] for k in range(max(1, depth - 1))])
+
+    slot = jnp.arange(len(order) * TILE, dtype=jnp.int32)
+    k, m, offset = slot // (ROW * TILE), slot // TILE % ROW, slot % TILE
+    seen = jnp.where(k == 0, (r ^ m) <= r, k <= z)
+    query = jnp.arange(queries.shape[0], dtype=jnp.int32)[:, None]
+    seen = seen & ((k > 0) | (m > 0) | (offset <= query))
+    bias = jnp.where(seen, 0.0, MASKED).astype(jnp.float32)
+    return attend(queries, bias, own, sources, [parts[key] for key in order])
+
+
 def solution(mesh):
     placed = (
         P(("groups", "ctx"), None, None),
         P(("groups", "ctx"), None),
         P(("groups", "ctx"), None),
     )
+    size = mesh.shape["ctx"]
+    shards = shards_rows if size <= TOPK and size % ROW == 0 else shards_general
     return jax.shard_map(
         shards,
         mesh=mesh,

time: 140 us -> 95.4 us (0.68); the launches traced: 137 us -> 95 us
  Pallas kernels: 0 us -> 56 us
  matrix products: 33.4 us -> 0 us
  other arithmetic: 36.2 us -> 3.45 us
  blocking collectives: 17.3 us -> 0 us
  local copies, waits for them, and re-layouts: 17.6 us -> 4.81 us
  waiting for transfers between devices: 24.1 us -> 11.5 us
  starting transfers between devices: 8.47 us -> 19 us
    pallas_call x0 -> x4, Pallas kernels: none -> 56 us  [the longest x3 37.7 us: pick_tiles(): pl.pallas_call(functools.partial(pick_kernel, outs_of), in_specs=[pl.Bloc...]
    dot_general x2 -> x0, matrix products: 33.4 us -> none  [the longest x1 19.6 us: shards(): jnp.einsum('qhc,kc->qhk', queries, keys, preferred_element_type=jnp.float32)]
    sub x1 -> x0, other arithmetic: 32.5 us -> none  [shards(): expo = jnp.where(allowed, jnp.exp(scores - top), 0.0)]
    all_to_all x1 -> x0, waiting for transfers between devices: 24.1 us -> none  [shards(): lax.all_to_all(outgoing, 'ctx', split_axis=0, concat_axis=0, tiled=True)]
    ppermute x0 -> x16, starting transfers between devices: none -> 19 us  [the longest x6 5.41 us: shards_rows(): sources.append(lax.ppermute(sent[m - 1], 'ctx', beside[m]))]
    all_gather x1 -> x0, blocking collectives: 17.3 us -> none  [shards(): lists_all = lax.all_gather(tile_lists, 'ctx', axis=0, tiled=True)]
    ppermute x0 -> x16, waiting for transfers between devices: none -> 11.5 us  [the longest x4 7.08 us: shards_rows(): sources.append(lax.ppermute(sent[m], 'ctx', hop))]
    gather x3 -> x0, local copies, waits for them, and re-layouts: 9.38 us -> none  [the longest x2 8.04 us: shards(): keys = jnp.take(incoming, position, axis=0)]
  transfers between devices with their start and end apart: 1 -> 16, of which waited for: 1 -> 6; matrix products, arithmetic and copies ran while one was open for 1% -> 5% of each run, Pallas kernels for 0% -> 40%
where the time goes in v1:
time: 95.4 us; the launch traced here: 95 us
  Pallas kernels  56 us (59%)
  starting transfers between devices  19 us (20%)
  waiting for transfers between devices  11.5 us (12%)
  local copies, waits for them, and re-layouts  4.81 us (5%)
  other arithmetic  3.45 us (4%)
    pallas_call x3, Pallas kernels, pick_tiles(): pl.pallas_call(functools.partial(pick_kernel, outs_of), in_specs=[pl.Bloc...  37.7 us
    pallas_call x1, Pallas kernels, attend(): pl.pallas_call(functools.partial(attend_kernel, heads, parts), grid=(coun...  18.3 us
    ppermute x4, waiting for transfers between devices, shards_rows(): sources.append(lax.ppermute(sent[m], 'ctx', hop))  7.08 us
    ppermute x6, starting transfers between devices, shards_rows(): sources.append(lax.ppermute(sent[m - 1], 'ctx', beside[m]))  5.41 us
    ppermute x4, starting transfers between devices, shards_rows(): sources.append(lax.ppermute(sent[m], 'ctx', hop))  5.16 us
    unnamed x13, local copies, waits for them, and re-layouts  4.81 us
    ppermute x1, waiting for transfers between devices, shards_rows(): above.append(lax.ppermute(latent_cache, 'ctx', up))  3.92 us
    ppermute x1, starting transfers between devices, shards_rows(): below = lax.ppermute(lists, 'ctx', down)  3.58 us
  transfers between devices with their start and end apart: 16, of which 6 were waited for; matrix products, arithmetic and copies ran while one was open for 5% of the time, Pallas kernels for 40%

profile of v1, /device:TPU:25, one launch (start us, length us, event | category | flops | bytes accessed | tf_op | source)
XLA Modules:
  0.0 95.0 jit_solution(102520392696436824)
XLA Ops:
  0.0 1.2 %collective-permute-start.1 = (s32[1,32]{1,0:T(1,128)}, s32[1,32]{1,0:T(1,128)S(1)}, u32[]{:S(2)}, u32[]{:S(2)}) collective-permute-start(s32[1,32]{1,0:T(1,128)} %param.5), channel_id=1, source_target_pairs={{0,2},{1,3},{2,0},{3,1},{4,6},{5,7},{6,4},{7,5},{8,10},{9,11},{10,... | collective-permute-start | bytes 392 | tf_op jit(solution)/shard_map/ppermute | solution.py:201
  1.2 1.0 %collective-permute-start = (s32[1,32]{1,0:T(1,128)}, s32[1,32]{1,0:T(1,128)S(1)}, u32[]{:S(2)}, u32[]{:S(2)}) collective-permute-start(s32[1,32]{1,0:T(1,128)} %param.5), channel_id=1, source_target_pairs={{0,1},{1,0},{2,3},{3,2},{4,5},{5,4},{6,7},{7,6},{8,9},{9,8},{10,11... | collective-permute-start | bytes 392 | tf_op jit(solution)/shard_map/ppermute | solution.py:201
  2.3 1.2 %copy.5.refs_0_.refs_10_ = bf16[256,576]{1,0:T(8,128)(2,1)S(1)} copy(bf16[256,576]{0,1:T(8,128)(2,1)} %param.4) | data formatting | bytes 589824 | tf_op args[1]
  3.5 1.3 %collective-permute-start.3 = (bf16[256,576]{1,0:T(8,128)(2,1)S(1)}, bf16[256,576]{1,0:T(8,128)(2,1)S(1)}, u32[]{:S(2)}, u32[]{:S(2)}) collective-permute-start(bf16[256,576]{1,0:T(8,128)(2,1)S(1)} %copy.5.refs_0_.refs_10_), channel_id=1, source_target_pairs={{0,4},{1,5},{2,6},{3,7},{4,8},{5,9},{6,10},{7,11},{8,12},{9,13},{1... | collective-permute-start | bytes 884744 | tf_op jit(solution)/shard_map/ppermute | solution.py:199
  6.0 3.6 %collective-permute-start.11 = (s32[4,32]{1,0:T(4,128)S(1)}, s32[4,32]{1,0:T(4,128)S(1)}, u32[]{:S(2)}, u32[]{:S(2)}) collective-permute-start(s32[4,32]{1,0:T(4,128)S(1)} %get-tuple-element.29), channel_id=1, source_target_pairs={{4,0},{5,1},{6,2},{7,3},{8,4},{9,5},{10,6},{11,7},{12,8},{13,9},{1... | collective-permute-start | bytes 1544 | tf_op jit(solution)/shard_map/ppermute | solution.py:203
  10.2 3.9 %collective-permute-done.3.refs_1_.refs_11_ = bf16[256,576]{1,0:T(8,128)(2,1)S(1)} collective-permute-done((bf16[256,576]{1,0:T(8,128)(2,1)S(1)}, bf16[256,576]{1,0:T(8,128)(2,1)S(1)}, u32[]{:S(2)}, u32[]{:S(2)}) %collective-permute-start.3) | collective-permute-done | bytes 294944 | tf_op jit(solution)/shard_map/ppermute | solution.py:199
  14.1 1.3 %collective-permute-start.7 = (bf16[256,576]{1,0:T(8,128)(2,1)S(1)}, bf16[256,576]{1,0:T(8,128)(2,1)S(1)}, u32[]{:S(2)}, u32[]{:S(2)}) collective-permute-start(bf16[256,576]{1,0:T(8,128)(2,1)S(1)} %collective-permute-done.3.refs_1_.refs_11_), channel_id=1, source_target_pairs={{0,4},{1,5},{2,6},{3,7},{4,8},{5,9},{6,10},{7,11},{8,12},{9,13},{1... | collective-permute-start | bytes 884744 | tf_op jit(solution)/shard_map/ppermute | solution.py:222
  16.1 16.7 %pick_tiles.3 = (bf16[128,576]{1,0:T(8,128)(2,1)}, bf16[128,576]{1,0:T(8,128)(2,1)}, bf16[128,576]{1,0:T(8,128)(2,1)}) custom-call(s32[8]{0:T(128)} %pad_add_fusion.2.sel_ref, bf16[256,576]{1,0:T(8,128)(2,1)} %copy-done, bf16[256,576]{1,0:T(8,128)(2,1)} %copy-done.4), custom_call_target="tpu_custom_call" | custom-call | bytes 884736 | tf_op jit(solution)/shard_map/pick_tiles/pallas_call | solution.py:102
  32.8 1.4 %collective-permute-start.4 = (bf16[128,576]{1,0:T(8,128)(2,1)}, bf16[128,576]{1,0:T(8,128)(2,1)S(1)}, u32[]{:S(2)}, u32[]{:S(2)}) collective-permute-start(bf16[128,576]{1,0:T(8,128)(2,1)} %get-tuple-element.15), channel_id=1, source_target_pairs={{0,1},{1,0},{2,3},{3,2},{4,5},{5,4},{6,7},{7,6},{8,9},{9,8},{10,11... | collective-permute-start | bytes 442376 | tf_op jit(solution)/shard_map/ppermute | solution.py:220
  34.2 1.3 %collective-permute-start.5 = (bf16[128,576]{1,0:T(8,128)(2,1)}, bf16[128,576]{1,0:T(8,128)(2,1)S(1)}, u32[]{:S(2)}, u32[]{:S(2)}) collective-permute-start(bf16[128,576]{1,0:T(8,128)(2,1)} %get-tuple-element.16), channel_id=1, source_target_pairs={{0,2},{1,3},{2,0},{3,1},{4,6},{5,7},{6,4},{7,5},{8,10},{9,11},{10,... | collective-permute-start | bytes 442376 | tf_op jit(solution)/shard_map/ppermute | solution.py:220
  36.7 9.2 %pick_tiles.4 = (bf16[64,576]{1,0:T(8,128)(2,1)}, bf16[64,576]{1,0:T(8,128)(2,1)}, bf16[64,576]{1,0:T(8,128)(2,1)}) custom-call(s32[4]{0:T(128)} %get-tuple-element.26.sel_ref, bf16[256,576]{1,0:T(8,128)(2,1)} %copy-done.2), custom_call_target="tpu_custom_call" | custom-call | bytes 442368 | tf_op jit(solution)/shard_map/pick_tiles/pallas_call | solution.py:102
  46.2 1.2 %collective-permute-start.9 = (bf16[64,576]{1,0:T(8,128)(2,1)}, bf16[64,576]{1,0:T(8,128)(2,1)S(1)}, u32[]{:S(2)}, u32[]{:S(2)}) collective-permute-start(bf16[64,576]{1,0:T(8,128)(2,1)} %get-tuple-element.19), channel_id=1, source_target_pairs={{0,2},{1,3},{2,0},{3,1},{4,6},{5,7},{6,4},{7,5},{8,10},{9,11},{10,... | collective-permute-start | bytes 221192 | tf_op jit(solution)/shard_map/ppermute | solution.py:226
  48.2 11.7 %pick_tiles.5 = (bf16[64,576]{1,0:T(8,128)(2,1)}, bf16[64,576]{1,0:T(8,128)(2,1)}, bf16[64,576]{1,0:T(8,128)(2,1)}, bf16[64,576]{1,0:T(8,128)(2,1)}) custom-call(s32[4]{0:T(128)} %fusion.18.sel_ref, bf16[256,576]{1,0:T(8,128)(2,1)} %copy-done.2), custom_call_target="tpu_custom_call" | custom-call | bytes 589824 | tf_op jit(solution)/shard_map/pick_tiles/pallas_call | solution.py:102
  60.7 1.3 %collective-permute-start.12 = (bf16[64,576]{1,0:T(8,128)(2,1)}, bf16[64,576]{1,0:T(8,128)(2,1)S(1)}, u32[]{:S(2)}, u32[]{:S(2)}) collective-permute-start(bf16[64,576]{1,0:T(8,128)(2,1)} %get-tuple-element.21), channel_id=1, source_target_pairs={{8,12},{9,13},{10,14},{11,15},{24,28},{25,29},{26,30},{27,31}} | collective-permute-start | bytes 221192 | tf_op jit(solution)/shard_map/ppermute | solution.py:234
  62.0 1.3 %collective-permute-start.13 = (bf16[64,576]{1,0:T(8,128)(2,1)}, bf16[64,576]{1,0:T(8,128)(2,1)S(1)}, u32[]{:S(2)}, u32[]{:S(2)}) collective-permute-start(bf16[64,576]{1,0:T(8,128)(2,1)} %get-tuple-element.22), channel_id=1, source_target_pairs={{8,13},{9,12},{10,15},{11,14},{24,29},{25,28},{26,31},{27,30}} | collective-permute-start | bytes 221192 | tf_op jit(solution)/shard_map/ppermute | solution.py:234
  63.3 1.3 %collective-permute-start.14 = (bf16[64,576]{1,0:T(8,128)(2,1)}, bf16[64,576]{1,0:T(8,128)(2,1)S(1)}, u32[]{:S(2)}, u32[]{:S(2)}) collective-permute-start(bf16[64,576]{1,0:T(8,128)(2,1)} %get-tuple-element.23), channel_id=1, source_target_pairs={{8,14},{9,15},{10,12},{11,13},{24,30},{25,31},{26,28},{27,29}} | collective-permute-start | bytes 221192 | tf_op jit(solution)/shard_map/ppermute | solution.py:234
  64.6 1.3 %collective-permute-start.15 = (bf16[64,576]{1,0:T(8,128)(2,1)}, bf16[64,576]{1,0:T(8,128)(2,1)S(1)}, u32[]{:S(2)}, u32[]{:S(2)}) collective-permute-start(bf16[64,576]{1,0:T(8,128)(2,1)} %get-tuple-element.24), channel_id=1, source_target_pairs={{8,15},{9,14},{10,13},{11,12},{24,31},{25,30},{26,29},{27,28}} | collective-permute-start | bytes 221192 | tf_op jit(solution)/shard_map/ppermute | solution.py:234
  67.5 1.8 %collective-permute-done.13.refs_7_ = bf16[64,576]{1,0:T(8,128)(2,1)S(1)} collective-permute-done((bf16[64,576]{1,0:T(8,128)(2,1)}, bf16[64,576]{1,0:T(8,128)(2,1)S(1)}, u32[]{:S(2)}, u32[]{:S(2)}) %collective-permute-start.13) | collective-permute-done | bytes 73760 | tf_op jit(solution)/shard_map/ppermute | solution.py:234
  69.2 2.7 %collective-permute-done.14.refs_8_ = bf16[64,576]{1,0:T(8,128)(2,1)S(1)} collective-permute-done((bf16[64,576]{1,0:T(8,128)(2,1)}, bf16[64,576]{1,0:T(8,128)(2,1)S(1)}, u32[]{:S(2)}, u32[]{:S(2)}) %collective-permute-start.14) | collective-permute-done | bytes 73760 | tf_op jit(solution)/shard_map/ppermute | solution.py:234
  72.0 1.8 %collective-permute-done.15.refs_9_ = bf16[64,576]{1,0:T(8,128)(2,1)S(1)} collective-permute-done((bf16[64,576]{1,0:T(8,128)(2,1)}, bf16[64,576]{1,0:T(8,128)(2,1)S(1)}, u32[]{:S(2)}, u32[]{:S(2)}) %collective-permute-start.15) | collective-permute-done | bytes 73760 | tf_op jit(solution)/shard_map/ppermute | solution.py:234
  73.7 1.0 %copy-done.1 = bf16[256,576]{1,0:T(8,128)(2,1)S(1)} copy-done((bf16[256,576]{1,0:T(8,128)(2,1)S(1)}, bf16[256,576]{1,0:T(8,128)(2,1)}, u32[]{:S(2)}) %copy-start.1) | copy-done | bytes 294936
  74.7 1.0 %copy-done.3 = bf16[256,576]{1,0:T(8,128)(2,1)S(1)} copy-done((bf16[256,576]{1,0:T(8,128)(2,1)S(1)}, bf16[256,576]{1,0:T(8,128)(2,1)}, u32[]{:S(2)}) %copy-start.3) | copy-done | bytes 294936
  75.7 1.0 %copy-done.5 = bf16[256,576]{1,0:T(8,128)(2,1)S(1)} copy-done((bf16[256,576]{1,0:T(8,128)(2,1)S(1)}, bf16[256,576]{1,0:T(8,128)(2,1)}, u32[]{:S(2)}) %copy-start.5) | copy-done | bytes 294936
  76.6 18.3 %attend.1 = bf16[4096,512]{1,0:T(8,128)(2,1)} custom-call(s32[3]{0:T(128)S(1)} %pad_add_fusion.1.sel_ref, f32[64,1024]{1,0:T(8,128)S(1)} %fusion.2.bias_ref, bf16[4096,576]{1,0:T(8,128)(2,1)} %bitcast.8, bf16[128,576]{1,0:T(8,128)(2,1)S(1)} %collective-permute-done.4.refs_0_, bf16[128,576]{1,0:T(8,128)(2,1)S(1)} %collective-permute-done.5.refs_1_, ...), custom_call_target="tpu_custom_call" | custom-call | flops 9126805504 | bytes 8912896 | tf_op jit(solution)/shard_map/attend/pallas_call | solution.py:160
  (33 shorter events, 7.1 us)
Async XLA Ops:
  0.0 4.9 %collective-permute-start.1 = (s32[1,32]{1,0:T(1,128)}, s32[1,32]{1,0:T(1,128)S(1)}, u32[]{:S(2)}, u32[]{:S(2)}) collective-permute-start(s32[1,32]{1,0:T(1,128)} %param.5), channel_id=1, source_target_pairs={{0,2},{1,3},{2,0},{3,1},{4,6},{5,7},{6,4},{7,5},{8,10},{9,11},{10,... | collective-permute-start | bytes 392 | tf_op jit(solution)/shard_map/ppermute | solution.py:201
  1.2 3.6 %collective-permute-start = (s32[1,32]{1,0:T(1,128)}, s32[1,32]{1,0:T(1,128)S(1)}, u32[]{:S(2)}, u32[]{:S(2)}) collective-permute-start(s32[1,32]{1,0:T(1,128)} %param.5), channel_id=1, source_target_pairs={{0,1},{1,0},{2,3},{3,2},{4,5},{5,4},{6,7},{7,6},{8,9},{9,8},{10,11... | collective-permute-start | bytes 392 | tf_op jit(solution)/shard_map/ppermute | solution.py:201
  2.2 3.1 %collective-permute-start.2 = (s32[1,32]{1,0:T(1,128)}, s32[1,32]{1,0:T(1,128)S(1)}, u32[]{:S(2)}, u32[]{:S(2)}) collective-permute-start(s32[1,32]{1,0:T(1,128)} %param.5), channel_id=1, source_target_pairs={{0,3},{1,2},{2,1},{3,0},{4,7},{5,6},{6,5},{7,4},{8,11},{9,10},{10,... | collective-permute-start | bytes 392 | tf_op jit(solution)/shard_map/ppermute | solution.py:201
  3.5 12.6 %copy-start = (bf16[256,576]{1,0:T(8,128)(2,1)}, bf16[256,576]{1,0:T(8,128)(2,1)S(1)}, u32[]{:S(2)}) copy-start(bf16[256,576]{1,0:T(8,128)(2,1)S(1)} %copy.5.refs_0_.refs_10_) | copy-start | bytes 884740
  3.5 10.7 %collective-permute-start.3 = (bf16[256,576]{1,0:T(8,128)(2,1)S(1)}, bf16[256,576]{1,0:T(8,128)(2,1)S(1)}, u32[]{:S(2)}, u32[]{:S(2)}) collective-permute-start(bf16[256,576]{1,0:T(8,128)(2,1)S(1)} %copy.5.refs_0_.refs_10_), channel_id=1, source_target_pairs={{0,4},{1,5},{2,6},{3,7},{4,8},{5,9},{6,10},{7,11},{8,12},{9,13},{1... | collective-permute-start | bytes 884744 | tf_op jit(solution)/shard_map/ppermute | solution.py:199
  6.0 40.3 %collective-permute-start.11 = (s32[4,32]{1,0:T(4,128)S(1)}, s32[4,32]{1,0:T(4,128)S(1)}, u32[]{:S(2)}, u32[]{:S(2)}) collective-permute-start(s32[4,32]{1,0:T(4,128)S(1)} %get-tuple-element.29), channel_id=1, source_target_pairs={{4,0},{5,1},{6,2},{7,3},{8,4},{9,5},{10,6},{11,7},{12,8},{13,9},{1... | collective-permute-start | bytes 1544 | tf_op jit(solution)/shard_map/ppermute | solution.py:203
  14.1 1.9 %copy-start.4 = (bf16[256,576]{1,0:T(8,128)(2,1)}, bf16[256,576]{1,0:T(8,128)(2,1)S(1)}, u32[]{:S(2)}) copy-start(bf16[256,576]{1,0:T(8,128)(2,1)S(1)} %collective-permute-done.3.refs_1_.refs_11_) | copy-start | bytes 884740
  14.1 21.9 %collective-permute-start.7 = (bf16[256,576]{1,0:T(8,128)(2,1)S(1)}, bf16[256,576]{1,0:T(8,128)(2,1)S(1)}, u32[]{:S(2)}, u32[]{:S(2)}) collective-permute-start(bf16[256,576]{1,0:T(8,128)(2,1)S(1)} %collective-permute-done.3.refs_1_.refs_11_), channel_id=1, source_target_pairs={{0,4},{1,5},{2,6},{3,7},{4,8},{5,9},{6,10},{7,11},{8,12},{9,13},{1... | collective-permute-start | bytes 884744 | tf_op jit(solution)/shard_map/ppermute | solution.py:222
  32.8 27.1 %collective-permute-start.4 = (bf16[128,576]{1,0:T(8,128)(2,1)}, bf16[128,576]{1,0:T(8,128)(2,1)S(1)}, u32[]{:S(2)}, u32[]{:S(2)}) collective-permute-start(bf16[128,576]{1,0:T(8,128)(2,1)} %get-tuple-element.15), channel_id=1, source_target_pairs={{0,1},{1,0},{2,3},{3,2},{4,5},{5,4},{6,7},{7,6},{8,9},{9,8},{10,11... | collective-permute-start | bytes 442376 | tf_op jit(solution)/shard_map/ppermute | solution.py:220
  34.2 26.5 %collective-permute-start.5 = (bf16[128,576]{1,0:T(8,128)(2,1)}, bf16[128,576]{1,0:T(8,128)(2,1)S(1)}, u32[]{:S(2)}, u32[]{:S(2)}) collective-permute-start(bf16[128,576]{1,0:T(8,128)(2,1)} %get-tuple-element.16), channel_id=1, source_target_pairs={{0,2},{1,3},{2,0},{3,1},{4,6},{5,7},{6,4},{7,5},{8,10},{9,11},{10,... | collective-permute-start | bytes 442376 | tf_op jit(solution)/shard_map/ppermute | solution.py:220
  35.5 26.5 %collective-permute-start.6 = (bf16[128,576]{1,0:T(8,128)(2,1)}, bf16[128,576]{1,0:T(8,128)(2,1)S(1)}, u32[]{:S(2)}, u32[]{:S(2)}) collective-permute-start(bf16[128,576]{1,0:T(8,128)(2,1)} %get-tuple-element.17), channel_id=1, source_target_pairs={{0,3},{1,2},{2,1},{3,0},{4,7},{5,6},{6,5},{7,4},{8,11},{9,10},{10,... | collective-permute-start | bytes 442376 | tf_op jit(solution)/shard_map/ppermute | solution.py:220
  36.0 0.7 copy-start.2
  46.0 17.3 %collective-permute-start.8 = (bf16[64,576]{1,0:T(8,128)(2,1)}, bf16[64,576]{1,0:T(8,128)(2,1)S(1)}, u32[]{:S(2)}, u32[]{:S(2)}) collective-permute-start(bf16[64,576]{1,0:T(8,128)(2,1)} %get-tuple-element.18), channel_id=1, source_target_pairs={{0,1},{1,0},{2,3},{3,2},{4,5},{5,4},{6,7},{7,6},{8,9},{9,8},{10,11... | collective-permute-start | bytes 221192 | tf_op jit(solution)/shard_map/ppermute | solution.py:226
  46.2 18.4 %collective-permute-start.9 = (bf16[64,576]{1,0:T(8,128)(2,1)}, bf16[64,576]{1,0:T(8,128)(2,1)S(1)}, u32[]{:S(2)}, u32[]{:S(2)}) collective-permute-start(bf16[64,576]{1,0:T(8,128)(2,1)} %get-tuple-element.19), channel_id=1, source_target_pairs={{0,2},{1,3},{2,0},{3,1},{4,6},{5,7},{6,4},{7,5},{8,10},{9,11},{10,... | collective-permute-start | bytes 221192 | tf_op jit(solution)/shard_map/ppermute | solution.py:226
  59.9 6.7 %collective-permute-start.10 = (bf16[64,576]{1,0:T(8,128)(2,1)}, bf16[64,576]{1,0:T(8,128)(2,1)S(1)}, u32[]{:S(2)}, u32[]{:S(2)}) collective-permute-start(bf16[64,576]{1,0:T(8,128)(2,1)} %get-tuple-element.20), channel_id=1, source_target_pairs={{0,3},{1,2},{2,1},{3,0},{4,7},{5,6},{6,5},{7,4},{8,11},{9,10},{10,... | collective-permute-start | bytes 221192 | tf_op jit(solution)/shard_map/ppermute | solution.py:226
  60.7 6.7 %collective-permute-start.12 = (bf16[64,576]{1,0:T(8,128)(2,1)}, bf16[64,576]{1,0:T(8,128)(2,1)S(1)}, u32[]{:S(2)}, u32[]{:S(2)}) collective-permute-start(bf16[64,576]{1,0:T(8,128)(2,1)} %get-tuple-element.21), channel_id=1, source_target_pairs={{8,12},{9,13},{10,14},{11,15},{24,28},{25,29},{26,30},{27,31}} | collective-permute-start | bytes 221192 | tf_op jit(solution)/shard_map/ppermute | solution.py:234
  62.0 7.2 %collective-permute-start.13 = (bf16[64,576]{1,0:T(8,128)(2,1)}, bf16[64,576]{1,0:T(8,128)(2,1)S(1)}, u32[]{:S(2)}, u32[]{:S(2)}) collective-permute-start(bf16[64,576]{1,0:T(8,128)(2,1)} %get-tuple-element.22), channel_id=1, source_target_pairs={{8,13},{9,12},{10,15},{11,14},{24,29},{25,28},{26,31},{27,30}} | collective-permute-start | bytes 221192 | tf_op jit(solution)/shard_map/ppermute | solution.py:234
  63.3 8.6 %collective-permute-start.14 = (bf16[64,576]{1,0:T(8,128)(2,1)}, bf16[64,576]{1,0:T(8,128)(2,1)S(1)}, u32[]{:S(2)}, u32[]{:S(2)}) collective-permute-start(bf16[64,576]{1,0:T(8,128)(2,1)} %get-tuple-element.23), channel_id=1, source_target_pairs={{8,14},{9,15},{10,12},{11,13},{24,30},{25,31},{26,28},{27,29}} | collective-permute-start | bytes 221192 | tf_op jit(solution)/shard_map/ppermute | solution.py:234
  64.6 9.1 %collective-permute-start.15 = (bf16[64,576]{1,0:T(8,128)(2,1)}, bf16[64,576]{1,0:T(8,128)(2,1)S(1)}, u32[]{:S(2)}, u32[]{:S(2)}) collective-permute-start(bf16[64,576]{1,0:T(8,128)(2,1)} %get-tuple-element.24), channel_id=1, source_target_pairs={{8,15},{9,14},{10,13},{11,12},{24,31},{25,30},{26,29},{27,28}} | collective-permute-start | bytes 221192 | tf_op jit(solution)/shard_map/ppermute | solution.py:234
  73.7 1.0 %copy-start.1 = (bf16[256,576]{1,0:T(8,128)(2,1)S(1)}, bf16[256,576]{1,0:T(8,128)(2,1)}, u32[]{:S(2)}) copy-start(bf16[256,576]{1,0:T(8,128)(2,1)} %copy-done) | copy-start | bytes 884740
  74.7 1.0 %copy-start.3 = (bf16[256,576]{1,0:T(8,128)(2,1)S(1)}, bf16[256,576]{1,0:T(8,128)(2,1)}, u32[]{:S(2)}) copy-start(bf16[256,576]{1,0:T(8,128)(2,1)} %copy-done.2) | copy-start | bytes 884740
  75.7 1.0 %copy-start.5 = (bf16[256,576]{1,0:T(8,128)(2,1)S(1)}, bf16[256,576]{1,0:T(8,128)(2,1)}, u32[]{:S(2)}) copy-start(bf16[256,576]{1,0:T(8,128)(2,1)} %copy-done.4) | copy-start | bytes 884740

commit v2 on v0

--- a/solution.py
+++ b/solution.py
@@ -1,6 +1,11 @@
+import functools
+import math
+
 import jax
 import jax.numpy as jnp
 from jax import lax
+from jax.experimental import pallas as pl
+from jax.experimental.pallas import tpu as pltpu
 from jax.sharding import PartitionSpec as P
 
 LAT = 512
@@ -8,9 +13,13 @@
 TOPK = 32
 CAP = 1
 TILES_DEV = 4
+ROW = 4
+DEPTH = 4
 
 
 softmax_scale = 192.0 ** (-0.5)
+LOG2E_SCALE = softmax_scale * math.log2(math.e)
+MASKED = -1e30
 
 
 def slot_ranks(holders):
@@ -28,7 +37,7 @@
     return jnp.sum(jnp.where(hits, local_tile[..., None] + 1, 0), axis=-2) - 1
 
 
-def shards(queries, latent_cache, tile_lists):
+def shards_general(queries, latent_cache, tile_lists):
     width = latent_cache.shape[1]
     listing = tile_lists[0]
     me = lax.axis_index("ctx")
@@ -59,7 +68,7 @@
         jnp.einsum("qhc,kc->qhk", queries, keys, preferred_element_type=jnp.float32) * softmax_scale
     )
     allowed = (key_ok[None, :] & (key_pos[None, :] <= query_pos[:, None]))[:, None, :]
-    scores = jnp.where(allowed, scores, -1e30)
+    scores = jnp.where(allowed, scores, MASKED)
     top = jnp.max(scores, axis=-1, keepdims=True)
     expo = jnp.where(allowed, jnp.exp(scores - top), 0.0)
     total = jnp.sum(expo, axis=-1, keepdims=True)
@@ -68,12 +77,218 @@
     return (summed / total).astype(jnp.bfloat16)
 
 
+def side_by_side(sel_ref, entry, blocks, out_ref):
+    for at in range(0, len(blocks), 2):
+        pair = []
+        for upper in (False, True):
+            block = blocks[at + upper][...]
+            swapped = jnp.concatenate([block[:, TILE:], block[:, :TILE]], axis=1)
+            odd = sel_ref[entry + at + upper] % 2 == 1
+            pair.append(jnp.where(odd != upper, swapped, block))
+        out_ref[:, at * TILE : (at + 2) * TILE] = jnp.concatenate(
+            [pair[0][:, :TILE], pair[1][:, TILE:]], axis=1
+        )
+
+
+def tile_blocks(width, entries):
+    return [
+        pl.BlockSpec((width, 2 * TILE), lambda i, sel, entry=entry: (0, sel[entry] // 2))
+        for entry in entries
+    ]
+
+
+def pick_kernel(sel_ref, *refs):
+    side_by_side(sel_ref, 0, refs[:-1], refs[-1])
+
+
+def pick_tiles(sel, caches):
+    width = caches[0].shape[0]
+    columns = len(caches) * TILE
+    return pl.pallas_call(
+        pick_kernel,
+        grid_spec=pltpu.PrefetchScalarGridSpec(
+            num_scalar_prefetch=1,
+            grid=(1,),
+            in_specs=tile_blocks(width, range(len(caches))),
+            out_specs=pl.BlockSpec((width, columns), lambda i, sel: (0, 0)),
+        ),
+        out_shape=jax.ShapeDtypeStruct((width, columns), caches[0].dtype),
+        compiler_params=pltpu.CompilerParams(vmem_limit_bytes=6 << 20),
+        cost_estimate=pl.CostEstimate(
+            flops=0, transcendentals=0, bytes_accessed=4 * columns * width
+        ),
+        name="pick_tiles",
+    )(sel, *caches)
+
+
+def attend_kernel(heads, entry, first, sel_ref, *refs):
+    count = ROW if not first else 2 * ROW
+    blocks, refs = refs[:count], refs[count:]
+    if first:
+        bias_ref, q_ref, out_ref, top_ref, total_ref, keys_ref = refs
+    else:
+        far_ref, q_ref, mean_ref, top_ref, total_ref, out_ref, keys_ref = refs
+    rows = q_ref.shape[0]
+    lanes = 2 * TILE
+    z = lax.axis_index("ctx") // ROW
+
+    def pieces(array):
+        return [array[:, at : at + lanes] for at in range(0, array.shape[1], lanes)]
+
+    def load():
+        side_by_side(sel_ref, entry, blocks, keys_ref)
+        if not first:
+            keys_ref[:, count * TILE :] = far_ref[...]
+
+    def merge():
+        scores = jnp.dot(q_ref[...], keys_ref[...], preferred_element_type=jnp.float32)
+        if first:
+            scores = scores.reshape(rows // heads, heads, -1) + bias_ref[...][:, None, :]
+            scores = pieces(scores.reshape(rows, -1))
+        else:
+            scores = pieces(scores)
+            far_bias = jnp.where(z >= DEPTH - 1, 0.0, MASKED)
+            half = len(scores) // 2
+            scores[half:] = [piece + far_bias for piece in scores[half:]]
+        top = jnp.max(functools.reduce(jnp.maximum, scores), axis=1, keepdims=True)
+        top = jnp.broadcast_to(top, (rows, lanes))
+        if not first:
+            top_before = top_ref[...]
+            top = jnp.maximum(top, top_before)
+        scaled_top = top * LOG2E_SCALE
+        expo = [jnp.exp2(piece * LOG2E_SCALE - scaled_top) for piece in scores]
+        total = jnp.sum(functools.reduce(jnp.add, expo), axis=1, keepdims=True)
+        total = jnp.broadcast_to(total, (rows, lanes))
+        expo = jnp.concatenate([piece.astype(jnp.bfloat16) for piece in expo], axis=1)
+        summed = lax.dot_general(
+            expo, keys_ref[:LAT, :], (((1,), (1,)), ((), ())), preferred_element_type=jnp.float32
+        )
+        summed = pieces(summed)
+        if first:
+            scale = 1.0 / total
+            result = [piece * scale for piece in summed]
+            top_ref[...] = top
+            total_ref[...] = total
+        else:
+            before = total_ref[...] * jnp.exp2(top_before * LOG2E_SCALE - scaled_top)
+            scale = 1.0 / (total + before)
+            share = before * scale
+            result = [
+                piece * scale + mean.astype(jnp.float32) * share
+                for piece, mean in zip(summed, pieces(mean_ref[...]))
+            ]
+        for at, piece in enumerate(result):
+            out_ref[:, at * lanes : (at + 1) * lanes] = piece.astype(out_ref.dtype)
+
+    if first:
+        pl.when(pl.program_id(0) == 0)(load)
+        merge()
+    else:
+        seen = z >= DEPTH - 2
+        pl.when(seen & (pl.program_id(0) == 0))(load)
+        pl.when(seen)(merge)
+
+        @pl.when(jnp.logical_not(seen))
+        def _():
+            out_ref[...] = mean_ref[...]
+
+
+def attend(queries, sel, entry, caches, bias=None, far=None, state=()):
+    count, heads, width = queries.shape
+    first = bias is not None
+    keys = 2 * ROW * TILE
+    step = 16
+    rows = step * heads
+
+    def rows_of(width):
+        return pl.BlockSpec((rows, width), lambda i, sel: (i, 0))
+
+    mean = jax.ShapeDtypeStruct((count * heads, LAT), jnp.bfloat16)
+    stats = jax.ShapeDtypeStruct((count * heads, 2 * TILE), jnp.float32)
+    grid_spec = pltpu.PrefetchScalarGridSpec(
+        num_scalar_prefetch=1,
+        grid=(count // step,),
+        in_specs=tile_blocks(width, range(entry, entry + len(caches)))
+        + [
+            pl.BlockSpec((step, keys), lambda i, sel: (i, 0))
+            if first
+            else pl.BlockSpec(far.shape, lambda i, sel: (0, 0))
+        ]
+        + [rows_of(width)]
+        + ([] if first else [rows_of(LAT), rows_of(2 * TILE), rows_of(2 * TILE)]),
+        out_specs=[rows_of(LAT), rows_of(2 * TILE), rows_of(2 * TILE)] if first else rows_of(LAT),
+        scratch_shapes=[pltpu.VMEM((width, keys), jnp.bfloat16)],
+    )
+    return pl.pallas_call(
+        functools.partial(attend_kernel, heads, entry, first),
+        grid_spec=grid_spec,
+        out_shape=[mean, stats, stats] if first else mean,
+        compiler_params=pltpu.CompilerParams(
+            vmem_limit_bytes=24 << 20, dimension_semantics=("arbitrary",)
+        ),
+        cost_estimate=pl.CostEstimate(
+            flops=2 * count * heads * keys * (width + LAT),
+            transcendentals=count * heads * keys,
+            bytes_accessed=2 * count * heads * (width + LAT),
+        ),
+        name="attend_near" if first else "attend_rest",
+    )(sel, *caches, bias if first else far, queries.reshape(count * heads, width), *state)
+
+
+def shards_rows(queries, latent_cache, tile_lists):
+    size = lax.axis_size("ctx")
+    span = size - ROW
+    me = lax.axis_index("ctx")
+    z, r = me // ROW, me % ROW
+
+    def beside(array, m):
+        return lax.ppermute(array, "ctx", [(i, i ^ m) for i in range(size)])
+
+    def further(array, rows, sources):
+        return lax.ppermute(array, "ctx", [(i, i + ROW * rows) for i in sources])
+
+    def named_tiles(listing, holders):
+        hit = (listing >= 0) & (listing // TILES_DEV == holders[:, None])
+        return jnp.sum(jnp.where(hit, listing % TILES_DEV, 0), axis=1)
+
+    cache = latent_cache.T
+    cache1 = further(cache, 1, range(span))
+    far_list = lax.ppermute(tile_lists, "ctx", [(i + span, i) for i in range(ROW)])
+    across = beside(cache, 2)
+    row0 = [cache, beside(cache, 1), across, beside(across, 1)]
+
+    slot = jnp.arange((DEPTH - 1) * ROW, dtype=jnp.int32)
+    sel = named_tiles(tile_lists, ROW * (z - slot // ROW) + (r ^ slot % ROW))
+
+    cache2 = further(cache1, 1, range(ROW, span))
+    far = pick_tiles(named_tiles(far_list, me ^ jnp.arange(ROW, dtype=jnp.int32)), row0)
+    far = further(far, DEPTH - 1, range(ROW))
+    across = beside(cache1, 2)
+    row1 = [cache1, beside(cache1, 1), across, beside(across, 1)]
+
+    slot = jnp.arange(2 * ROW * TILE, dtype=jnp.int32)
+    k, m, offset = slot // (ROW * TILE), slot // TILE % ROW, slot % TILE
+    seen = jnp.where(k == 0, (r ^ m) <= r, k <= z)
+    query = jnp.arange(queries.shape[0], dtype=jnp.int32)[:, None]
+    seen = seen & ((k > 0) | (m > 0) | (offset <= query))
+    bias = jnp.where(seen, 0.0, MASKED).astype(jnp.float32)
+
+    state = attend(queries, sel, 0, [*row0, *row1], bias=bias)
+    across, beside2 = beside(cache2, 2), beside(cache2, 1)
+    across, *state = lax.optimization_barrier((across, *state))
+    row2 = [cache2, beside2, across, beside(across, 1)]
+    out = attend(queries, sel, 2 * ROW, row2, far=far, state=state)
+    return out.reshape(*queries.shape[:2], LAT)
+
+
 def solution(mesh):
     placed = (
         P(("groups", "ctx"), None, None),
         P(("groups", "ctx"), None),
         P(("groups", "ctx"), None),
     )
+    size = mesh.shape["ctx"]
+    shards = shards_rows if size == ROW * DEPTH else shards_general
     return jax.shard_map(
         shards,
         mesh=mesh,

time: 140 us -> 50.9 us (0.36); the launches traced: 137 us -> 50.6 us
  other arithmetic: 36.2 us -> 1.77 us
  matrix products: 33.4 us -> 0 us
  Pallas kernels: 0 us -> 19.1 us
  blocking collectives: 17.3 us -> 0 us
  waiting for transfers between devices: 24.1 us -> 10.6 us
  local copies, waits for them, and re-layouts: 17.6 us -> 4.41 us
  starting transfers between devices: 8.47 us -> 14.5 us
    dot_general x2 -> x0, matrix products: 33.4 us -> none  [the longest x1 19.6 us: shards(): jnp.einsum('qhc,kc->qhk', queries, keys, preferred_element_type=jnp.float32)]
    sub x1 -> x0, other arithmetic: 32.5 us -> none  [shards(): expo = jnp.where(allowed, jnp.exp(scores - top), 0.0)]
    all_to_all x1 -> x0, waiting for transfers between devices: 24.1 us -> none  [shards(): lax.all_to_all(outgoing, 'ctx', split_axis=0, concat_axis=0, tiled=True)]
    pallas_call x0 -> x3, Pallas kernels: none -> 19.1 us  [the longest x2 18.3 us: attend(): pl.pallas_call(functools.partial(attend_kernel, heads, entry, first), gri...]
    all_gather x1 -> x0, blocking collectives: 17.3 us -> none  [shards(): lists_all = lax.all_gather(tile_lists, 'ctx', axis=0, tiled=True)]
    ppermute x0 -> x13, starting transfers between devices: none -> 14.5 us  [the longest x9 6.86 us: beside(): return lax.ppermute(array, 'ctx', [(i, i ^ m) for i in range(size)])]
    ppermute x0 -> x13, waiting for transfers between devices: none -> 10.6 us  [the longest x9 6.55 us: beside(): return lax.ppermute(array, 'ctx', [(i, i ^ m) for i in range(size)])]
    gather x3 -> x0, local copies, waits for them, and re-layouts: 9.38 us -> none  [the longest x2 8.04 us: shards(): keys = jnp.take(incoming, position, axis=0)]
  transfers between devices with their start and end apart: 1 -> 13, of which waited for: 1 -> 3; matrix products, arithmetic and copies ran while one was open for 1% -> 3% of each run, Pallas kernels for 0% -> 19%
where the time goes in v2:
time: 50.9 us; the launch traced here: 50.6 us
  Pallas kernels  19.1 us (38%)
  starting transfers between devices  14.5 us (28%)
  waiting for transfers between devices  10.6 us (21%)
  local copies, waits for them, and re-layouts  4.41 us (9%)
  other arithmetic  1.77 us (3%)
    pallas_call x2, Pallas kernels, attend(): pl.pallas_call(functools.partial(attend_kernel, heads, entry, first), gri...  18.3 us
    ppermute x9, starting transfers between devices, beside(): return lax.ppermute(array, 'ctx', [(i, i ^ m) for i in range(size)])  6.86 us
    ppermute x9, waiting for transfers between devices, beside(): return lax.ppermute(array, 'ctx', [(i, i ^ m) for i in range(size)])  6.55 us
    unnamed x8, local copies, waits for them, and re-layouts  4.41 us
    ppermute x3, waiting for transfers between devices, further(): return lax.ppermute(array, 'ctx', [(i, i + ROW * rows) for i in sources])  4.05 us
    ppermute x3, starting transfers between devices, further(): return lax.ppermute(array, 'ctx', [(i, i + ROW * rows) for i in sources])  3.85 us
    ppermute x1, starting transfers between devices, shards_rows(): lax.ppermute(tile_lists, 'ctx', [(i + span, i) for i in range(ROW)])  3.78 us
  transfers between devices with their start and end apart: 13, of which 3 were waited for; matrix products, arithmetic and copies ran while one was open for 3% of the time, Pallas kernels for 19%

profile of v2, /device:TPU:25, one launch (start us, length us, event | category | flops | bytes accessed | tf_op | source)
XLA Modules:
  0.0 50.6 jit_solution(3285978864791104763)
XLA Ops:
  0.0 1.2 %collective-permute-start.5 = (bf16[576,256]{1,0:T(8,128)(2,1)}, bf16[576,256]{1,0:T(8,128)(2,1)S(1)}, u32[]{:S(2)}, u32[]{:S(2)}) collective-permute-start(bf16[576,256]{1,0:T(8,128)(2,1)} %bitcast.17), channel_id=1, source_target_pairs={{0,2},{1,3},{2,0},{3,1},{4,6},{5,7},{6,4},{7,5},{8,10},{9,11},{10,... | collective-permute-start | bytes 884744 | tf_op jit(solution)/shard_map/ppermute | solution.py:245
  1.2 1.0 %collective-permute-start.4 = (bf16[576,256]{1,0:T(8,128)(2,1)}, bf16[576,256]{1,0:T(8,128)(2,1)S(1)}, u32[]{:S(2)}, u32[]{:S(2)}) collective-permute-start(bf16[576,256]{1,0:T(8,128)(2,1)} %bitcast.18), channel_id=1, source_target_pairs={{0,1},{1,0},{2,3},{3,2},{4,5},{5,4},{6,7},{7,6},{8,9},{9,8},{10,11... | collective-permute-start | bytes 884744 | tf_op jit(solution)/shard_map/ppermute | solution.py:245
  2.2 1.3 %collective-permute-start = (bf16[576,256]{1,0:T(8,128)(2,1)}, bf16[576,256]{1,0:T(8,128)(2,1)S(1)}, u32[]{:S(2)}, u32[]{:S(2)}) collective-permute-start(bf16[576,256]{1,0:T(8,128)(2,1)} %bitcast.19), channel_id=1, source_target_pairs={{0,4},{1,5},{2,6},{3,7},{4,8},{5,9},{6,10},{7,11},{8,12},{9,13},{1... | collective-permute-start | bytes 884744 | tf_op jit(solution)/shard_map/ppermute | solution.py:248
  3.5 3.8 %collective-permute-start.11 = (s32[1,32]{1,0:T(1,128)}, s32[1,32]{1,0:T(1,128)S(1)}, u32[]{:S(2)}, u32[]{:S(2)}) collective-permute-start(s32[1,32]{1,0:T(1,128)} %param.5), channel_id=1, source_target_pairs={{12,0},{13,1},{14,2},{15,3},{28,16},{29,17},{30,18},{31,19}} | collective-permute-start | bytes 392 | tf_op jit(solution)/shard_map/ppermute | solution.py:256
  7.3 0.7 %compare_bitcast_fusion.1 = pred[32]{0:T(512)(128)(4,1)S(1)} fusion(s32[1,32]{1,0:T(1,128)} %param.5), kind=kLoop, calls=%fused_computation.37 | loop fusion | flops 32 | bytes 160 | tf_op jit(solution)/shard_map/and | solution.py:251
  7.9 0.7 %fusion.21 = (s32[32]{0:T(128)S(1)}, s32[32]{0:T(128)S(1)}) fusion(s32[1,32]{1,0:T(1,128)} %param.5), kind=kLoop, calls=%fused_computation.54 | loop fusion | flops 608 | bytes 384 | tf_op jit(solution)/shard_map/eq | solution.py:251
  8.6 0.2 select_reduce_fusion.sel_ref
  8.9 4.0 %collective-permute-done.refs_4_ = bf16[576,256]{1,0:T(8,128)(2,1)S(1)} collective-permute-done((bf16[576,256]{1,0:T(8,128)(2,1)}, bf16[576,256]{1,0:T(8,128)(2,1)S(1)}, u32[]{:S(2)}, u32[]{:S(2)}) %collective-permute-start) | collective-permute-done | bytes 294944 | tf_op jit(solution)/shard_map/ppermute | solution.py:248
  12.9 0.2 collective-permute-start.8
  13.2 1.1 %collective-permute-start.7 = (bf16[576,256]{1,0:T(8,128)(2,1)S(1)}, bf16[576,256]{1,0:T(8,128)(2,1)S(1)}, u32[]{:S(2)}, u32[]{:S(2)}) collective-permute-start(bf16[576,256]{1,0:T(8,128)(2,1)S(1)} %collective-permute-done.refs_4_), channel_id=1, source_target_pairs={{0,1},{1,0},{2,3},{3,2},{4,5},{5,4},{6,7},{7,6},{8,9},{9,8},{10,11... | collective-permute-start | bytes 884744 | tf_op jit(solution)/shard_map/ppermute | solution.py:245
  14.3 1.3 %collective-permute-start.1 = (bf16[576,256]{1,0:T(8,128)(2,1)S(1)}, bf16[576,256]{1,0:T(8,128)(2,1)S(1)}, u32[]{:S(2)}, u32[]{:S(2)}) collective-permute-start(bf16[576,256]{1,0:T(8,128)(2,1)S(1)} %collective-permute-done.refs_4_), channel_id=1, source_target_pairs={{4,8},{5,9},{6,10},{7,11},{8,12},{9,13},{10,14},{11,15},{20,24},{2... | collective-permute-start | bytes 884744 | tf_op jit(solution)/shard_map/ppermute | solution.py:248
  15.7 5.0 %collective-permute-done.8.refs_6_ = bf16[576,256]{1,0:T(8,128)(2,1)S(1)} collective-permute-done((bf16[576,256]{1,0:T(8,128)(2,1)S(1)}, bf16[576,256]{1,0:T(8,128)(2,1)S(1)}, u32[]{:S(2)}, u32[]{:S(2)}) %collective-permute-start.8) | collective-permute-done | bytes 294944 | tf_op jit(solution)/shard_map/ppermute | solution.py:245
  20.7 1.7 %collective-permute-start.9 = (bf16[576,256]{1,0:T(8,128)(2,1)S(1)}, bf16[576,256]{1,0:T(8,128)(2,1)S(1)}, u32[]{:S(2)}, u32[]{:S(2)}) collective-permute-start(bf16[576,256]{1,0:T(8,128)(2,1)S(1)} %collective-permute-done.8.refs_6_), channel_id=1, source_target_pairs={{0,1},{1,0},{2,3},{3,2},{4,5},{5,4},{6,7},{7,6},{8,9},{9,8},{10,11... | collective-permute-start | bytes 884744 | tf_op jit(solution)/shard_map/ppermute | solution.py:245
  22.4 0.2 select_reduce_fusion.1.sel_ref
  22.6 1.0 %copy-done.2 = bf16[256,576]{0,1:T(8,128)(2,1)S(1)} copy-done((bf16[256,576]{0,1:T(8,128)(2,1)S(1)}, bf16[256,576]{0,1:T(8,128)(2,1)}, u32[]{:S(2)}) %copy-start.2) | copy-done | bytes 294936
  23.5 0.8 %pick_tiles.1 = bf16[576,256]{1,0:T(8,128)(2,1)S(1)} custom-call(s32[4]{0:T(128)S(1)} %select_reduce_fusion.1.sel_ref, bf16[576,256]{1,0:T(8,128)(2,1)S(1)} %bitcast.20, bf16[576,256]{1,0:T(8,128)(2,1)S(1)} %collective-permute-done.4.refs_1_, bf16[576,256]{1,0:T(8,128)(2,1)S(1)} %collective-permute-done.5.refs_2_, ...), custom_call_target="tpu_custom_call" | custom-call | bytes 589824 | tf_op jit(solution)/shard_map/pick_tiles/pallas_call | solution.py:107
  24.3 1.3 %collective-permute-start.12 = (bf16[576,256]{1,0:T(8,128)(2,1)S(1)}, bf16[576,256]{1,0:T(8,128)(2,1)S(1)}, u32[]{:S(2)}, u32[]{:S(2)}) collective-permute-start(bf16[576,256]{1,0:T(8,128)(2,1)S(1)} %pick_tiles.1), channel_id=1, source_target_pairs={{0,12},{1,13},{2,14},{3,15},{16,28},{17,29},{18,30},{19,31}} | collective-permute-start | bytes 884744 | tf_op jit(solution)/shard_map/ppermute | solution.py:248
  25.7 0.4 collective-permute-start.3
  26.0 1.1 %collective-permute-start.2 = (bf16[576,256]{1,0:T(8,128)(2,1)S(1)}, bf16[576,256]{1,0:T(8,128)(2,1)S(1)}, u32[]{:S(2)}, u32[]{:S(2)}) collective-permute-start(bf16[576,256]{1,0:T(8,128)(2,1)S(1)} %collective-permute-done.1.refs_0_), channel_id=1, source_target_pairs={{0,1},{1,0},{2,3},{3,2},{4,5},{5,4},{6,7},{7,6},{8,9},{9,8},{10,11... | collective-permute-start | bytes 884744 | tf_op jit(solution)/shard_map/ppermute | solution.py:245
  27.1 2.5 %copy-done = bf16[64,64,576]{2,1,0:T(8,128)(2,1)S(1)} copy-done((bf16[64,64,576]{2,1,0:T(8,128)(2,1)S(1)}, bf16[64,64,576]{2,1,0:T(8,128)(2,1)}, u32[]{:S(2)}) %copy-start) | copy-done | bytes 4718616
  29.6 1.0 %copy-done.3 = bf16[256,576]{0,1:T(8,128)(2,1)S(1)} copy-done((bf16[256,576]{0,1:T(8,128)(2,1)S(1)}, bf16[256,576]{0,1:T(8,128)(2,1)}, u32[]{:S(2)}) %copy-start.3) | copy-done | bytes 294936
  30.6 8.6 %attend_near.1 = (bf16[4096,512]{1,0:T(8,128)(2,1)S(1)}, f32[4096,128]{1,0:T(8,128)S(1)}, f32[4096,128]{1,0:T(8,128)S(1)}) custom-call(s32[12]{0:T(128)S(1)} %select_reduce_fusion.sel_ref, bf16[576,256]{1,0:T(8,128)(2,1)S(1)} %bitcast.21, bf16[576,256]{1,0:T(8,128)(2,1)S(1)} %collective-permute-done.4.refs_1_, ...), custom_call_target="tpu_custom_call" | custom-call | flops 4563402752 | bytes 8912896 | tf_op jit(solution)/shard_map/attend_near/pallas_call | solution.py:222
  39.3 1.5 %collective-permute-done.10.refs_3_ = bf16[576,256]{1,0:T(8,128)(2,1)S(1)} collective-permute-done((bf16[576,256]{1,0:T(8,128)(2,1)S(1)}, bf16[576,256]{1,0:T(8,128)(2,1)S(1)}, u32[]{:S(2)}, u32[]{:S(2)}) %collective-permute-start.10) | collective-permute-done | bytes 294944 | tf_op jit(solution)/shard_map/ppermute | solution.py:245
  40.8 9.7 %attend_rest.1 = bf16[4096,512]{1,0:T(8,128)(2,1)} custom-call(s32[12]{0:T(128)S(1)} %select_reduce_fusion.sel_ref, bf16[576,256]{1,0:T(8,128)(2,1)S(1)} %collective-permute-done.1.refs_0_, bf16[576,256]{1,0:T(8,128)(2,1)S(1)} %collective-permute-done.2.refs_1_, bf16[576,256]{1,0:T(8,128)(2,1)S(1)} %collective-permute-done.3.refs_2_, ...), custom_call_target="tpu_custom_call" | custom-call | flops 4563402752 | bytes 8912896 | tf_op jit(solution)/shard_map/attend_rest/pallas_call | solution.py:222
  (24 shorter events, 0.3 us)
Async XLA Ops:
  0.0 15.6 %collective-permute-start.5 = (bf16[576,256]{1,0:T(8,128)(2,1)}, bf16[576,256]{1,0:T(8,128)(2,1)S(1)}, u32[]{:S(2)}, u32[]{:S(2)}) collective-permute-start(bf16[576,256]{1,0:T(8,128)(2,1)} %bitcast.17), channel_id=1, source_target_pairs={{0,2},{1,3},{2,0},{3,1},{4,6},{5,7},{6,4},{7,5},{8,10},{9,11},{10,... | collective-permute-start | bytes 884744 | tf_op jit(solution)/shard_map/ppermute | solution.py:245
  1.2 21.3 %collective-permute-start.4 = (bf16[576,256]{1,0:T(8,128)(2,1)}, bf16[576,256]{1,0:T(8,128)(2,1)S(1)}, u32[]{:S(2)}, u32[]{:S(2)}) collective-permute-start(bf16[576,256]{1,0:T(8,128)(2,1)} %bitcast.18), channel_id=1, source_target_pairs={{0,1},{1,0},{2,3},{3,2},{4,5},{5,4},{6,7},{7,6},{8,9},{9,8},{10,11... | collective-permute-start | bytes 884744 | tf_op jit(solution)/shard_map/ppermute | solution.py:245
  2.2 10.7 %collective-permute-start = (bf16[576,256]{1,0:T(8,128)(2,1)}, bf16[576,256]{1,0:T(8,128)(2,1)S(1)}, u32[]{:S(2)}, u32[]{:S(2)}) collective-permute-start(bf16[576,256]{1,0:T(8,128)(2,1)} %bitcast.19), channel_id=1, source_target_pairs={{0,4},{1,5},{2,6},{3,7},{4,8},{5,9},{6,10},{7,11},{8,12},{9,13},{1... | collective-permute-start | bytes 884744 | tf_op jit(solution)/shard_map/ppermute | solution.py:248
  3.5 9.7 %collective-permute-start.11 = (s32[1,32]{1,0:T(1,128)}, s32[1,32]{1,0:T(1,128)S(1)}, u32[]{:S(2)}, u32[]{:S(2)}) collective-permute-start(s32[1,32]{1,0:T(1,128)} %param.5), channel_id=1, source_target_pairs={{12,0},{13,1},{14,2},{15,3},{28,16},{29,17},{30,18},{31,19}} | collective-permute-start | bytes 392 | tf_op jit(solution)/shard_map/ppermute | solution.py:256
  12.9 7.8 %collective-permute-start.8 = (bf16[576,256]{1,0:T(8,128)(2,1)S(1)}, bf16[576,256]{1,0:T(8,128)(2,1)S(1)}, u32[]{:S(2)}, u32[]{:S(2)}) collective-permute-start(bf16[576,256]{1,0:T(8,128)(2,1)S(1)} %collective-permute-done.refs_4_), channel_id=1, source_target_pairs={{0,2},{1,3},{2,0},{3,1},{4,6},{5,7},{6,4},{7,5},{8,10},{9,11},{10,... | collective-permute-start | bytes 884744 | tf_op jit(solution)/shard_map/ppermute | solution.py:245
  13.2 14.0 %collective-permute-start.7 = (bf16[576,256]{1,0:T(8,128)(2,1)S(1)}, bf16[576,256]{1,0:T(8,128)(2,1)S(1)}, u32[]{:S(2)}, u32[]{:S(2)}) collective-permute-start(bf16[576,256]{1,0:T(8,128)(2,1)S(1)} %collective-permute-done.refs_4_), channel_id=1, source_target_pairs={{0,1},{1,0},{2,3},{3,2},{4,5},{5,4},{6,7},{7,6},{8,9},{9,8},{10,11... | collective-permute-start | bytes 884744 | tf_op jit(solution)/shard_map/ppermute | solution.py:245
  14.3 11.3 %collective-permute-start.1 = (bf16[576,256]{1,0:T(8,128)(2,1)S(1)}, bf16[576,256]{1,0:T(8,128)(2,1)S(1)}, u32[]{:S(2)}, u32[]{:S(2)}) collective-permute-start(bf16[576,256]{1,0:T(8,128)(2,1)S(1)} %collective-permute-done.refs_4_), channel_id=1, source_target_pairs={{4,8},{5,9},{6,10},{7,11},{8,12},{9,13},{10,14},{11,15},{20,24},{2... | collective-permute-start | bytes 884744 | tf_op jit(solution)/shard_map/ppermute | solution.py:248
  15.6 6.9 %collective-permute-start.6 = (bf16[576,256]{1,0:T(8,128)(2,1)S(1)}, bf16[576,256]{1,0:T(8,128)(2,1)S(1)}, u32[]{:S(2)}, u32[]{:S(2)}) collective-permute-start(bf16[576,256]{1,0:T(8,128)(2,1)S(1)} %collective-permute-done.5.refs_2_), channel_id=1, source_target_pairs={{0,1},{1,0},{2,3},{3,2},{4,5},{5,4},{6,7},{7,6},{8,9},{9,8},{10,11... | collective-permute-start | bytes 884744 | tf_op jit(solution)/shard_map/ppermute | solution.py:245
  20.7 6.5 %collective-permute-start.9 = (bf16[576,256]{1,0:T(8,128)(2,1)S(1)}, bf16[576,256]{1,0:T(8,128)(2,1)S(1)}, u32[]{:S(2)}, u32[]{:S(2)}) collective-permute-start(bf16[576,256]{1,0:T(8,128)(2,1)S(1)} %collective-permute-done.8.refs_6_), channel_id=1, source_target_pairs={{0,1},{1,0},{2,3},{3,2},{4,5},{5,4},{6,7},{7,6},{8,9},{9,8},{10,11... | collective-permute-start | bytes 884744 | tf_op jit(solution)/shard_map/ppermute | solution.py:245
  22.6 1.0 %copy-start.2 = (bf16[256,576]{0,1:T(8,128)(2,1)S(1)}, bf16[256,576]{0,1:T(8,128)(2,1)}, u32[]{:S(2)}) copy-start(bf16[256,576]{0,1:T(8,128)(2,1)} %param.4) | copy-start | bytes 884740
  24.3 14.9 %collective-permute-start.12 = (bf16[576,256]{1,0:T(8,128)(2,1)S(1)}, bf16[576,256]{1,0:T(8,128)(2,1)S(1)}, u32[]{:S(2)}, u32[]{:S(2)}) collective-permute-start(bf16[576,256]{1,0:T(8,128)(2,1)S(1)} %pick_tiles.1), channel_id=1, source_target_pairs={{0,12},{1,13},{2,14},{3,15},{16,28},{17,29},{18,30},{19,31}} | collective-permute-start | bytes 884744 | tf_op jit(solution)/shard_map/ppermute | solution.py:248
  25.7 13.5 %collective-permute-start.3 = (bf16[576,256]{1,0:T(8,128)(2,1)S(1)}, bf16[576,256]{1,0:T(8,128)(2,1)S(1)}, u32[]{:S(2)}, u32[]{:S(2)}) collective-permute-start(bf16[576,256]{1,0:T(8,128)(2,1)S(1)} %collective-permute-done.1.refs_0_), channel_id=1, source_target_pairs={{0,2},{1,3},{2,0},{3,1},{4,6},{5,7},{6,4},{7,5},{8,10},{9,11},{10,... | collective-permute-start | bytes 884744 | tf_op jit(solution)/shard_map/ppermute | solution.py:245
  26.0 13.2 %collective-permute-start.2 = (bf16[576,256]{1,0:T(8,128)(2,1)S(1)}, bf16[576,256]{1,0:T(8,128)(2,1)S(1)}, u32[]{:S(2)}, u32[]{:S(2)}) collective-permute-start(bf16[576,256]{1,0:T(8,128)(2,1)S(1)} %collective-permute-done.1.refs_0_), channel_id=1, source_target_pairs={{0,1},{1,0},{2,3},{3,2},{4,5},{5,4},{6,7},{7,6},{8,9},{9,8},{10,11... | collective-permute-start | bytes 884744 | tf_op jit(solution)/shard_map/ppermute | solution.py:245
  27.1 2.5 %copy-start = (bf16[64,64,576]{2,1,0:T(8,128)(2,1)S(1)}, bf16[64,64,576]{2,1,0:T(8,128)(2,1)}, u32[]{:S(2)}) copy-start(bf16[64,64,576]{2,1,0:T(8,128)(2,1)} %param.3) | copy-start | bytes 14155780
  29.6 1.0 %copy-start.3 = (bf16[256,576]{0,1:T(8,128)(2,1)S(1)}, bf16[256,576]{0,1:T(8,128)(2,1)}, u32[]{:S(2)}) copy-start(bf16[256,576]{0,1:T(8,128)(2,1)} %param.4) | copy-start | bytes 884740
  30.6 10.2 %copy-start.1 = (bf16[64,64,576]{2,1,0:T(8,128)(2,1)S(1)}, bf16[64,64,576]{2,1,0:T(8,128)(2,1)}, u32[]{:S(2)}) copy-start(bf16[64,64,576]{2,1,0:T(8,128)(2,1)} %param.3) | copy-start | bytes 14155780
  39.2 1.6 %collective-permute-start.10 = (bf16[576,256]{1,0:T(8,128)(2,1)S(1)}, bf16[576,256]{1,0:T(8,128)(2,1)S(1)}, u32[]{:S(2)}, u32[]{:S(2)}) collective-permute-start(bf16[576,256]{1,0:T(8,128)(2,1)S(1)} %collective-permute-done.3.refs_2_), channel_id=1, source_target_pairs={{0,1},{1,0},{2,3},{3,2},{4,5},{5,4},{6,7},{7,6},{8,9},{9,8},{10,11... | collective-permute-start | bytes 884744 | tf_op jit(solution)/shard_map/ppermute | solution.py:245

commit v3 on v2

--- a/solution.py
+++ b/solution.py
@@ -14,6 +14,7 @@
 CAP = 1
 TILES_DEV = 4
 ROW = 4
+STAGES = 4
 DEPTH = 4
 
 
@@ -121,27 +122,63 @@
     )(sel, *caches)
 
 
-def attend_kernel(heads, entry, first, sel_ref, *refs):
-    count = ROW if not first else 2 * ROW
+def stage_kernel(*refs):
+    *refs, sems = refs
+    half = len(refs) // 2
+    copies = []
+    for source_ref, out_ref in zip(refs[:half], refs[half:]):
+        rows = source_ref.shape[0] // STAGES
+        for at in range(STAGES):
+            block = pl.ds(at * rows, rows)
+            copies.append(
+                pltpu.make_async_copy(
+                    source_ref.at[block, :], out_ref.at[block, :], sems.at[len(copies)]
+                )
+            )
+    for copy in copies:
+        copy.start()
+    for copy in copies:
+        copy.wait()
+
+
+def stage(*arrays):
+    return pl.pallas_call(
+        stage_kernel,
+        in_specs=[pl.BlockSpec(memory_space=pltpu.HBM)] * len(arrays),
+        out_specs=[pl.BlockSpec(memory_space=pltpu.VMEM)] * len(arrays),
+        out_shape=[pltpu.VMEM(array.shape, array.dtype) for array in arrays],
+        scratch_shapes=[pltpu.SemaphoreType.DMA((STAGES * len(arrays),))],
+        compiler_params=pltpu.CompilerParams(vmem_limit_bytes=8 << 20),
+        cost_estimate=pl.CostEstimate(
+            flops=0, transcendentals=0, bytes_accessed=4 * sum(array.size for array in arrays)
+        ),
+        name="stage",
+    )(*(pltpu.with_memory_space_constraint(array, pltpu.HBM) for array in arrays))
+
+
+def attend_kernel(heads, step, first, sel_ref, *refs):
+    count = 2 * ROW if first else ROW
     blocks, refs = refs[:count], refs[count:]
     if first:
         bias_ref, q_ref, out_ref, top_ref, total_ref, keys_ref = refs
     else:
         far_ref, q_ref, mean_ref, top_ref, total_ref, out_ref, keys_ref = refs
-    rows = q_ref.shape[0]
+    rows = step
     lanes = 2 * TILE
+    block = pl.ds(pl.multiple_of(pl.program_id(0) * rows, rows), rows)
+    written = block if first else slice(None)
     z = lax.axis_index("ctx") // ROW
 
     def pieces(array):
         return [array[:, at : at + lanes] for at in range(0, array.shape[1], lanes)]
 
     def load():
-        side_by_side(sel_ref, entry, blocks, keys_ref)
+        side_by_side(sel_ref, 0 if first else 2 * ROW, blocks, keys_ref)
         if not first:
-            keys_ref[:, count * TILE :] = far_ref[...]
+            keys_ref[:, ROW * TILE :] = far_ref[...]
 
     def merge():
-        scores = jnp.dot(q_ref[...], keys_ref[...], preferred_element_type=jnp.float32)
+        scores = jnp.dot(q_ref[block, :], keys_ref[...], preferred_element_type=jnp.float32)
         if first:
             scores = scores.reshape(rows // heads, heads, -1) + bias_ref[...][:, None, :]
             scores = pieces(scores.reshape(rows, -1))
@@ -153,7 +190,7 @@
         top = jnp.max(functools.reduce(jnp.maximum, scores), axis=1, keepdims=True)
         top = jnp.broadcast_to(top, (rows, lanes))
         if not first:
-            top_before = top_ref[...]
+            top_before = top_ref[block, :]
             top = jnp.maximum(top, top_before)
         scaled_top = top * LOG2E_SCALE
         expo = [jnp.exp2(piece * LOG2E_SCALE - scaled_top) for piece in scores]
@@ -167,18 +204,18 @@
         if first:
             scale = 1.0 / total
             result = [piece * scale for piece in summed]
-            top_ref[...] = top
-            total_ref[...] = total
+            top_ref[block, :] = top
+            total_ref[block, :] = total
         else:
-            before = total_ref[...] * jnp.exp2(top_before * LOG2E_SCALE - scaled_top)
+            before = total_ref[block, :] * jnp.exp2(top_before * LOG2E_SCALE - scaled_top)
             scale = 1.0 / (total + before)
             share = before * scale
             result = [
                 piece * scale + mean.astype(jnp.float32) * share
-                for piece, mean in zip(summed, pieces(mean_ref[...]))
+                for piece, mean in zip(summed, pieces(mean_ref[block, :]))
             ]
         for at, piece in enumerate(result):
-            out_ref[:, at * lanes : (at + 1) * lanes] = piece.astype(out_ref.dtype)
+            out_ref[written, at * lanes : (at + 1) * lanes] = piece.astype(out_ref.dtype)
 
     if first:
         pl.when(pl.program_id(0) == 0)(load)
@@ -190,11 +227,11 @@
 
         @pl.when(jnp.logical_not(seen))
         def _():
-            out_ref[...] = mean_ref[...]
-
-
-def attend(queries, sel, entry, caches, bias=None, far=None, state=()):
-    count, heads, width = queries.shape
+            out_ref[...] = mean_ref[block, :]
+
+
+def attend(queries, heads, sel, tiles, bias=None, state=()):
+    count, width = queries.shape[0] // heads, queries.shape[1]
     first = bias is not None
     keys = 2 * ROW * TILE
     step = 16
@@ -203,26 +240,28 @@
     def rows_of(width):
         return pl.BlockSpec((rows, width), lambda i, sel: (i, 0))
 
-    mean = jax.ShapeDtypeStruct((count * heads, LAT), jnp.bfloat16)
-    stats = jax.ShapeDtypeStruct((count * heads, 2 * TILE), jnp.float32)
+    if first:
+        in_specs = tile_blocks(width, range(2 * ROW))
+        in_specs.append(pl.BlockSpec((step, keys), lambda i, sel: (i, 0)))
+        tiles = (*tiles, bias)
+    else:
+        in_specs = tile_blocks(width, range(2 * ROW, 3 * ROW))
+        in_specs.append(pl.BlockSpec(memory_space=pltpu.VMEM))
+    in_specs.append(pl.BlockSpec(memory_space=pltpu.VMEM))
+    state_specs = [pl.BlockSpec(memory_space=pltpu.VMEM)] * 3
+    shape, dtype = (count * heads, LAT), queries.dtype
+    stats = pltpu.VMEM((count * heads, 2 * TILE), jnp.float32)
     grid_spec = pltpu.PrefetchScalarGridSpec(
         num_scalar_prefetch=1,
         grid=(count // step,),
-        in_specs=tile_blocks(width, range(entry, entry + len(caches)))
-        + [
-            pl.BlockSpec((step, keys), lambda i, sel: (i, 0))
-            if first
-            else pl.BlockSpec(far.shape, lambda i, sel: (0, 0))
-        ]
-        + [rows_of(width)]
-        + ([] if first else [rows_of(LAT), rows_of(2 * TILE), rows_of(2 * TILE)]),
-        out_specs=[rows_of(LAT), rows_of(2 * TILE), rows_of(2 * TILE)] if first else rows_of(LAT),
+        in_specs=in_specs if first else in_specs + state_specs,
+        out_specs=state_specs if first else rows_of(LAT),
         scratch_shapes=[pltpu.VMEM((width, keys), jnp.bfloat16)],
     )
     return pl.pallas_call(
-        functools.partial(attend_kernel, heads, entry, first),
+        functools.partial(attend_kernel, heads, rows, first),
         grid_spec=grid_spec,
-        out_shape=[mean, stats, stats] if first else mean,
+        out_shape=[pltpu.VMEM(shape, dtype), stats, stats] if first else jax.ShapeDtypeStruct(shape, dtype),
         compiler_params=pltpu.CompilerParams(
             vmem_limit_bytes=24 << 20, dimension_semantics=("arbitrary",)
         ),
@@ -232,7 +271,7 @@
             bytes_accessed=2 * count * heads * (width + LAT),
         ),
         name="attend_near" if first else "attend_rest",
-    )(sel, *caches, bias if first else far, queries.reshape(count * heads, width), *state)
+    )(sel, *tiles, queries, *state)
 
 
 def shards_rows(queries, latent_cache, tile_lists):
@@ -251,34 +290,40 @@
         hit = (listing >= 0) & (listing // TILES_DEV == holders[:, None])
         return jnp.sum(jnp.where(hit, listing % TILES_DEV, 0), axis=1)
 
+    shape = queries.shape
     cache = latent_cache.T
     cache1 = further(cache, 1, range(span))
+    across = beside(cache, 2)
     far_list = lax.ppermute(tile_lists, "ctx", [(i + span, i) for i in range(ROW)])
-    across = beside(cache, 2)
+    queries, cache = stage(queries.reshape(-1, shape[2]), cache)
+    cache, across = lax.optimization_barrier((cache, across))
     row0 = [cache, beside(cache, 1), across, beside(across, 1)]
+    cache1, queries = lax.optimization_barrier((cache1, queries))
 
     slot = jnp.arange((DEPTH - 1) * ROW, dtype=jnp.int32)
     sel = named_tiles(tile_lists, ROW * (z - slot // ROW) + (r ^ slot % ROW))
 
+    far = pick_tiles(named_tiles(far_list, me ^ jnp.arange(ROW, dtype=jnp.int32)), row0)
     cache2 = further(cache1, 1, range(ROW, span))
-    far = pick_tiles(named_tiles(far_list, me ^ jnp.arange(ROW, dtype=jnp.int32)), row0)
+    across, beside1 = beside(cache1, 2), beside(cache1, 1)
+    across, far = lax.optimization_barrier((across, far))
     far = further(far, DEPTH - 1, range(ROW))
-    across = beside(cache1, 2)
-    row1 = [cache1, beside(cache1, 1), across, beside(across, 1)]
+    row1 = [cache1, beside1, across, beside(across, 1)]
 
     slot = jnp.arange(2 * ROW * TILE, dtype=jnp.int32)
     k, m, offset = slot // (ROW * TILE), slot // TILE % ROW, slot % TILE
     seen = jnp.where(k == 0, (r ^ m) <= r, k <= z)
-    query = jnp.arange(queries.shape[0], dtype=jnp.int32)[:, None]
+    query = jnp.arange(shape[0], dtype=jnp.int32)[:, None]
     seen = seen & ((k > 0) | (m > 0) | (offset <= query))
     bias = jnp.where(seen, 0.0, MASKED).astype(jnp.float32)
 
-    state = attend(queries, sel, 0, [*row0, *row1], bias=bias)
+    *row1, cache2 = lax.optimization_barrier((*row1, cache2))
     across, beside2 = beside(cache2, 2), beside(cache2, 1)
+    state = attend(queries, shape[1], sel, [*row0, *row1], bias=bias)
     across, *state = lax.optimization_barrier((across, *state))
     row2 = [cache2, beside2, across, beside(across, 1)]
-    out = attend(queries, sel, 2 * ROW, row2, far=far, state=state)
-    return out.reshape(*queries.shape[:2], LAT)
+    out = attend(queries, shape[1], sel, [*row2, far], state=state)
+    return out.reshape(*shape[:2], LAT)
 
 
 def solution(mesh):

time: 50.9 us -> 46.2 us (0.908)
  local copies, waits for them, and re-layouts: 4.41 us -> 0 us
  waiting for transfers between devices: 10.6 us -> 6.62 us
  Pallas kernels: 19.1 us -> 21.7 us
  starting transfers between devices: 14.5 us -> 15.7 us
    unnamed x8 -> x0, local copies, waits for them, and re-layouts: 4.41 us -> none
    ppermute x3, waiting for transfers between devices: 4.05 us -> 0.39 us  [further(): return lax.ppermute(array, 'ctx', [(i, i + ROW * rows) for i in sources])]
    pallas_call x2 -> x3, Pallas kernels: 18.3 us -> 20.9 us  [the longest x2 18.3 us: attend(): pl.pallas_call(functools.partial(attend_kernel, heads, rows, first), grid...]
    ppermute x9, starting transfers between devices: 6.86 us -> 8.09 us  [beside(): return lax.ppermute(array, 'ctx', [(i, i ^ m) for i in range(size)])]
  transfers between devices with their start and end apart: 13 -> 13, of which waited for: 3 -> 3; matrix products, arithmetic and copies ran while one was open for 3% -> 4% of each run, Pallas kernels for 19% -> 26%
where the time goes in v3:
time: 46.2 us; the launch traced here: 46 us
  Pallas kernels  21.7 us (47%)
  starting transfers between devices  15.7 us (34%)
  waiting for transfers between devices  6.62 us (14%)
  other arithmetic  1.77 us (4%)
    pallas_call x2, Pallas kernels, attend(): pl.pallas_call(functools.partial(attend_kernel, heads, rows, first), grid...  18.3 us
    ppermute x9, starting transfers between devices, beside(): return lax.ppermute(array, 'ctx', [(i, i ^ m) for i in range(size)])  8.09 us
    ppermute x9, waiting for transfers between devices, beside(): return lax.ppermute(array, 'ctx', [(i, i ^ m) for i in range(size)])  6.23 us
    ppermute x3, starting transfers between devices, further(): return lax.ppermute(array, 'ctx', [(i, i + ROW * rows) for i in sources])  3.86 us
    ppermute x1, starting transfers between devices, shards_rows(): lax.ppermute(tile_lists, 'ctx', [(i + span, i) for i in range(ROW)])  3.78 us
    pallas_call x1, Pallas kernels, stage(): pl.pallas_call(stage_kernel, in_specs=[pl.BlockSpec(memory_space=pltpu.HB...  2.59 us
  transfers between devices with their start and end apart: 13, of which 3 were waited for; matrix products, arithmetic and copies ran while one was open for 4% of the time, Pallas kernels for 26%

profile of v3, /device:TPU:25, one launch (start us, length us, event | category | flops | bytes accessed | tf_op | source)
XLA Modules:
  0.0 46.0 jit_solution(5176504784136414626)
XLA Ops:
  0.0 1.2 %collective-permute-start.4 = (bf16[576,256]{1,0:T(8,128)(2,1)}, bf16[576,256]{1,0:T(8,128)(2,1)S(1)}, u32[]{:S(2)}, u32[]{:S(2)}) collective-permute-start(bf16[576,256]{1,0:T(8,128)(2,1)} %bitcast.16), channel_id=1, source_target_pairs={{0,2},{1,3},{2,0},{3,1},{4,6},{5,7},{6,4},{7,5},{8,10},{9,11},{10,... | collective-permute-start | bytes 884744 | tf_op jit(solution)/shard_map/ppermute | solution.py:284
  1.2 1.3 %collective-permute-start = (bf16[576,256]{1,0:T(8,128)(2,1)}, bf16[576,256]{1,0:T(8,128)(2,1)S(1)}, u32[]{:S(2)}, u32[]{:S(2)}) collective-permute-start(bf16[576,256]{1,0:T(8,128)(2,1)} %bitcast.17), channel_id=1, source_target_pairs={{0,4},{1,5},{2,6},{3,7},{4,8},{5,9},{6,10},{7,11},{8,12},{9,13},{1... | collective-permute-start | bytes 884744 | tf_op jit(solution)/shard_map/ppermute | solution.py:287
  2.5 3.8 %collective-permute-start.3 = (s32[1,32]{1,0:T(1,128)}, s32[1,32]{1,0:T(1,128)S(1)}, u32[]{:S(2)}, u32[]{:S(2)}) collective-permute-start(s32[1,32]{1,0:T(1,128)} %param.5), channel_id=1, source_target_pairs={{12,0},{13,1},{14,2},{15,3},{28,16},{29,17},{30,18},{31,19}} | collective-permute-start | bytes 392 | tf_op jit(solution)/shard_map/ppermute | solution.py:297
  6.3 0.7 %compare_bitcast_fusion.1 = pred[32]{0:T(512)(128)(4,1)S(1)} fusion(s32[1,32]{1,0:T(1,128)} %param.5), kind=kLoop, calls=%fused_computation.37 | loop fusion | flops 32 | bytes 160 | tf_op jit(solution)/shard_map/and | solution.py:290
  7.0 0.7 %fusion.21 = (s32[32]{0:T(128)S(1)}, s32[32]{0:T(128)S(1)}) fusion(s32[1,32]{1,0:T(1,128)} %param.5), kind=kLoop, calls=%fused_computation.54 | loop fusion | flops 608 | bytes 384 | tf_op jit(solution)/shard_map/eq | solution.py:290
  7.7 0.2 select_reduce_fusion.sel_ref
  7.9 2.6 %stage.1 = (bf16[4096,576]{1,0:T(8,128)(2,1)S(1)}, bf16[576,256]{1,0:T(8,128)(2,1)S(1)}) custom-call(bf16[4096,576]{1,0:T(8,128)(2,1)} %bitcast.15, bf16[576,256]{1,0:T(8,128)(2,1)} %bitcast.18), custom_call_target="tpu_custom_call" | custom-call | bytes 10027008 | tf_op jit(solution)/shard_map/stage/pallas_call | solution.py:145
  10.5 0.4 collective-permute-done.refs_4_
  10.9 1.9 %collective-permute-start.5 = (bf16[576,256]{1,0:T(8,128)(2,1)S(1)}, bf16[576,256]{1,0:T(8,128)(2,1)S(1)}, u32[]{:S(2)}, u32[]{:S(2)}) collective-permute-start(bf16[576,256]{1,0:T(8,128)(2,1)S(1)} %get-tuple-element.28.refs_0_), channel_id=1, source_target_pairs={{0,1},{1,0},{2,3},{3,2},{4,5},{5,4},{6,7},{7,6},{8,9},{9,8},{10,11... | collective-permute-start | bytes 884744 | tf_op jit(solution)/shard_map/ppermute | solution.py:284
  12.8 0.0 collective-permute-start.6
  12.8 0.2 collective-permute-start.2
  13.0 0.2 select_reduce_fusion.1.sel_ref
  13.2 1.3 %collective-permute-start.8 = (bf16[576,256]{1,0:T(8,128)(2,1)S(1)}, bf16[576,256]{1,0:T(8,128)(2,1)S(1)}, u32[]{:S(2)}, u32[]{:S(2)}) collective-permute-start(bf16[576,256]{1,0:T(8,128)(2,1)S(1)} %collective-permute-done.refs_4_), channel_id=1, source_target_pairs={{4,8},{5,9},{6,10},{7,11},{8,12},{9,13},{10,14},{11,15},{20,24},{2... | collective-permute-start | bytes 884744 | tf_op jit(solution)/shard_map/ppermute | solution.py:287
  14.5 0.9 %collective-permute-start.1 = (bf16[576,256]{1,0:T(8,128)(2,1)S(1)}, bf16[576,256]{1,0:T(8,128)(2,1)S(1)}, u32[]{:S(2)}, u32[]{:S(2)}) collective-permute-start(bf16[576,256]{1,0:T(8,128)(2,1)S(1)} %collective-permute-done.refs_4_), channel_id=1, source_target_pairs={{0,1},{1,0},{2,3},{3,2},{4,5},{5,4},{6,7},{7,6},{8,9},{9,8},{10,11... | collective-permute-start | bytes 884744 | tf_op jit(solution)/shard_map/ppermute | solution.py:284
  15.3 0.8 %pick_tiles.1 = bf16[576,256]{1,0:T(8,128)(2,1)S(1)} custom-call(s32[4]{0:T(128)S(1)} %select_reduce_fusion.1.sel_ref, bf16[576,256]{1,0:T(8,128)(2,1)S(1)} %get-tuple-element.28.refs_0_, bf16[576,256]{1,0:T(8,128)(2,1)S(1)} %collective-permute-done.5.refs_1_, bf16[576,256]{1,0:T(8,128)(2,1)S(1)} %collective-permute-done.4.refs_2_, ...), custom_call_target="tpu_custom_call" | custom-call | bytes 589824 | tf_op jit(solution)/shard_map/pick_tiles/pallas_call | solution.py:108
  16.2 4.7 %collective-permute-done.2.refs_6_ = bf16[576,256]{1,0:T(8,128)(2,1)S(1)} collective-permute-done((bf16[576,256]{1,0:T(8,128)(2,1)S(1)}, bf16[576,256]{1,0:T(8,128)(2,1)S(1)}, u32[]{:S(2)}, u32[]{:S(2)}) %collective-permute-start.2) | collective-permute-done | bytes 294944 | tf_op jit(solution)/shard_map/ppermute | solution.py:284
  20.8 1.4 %collective-permute-start.7 = (bf16[576,256]{1,0:T(8,128)(2,1)S(1)}, bf16[576,256]{1,0:T(8,128)(2,1)S(1)}, u32[]{:S(2)}, u32[]{:S(2)}) collective-permute-start(bf16[576,256]{1,0:T(8,128)(2,1)S(1)} %collective-permute-done.2.refs_6_), channel_id=1, source_target_pairs={{0,1},{1,0},{2,3},{3,2},{4,5},{5,4},{6,7},{7,6},{8,9},{9,8},{10,11... | collective-permute-start | bytes 884744 | tf_op jit(solution)/shard_map/ppermute | solution.py:284
  22.2 1.3 %collective-permute-start.12 = (bf16[576,256]{1,0:T(8,128)(2,1)S(1)}, bf16[576,256]{1,0:T(8,128)(2,1)S(1)}, u32[]{:S(2)}, u32[]{:S(2)}) collective-permute-start(bf16[576,256]{1,0:T(8,128)(2,1)S(1)} %pick_tiles.1), channel_id=1, source_target_pairs={{0,12},{1,13},{2,14},{3,15},{16,28},{17,29},{18,30},{19,31}} | collective-permute-start | bytes 884744 | tf_op jit(solution)/shard_map/ppermute | solution.py:287
  23.6 0.5 %collective-permute-start.10 = (bf16[576,256]{1,0:T(8,128)(2,1)S(1)}, bf16[576,256]{1,0:T(8,128)(2,1)S(1)}, u32[]{:S(2)}, u32[]{:S(2)}) collective-permute-start(bf16[576,256]{1,0:T(8,128)(2,1)S(1)} %collective-permute-done.8.refs_0_), channel_id=1, source_target_pairs={{0,2},{1,3},{2,0},{3,1},{4,6},{5,7},{6,4},{7,5},{8,10},{9,11},{10,... | collective-permute-start | bytes 884744 | tf_op jit(solution)/shard_map/ppermute | solution.py:284
  24.1 2.0 %collective-permute-start.9 = (bf16[576,256]{1,0:T(8,128)(2,1)S(1)}, bf16[576,256]{1,0:T(8,128)(2,1)S(1)}, u32[]{:S(2)}, u32[]{:S(2)}) collective-permute-start(bf16[576,256]{1,0:T(8,128)(2,1)S(1)} %collective-permute-done.8.refs_0_), channel_id=1, source_target_pairs={{0,1},{1,0},{2,3},{3,2},{4,5},{5,4},{6,7},{7,6},{8,9},{9,8},{10,11... | collective-permute-start | bytes 884744 | tf_op jit(solution)/shard_map/ppermute | solution.py:284
  26.0 8.6 %attend_near.1 = (bf16[4096,512]{1,0:T(8,128)(2,1)S(1)}, f32[4096,128]{1,0:T(8,128)S(1)}, f32[4096,128]{1,0:T(8,128)S(1)}) custom-call(s32[12]{0:T(128)S(1)} %select_reduce_fusion.sel_ref, bf16[576,256]{1,0:T(8,128)(2,1)S(1)} %get-tuple-element.28.refs_0_, bf16[576,256]{1,0:T(8,128)(2,1)S(1)} %collective-permute-done.5.refs_1_, ...), custom_call_target="tpu_custom_call" | custom-call | flops 4563402752 | bytes 8912896 | tf_op jit(solution)/shard_map/attend_near/pallas_call | solution.py:261
  34.6 0.1 collective-permute-start.11
  34.7 1.5 %collective-permute-done.11.refs_3_ = bf16[576,256]{1,0:T(8,128)(2,1)S(1)} collective-permute-done((bf16[576,256]{1,0:T(8,128)(2,1)S(1)}, bf16[576,256]{1,0:T(8,128)(2,1)S(1)}, u32[]{:S(2)}, u32[]{:S(2)}) %collective-permute-start.11) | collective-permute-done | bytes 294944 | tf_op jit(solution)/shard_map/ppermute | solution.py:284
  36.3 9.7 %attend_rest.1 = bf16[4096,512]{1,0:T(8,128)(2,1)} custom-call(s32[12]{0:T(128)S(1)} %select_reduce_fusion.sel_ref, bf16[576,256]{1,0:T(8,128)(2,1)S(1)} %collective-permute-done.8.refs_0_, bf16[576,256]{1,0:T(8,128)(2,1)S(1)} %collective-permute-done.9.refs_1_, bf16[576,256]{1,0:T(8,128)(2,1)S(1)} %collective-permute-done.10.refs_2_, ...), custom_call_target="tpu_custom_call" | custom-call | flops 4563402752 | bytes 8912896 | tf_op jit(solution)/shard_map/attend_rest/pallas_call | solution.py:261
  (17 shorter events, 0.1 us)
Async XLA Ops:
  0.0 10.9 %collective-permute-start.4 = (bf16[576,256]{1,0:T(8,128)(2,1)}, bf16[576,256]{1,0:T(8,128)(2,1)S(1)}, u32[]{:S(2)}, u32[]{:S(2)}) collective-permute-start(bf16[576,256]{1,0:T(8,128)(2,1)} %bitcast.16), channel_id=1, source_target_pairs={{0,2},{1,3},{2,0},{3,1},{4,6},{5,7},{6,4},{7,5},{8,10},{9,11},{10,... | collective-permute-start | bytes 884744 | tf_op jit(solution)/shard_map/ppermute | solution.py:284
  1.2 9.7 %collective-permute-start = (bf16[576,256]{1,0:T(8,128)(2,1)}, bf16[576,256]{1,0:T(8,128)(2,1)S(1)}, u32[]{:S(2)}, u32[]{:S(2)}) collective-permute-start(bf16[576,256]{1,0:T(8,128)(2,1)} %bitcast.17), channel_id=1, source_target_pairs={{0,4},{1,5},{2,6},{3,7},{4,8},{5,9},{6,10},{7,11},{8,12},{9,13},{1... | collective-permute-start | bytes 884744 | tf_op jit(solution)/shard_map/ppermute | solution.py:287
  2.5 8.0 %collective-permute-start.3 = (s32[1,32]{1,0:T(1,128)}, s32[1,32]{1,0:T(1,128)S(1)}, u32[]{:S(2)}, u32[]{:S(2)}) collective-permute-start(s32[1,32]{1,0:T(1,128)} %param.5), channel_id=1, source_target_pairs={{12,0},{13,1},{14,2},{15,3},{28,16},{29,17},{30,18},{31,19}} | collective-permute-start | bytes 392 | tf_op jit(solution)/shard_map/ppermute | solution.py:297
  10.9 4.4 %collective-permute-start.5 = (bf16[576,256]{1,0:T(8,128)(2,1)S(1)}, bf16[576,256]{1,0:T(8,128)(2,1)S(1)}, u32[]{:S(2)}, u32[]{:S(2)}) collective-permute-start(bf16[576,256]{1,0:T(8,128)(2,1)S(1)} %get-tuple-element.28.refs_0_), channel_id=1, source_target_pairs={{0,1},{1,0},{2,3},{3,2},{4,5},{5,4},{6,7},{7,6},{8,9},{9,8},{10,11... | collective-permute-start | bytes 884744 | tf_op jit(solution)/shard_map/ppermute | solution.py:284
  12.8 2.6 %collective-permute-start.6 = (bf16[576,256]{1,0:T(8,128)(2,1)S(1)}, bf16[576,256]{1,0:T(8,128)(2,1)S(1)}, u32[]{:S(2)}, u32[]{:S(2)}) collective-permute-start(bf16[576,256]{1,0:T(8,128)(2,1)S(1)} %collective-permute-done.4.refs_2_), channel_id=1, source_target_pairs={{0,1},{1,0},{2,3},{3,2},{4,5},{5,4},{6,7},{7,6},{8,9},{9,8},{10,11... | collective-permute-start | bytes 884744 | tf_op jit(solution)/shard_map/ppermute | solution.py:284
  12.8 8.1 %collective-permute-start.2 = (bf16[576,256]{1,0:T(8,128)(2,1)S(1)}, bf16[576,256]{1,0:T(8,128)(2,1)S(1)}, u32[]{:S(2)}, u32[]{:S(2)}) collective-permute-start(bf16[576,256]{1,0:T(8,128)(2,1)S(1)} %collective-permute-done.refs_4_), channel_id=1, source_target_pairs={{0,2},{1,3},{2,0},{3,1},{4,6},{5,7},{6,4},{7,5},{8,10},{9,11},{10,... | collective-permute-start | bytes 884744 | tf_op jit(solution)/shard_map/ppermute | solution.py:284
  13.2 10.4 %collective-permute-start.8 = (bf16[576,256]{1,0:T(8,128)(2,1)S(1)}, bf16[576,256]{1,0:T(8,128)(2,1)S(1)}, u32[]{:S(2)}, u32[]{:S(2)}) collective-permute-start(bf16[576,256]{1,0:T(8,128)(2,1)S(1)} %collective-permute-done.refs_4_), channel_id=1, source_target_pairs={{4,8},{5,9},{6,10},{7,11},{8,12},{9,13},{10,14},{11,15},{20,24},{2... | collective-permute-start | bytes 884744 | tf_op jit(solution)/shard_map/ppermute | solution.py:287
  14.5 9.1 %collective-permute-start.1 = (bf16[576,256]{1,0:T(8,128)(2,1)S(1)}, bf16[576,256]{1,0:T(8,128)(2,1)S(1)}, u32[]{:S(2)}, u32[]{:S(2)}) collective-permute-start(bf16[576,256]{1,0:T(8,128)(2,1)S(1)} %collective-permute-done.refs_4_), channel_id=1, source_target_pairs={{0,1},{1,0},{2,3},{3,2},{4,5},{5,4},{6,7},{7,6},{8,9},{9,8},{10,11... | collective-permute-start | bytes 884744 | tf_op jit(solution)/shard_map/ppermute | solution.py:284
  20.8 2.7 %collective-permute-start.7 = (bf16[576,256]{1,0:T(8,128)(2,1)S(1)}, bf16[576,256]{1,0:T(8,128)(2,1)S(1)}, u32[]{:S(2)}, u32[]{:S(2)}) collective-permute-start(bf16[576,256]{1,0:T(8,128)(2,1)S(1)} %collective-permute-done.2.refs_6_), channel_id=1, source_target_pairs={{0,1},{1,0},{2,3},{3,2},{4,5},{5,4},{6,7},{7,6},{8,9},{9,8},{10,11... | collective-permute-start | bytes 884744 | tf_op jit(solution)/shard_map/ppermute | solution.py:284
  22.2 12.5 %collective-permute-start.12 = (bf16[576,256]{1,0:T(8,128)(2,1)S(1)}, bf16[576,256]{1,0:T(8,128)(2,1)S(1)}, u32[]{:S(2)}, u32[]{:S(2)}) collective-permute-start(bf16[576,256]{1,0:T(8,128)(2,1)S(1)} %pick_tiles.1), channel_id=1, source_target_pairs={{0,12},{1,13},{2,14},{3,15},{16,28},{17,29},{18,30},{19,31}} | collective-permute-start | bytes 884744 | tf_op jit(solution)/shard_map/ppermute | solution.py:287
  23.6 11.0 %collective-permute-start.10 = (bf16[576,256]{1,0:T(8,128)(2,1)S(1)}, bf16[576,256]{1,0:T(8,128)(2,1)S(1)}, u32[]{:S(2)}, u32[]{:S(2)}) collective-permute-start(bf16[576,256]{1,0:T(8,128)(2,1)S(1)} %collective-permute-done.8.refs_0_), channel_id=1, source_target_pairs={{0,2},{1,3},{2,0},{3,1},{4,6},{5,7},{6,4},{7,5},{8,10},{9,11},{10,... | collective-permute-start | bytes 884744 | tf_op jit(solution)/shard_map/ppermute | solution.py:284
  24.1 10.6 %collective-permute-start.9 = (bf16[576,256]{1,0:T(8,128)(2,1)S(1)}, bf16[576,256]{1,0:T(8,128)(2,1)S(1)}, u32[]{:S(2)}, u32[]{:S(2)}) collective-permute-start(bf16[576,256]{1,0:T(8,128)(2,1)S(1)} %collective-permute-done.8.refs_0_), channel_id=1, source_target_pairs={{0,1},{1,0},{2,3},{3,2},{4,5},{5,4},{6,7},{7,6},{8,9},{9,8},{10,11... | collective-permute-start | bytes 884744 | tf_op jit(solution)/shard_map/ppermute | solution.py:284
  34.6 1.6 %collective-permute-start.11 = (bf16[576,256]{1,0:T(8,128)(2,1)S(1)}, bf16[576,256]{1,0:T(8,128)(2,1)S(1)}, u32[]{:S(2)}, u32[]{:S(2)}) collective-permute-start(bf16[576,256]{1,0:T(8,128)(2,1)S(1)} %collective-permute-done.10.refs_2_), channel_id=1, source_target_pairs={{0,1},{1,0},{2,3},{3,2},{4,5},{5,4},{6,7},{7,6},{8,9},{9,8},{10,11... | collective-permute-start | bytes 884744 | tf_op jit(solution)/shard_map/ppermute | solution.py:284

commit v4 on v0

--- a/solution.py
+++ b/solution.py
@@ -1,6 +1,11 @@
+import functools
+import math
+
 import jax
 import jax.numpy as jnp
 from jax import lax
+from jax.experimental import pallas as pl
+from jax.experimental.pallas import tpu as pltpu
 from jax.sharding import PartitionSpec as P
 
 LAT = 512
@@ -8,9 +13,15 @@
 TOPK = 32
 CAP = 1
 TILES_DEV = 4
+ROW = 4
+STAGES = 4
+BLOCKS = 4
+DEPTH = 4
 
 
 softmax_scale = 192.0 ** (-0.5)
+LOG2E_SCALE = softmax_scale * math.log2(math.e)
+MASKED = -1e30
 
 
 def slot_ranks(holders):
@@ -28,7 +39,7 @@
     return jnp.sum(jnp.where(hits, local_tile[..., None] + 1, 0), axis=-2) - 1
 
 
-def shards(queries, latent_cache, tile_lists):
+def shards_general(queries, latent_cache, tile_lists):
     width = latent_cache.shape[1]
     listing = tile_lists[0]
     me = lax.axis_index("ctx")
@@ -59,7 +70,7 @@
         jnp.einsum("qhc,kc->qhk", queries, keys, preferred_element_type=jnp.float32) * softmax_scale
     )
     allowed = (key_ok[None, :] & (key_pos[None, :] <= query_pos[:, None]))[:, None, :]
-    scores = jnp.where(allowed, scores, -1e30)
+    scores = jnp.where(allowed, scores, MASKED)
     top = jnp.max(scores, axis=-1, keepdims=True)
     expo = jnp.where(allowed, jnp.exp(scores - top), 0.0)
     total = jnp.sum(expo, axis=-1, keepdims=True)
@@ -68,12 +79,265 @@
     return (summed / total).astype(jnp.bfloat16)
 
 
+def side_by_side(sel_ref, entry, caches, out_ref):
+    for at in range(0, len(caches), 2):
+        pair = []
+        for upper in (False, True):
+            tile = sel_ref[entry + at + upper]
+            start = pl.multiple_of(tile // 2 * 2 * TILE, 2 * TILE)
+            block = caches[at + upper][:, pl.ds(start, 2 * TILE)]
+            swapped = jnp.concatenate([block[:, TILE:], block[:, :TILE]], axis=1)
+            pair.append(jnp.where((tile % 2 == 1) != upper, swapped, block))
+        out_ref[:, at * TILE : (at + 2) * TILE] = jnp.concatenate(
+            [pair[0][:, :TILE], pair[1][:, TILE:]], axis=1
+        )
+
+
+def pick_kernel(sel_ref, own_ref, *refs):
+    *caches, sent_ref, kept_ref = refs
+    side_by_side(sel_ref, 0, caches, sent_ref)
+    side_by_side(own_ref, 0, caches, kept_ref)
+
+
+def pick_tiles(sel, own, caches):
+    width = caches[0].shape[0]
+    columns = len(caches) * TILE
+    vmem = pl.BlockSpec(memory_space=pltpu.VMEM)
+    return pl.pallas_call(
+        pick_kernel,
+        in_specs=[pl.BlockSpec(memory_space=pltpu.SMEM)] * 2 + [vmem] * len(caches),
+        out_specs=[vmem] * 2,
+        out_shape=[jax.ShapeDtypeStruct((width, columns), caches[0].dtype)] * 2,
+        compiler_params=pltpu.CompilerParams(vmem_limit_bytes=6 << 20),
+        cost_estimate=pl.CostEstimate(
+            flops=0, transcendentals=0, bytes_accessed=8 * columns * width
+        ),
+        name="pick_tiles",
+    )(sel, own, *caches)
+
+
+def pieces(array):
+    return [array[:, at : at + 2 * TILE] for at in range(0, array.shape[1], 2 * TILE)]
+
+
+def score(queries, keys):
+    return jnp.dot(queries, keys, preferred_element_type=jnp.float32)
+
+
+def weigh(scores, top):
+    scaled_top = top * LOG2E_SCALE
+    expo = [jnp.exp2(piece * LOG2E_SCALE - scaled_top) for piece in scores]
+    total = jnp.sum(functools.reduce(jnp.add, expo), axis=1, keepdims=True)
+    expo = jnp.concatenate([piece.astype(jnp.bfloat16) for piece in expo], axis=1)
+    return expo, jnp.broadcast_to(total, top.shape)
+
+
+def tops(scores):
+    top = jnp.max(functools.reduce(jnp.maximum, scores), axis=1, keepdims=True)
+    return jnp.broadcast_to(top, (top.shape[0], 2 * TILE))
+
+
+def mix(expo, keys_ref):
+    summed = lax.dot_general(
+        expo, keys_ref[:LAT, :], (((1,), (1,)), ((), ())), preferred_element_type=jnp.float32
+    )
+    return pieces(summed)
+
+
+def near_kernel(heads, sel_ref, *refs):
+    caches, refs = refs[:ROW], refs[ROW:]
+    own_ref, bias_ref, q_ref, mean_ref, top_ref, total_ref, keys_ref = refs
+    half = ROW * TILE
+    side_by_side(sel_ref, ROW, caches, keys_ref)
+    keys_ref[:, half:] = own_ref[...]
+    hidden = jnp.where(lax.axis_index("ctx") >= ROW, 0.0, MASKED)
+    rows = q_ref.shape[0] // BLOCKS
+    for at in range(BLOCKS):
+        block = pl.ds(at * rows, rows)
+        own = score(q_ref[block, :], own_ref[...])
+        bias = bias_ref[pl.ds(at * (rows // heads), rows // heads), :]
+        own = own.reshape(rows // heads, heads, -1) + bias[:, None, :]
+        scores = [piece + hidden for piece in pieces(score(q_ref[block, :], keys_ref[:, :half]))]
+        scores += pieces(own.reshape(rows, -1))
+        top = tops(scores)
+        expo, total = weigh(scores, top)
+        scale = 1.0 / total
+        for lane, piece in enumerate(mix(expo, keys_ref)):
+            lanes = slice(lane * 2 * TILE, (lane + 1) * 2 * TILE)
+            mean_ref[block, lanes] = (piece * scale).astype(mean_ref.dtype)
+        top_ref[block, :] = top
+        total_ref[block, :] = total
+
+
+def rest_kernel(sel_ref, *refs):
+    caches, refs = refs[:ROW], refs[ROW:]
+    far_ref, q_ref, mean_ref, top_ref, total_ref, out_hbm, keys_ref, out_ref, sems = refs
+    z = lax.axis_index("ctx") // ROW
+    rows = q_ref.shape[0] // BLOCKS
+
+    def put(at):
+        block = pl.ds(at * rows, rows)
+        return pltpu.make_async_copy(out_ref.at[block, :], out_hbm.at[block, :], sems.at[at])
+
+    @pl.when(z >= DEPTH - 2)
+    def _():
+        half = ROW * TILE
+        side_by_side(sel_ref, 2 * ROW, caches, keys_ref)
+        keys_ref[:, half:] = far_ref[...]
+        hidden = jnp.where(z >= DEPTH - 1, 0.0, MASKED)
+        for at in range(BLOCKS):
+            block = pl.ds(at * rows, rows)
+            far = [piece + hidden for piece in pieces(score(q_ref[block, :], far_ref[...]))]
+            scores = pieces(score(q_ref[block, :], keys_ref[:, :half])) + far
+            top_before = top_ref[block, :]
+            top = jnp.maximum(tops(scores), top_before)
+            expo, total = weigh(scores, top)
+            before = total_ref[block, :] * jnp.exp2((top_before - top) * LOG2E_SCALE)
+            scale = 1.0 / (total + before)
+            share = before * scale
+            for lane, piece in enumerate(mix(expo, keys_ref)):
+                lanes = slice(lane * 2 * TILE, (lane + 1) * 2 * TILE)
+                mean = mean_ref[block, lanes].astype(jnp.float32)
+                out_ref[block, lanes] = (piece * scale + mean * share).astype(out_ref.dtype)
+            put(at).start()
+
+    @pl.when(z < DEPTH - 2)
+    def _():
+        for at in range(BLOCKS):
+            block = pl.ds(at * rows, rows)
+            out_ref[block, :] = mean_ref[block, :]
+            put(at).start()
+
+    for at in range(BLOCKS):
+        put(at).wait()
+
+
+def attend(kernel, queries, sel, tiles, state=()):
+    count, width = queries.shape
+    keys = 2 * ROW * TILE
+    vmem = pl.BlockSpec(memory_space=pltpu.VMEM)
+    near = not state
+    scratch = [pltpu.VMEM((width, keys), queries.dtype)]
+    if near:
+        stats = pltpu.VMEM((count, 2 * TILE), jnp.float32)
+        out_shape = [pltpu.VMEM((count, LAT), queries.dtype), stats, stats]
+    else:
+        out_shape = jax.ShapeDtypeStruct((count, LAT), queries.dtype)
+        scratch += [pltpu.VMEM((count, LAT), queries.dtype), pltpu.SemaphoreType.DMA((BLOCKS,))]
+    return pl.pallas_call(
+        kernel,
+        in_specs=[pl.BlockSpec(memory_space=pltpu.SMEM)] + [vmem] * (len(tiles) + 1 + len(state)),
+        out_specs=[vmem] * 3 if near else pl.BlockSpec(memory_space=pl.ANY),
+        out_shape=out_shape,
+        scratch_shapes=scratch,
+        compiler_params=pltpu.CompilerParams(vmem_limit_bytes=24 << 20),
+        cost_estimate=pl.CostEstimate(
+            flops=2 * count * keys * (width + LAT),
+            transcendentals=count * keys,
+            bytes_accessed=2 * count * (width + LAT),
+        ),
+        name="attend_near" if near else "attend_rest",
+    )(sel, *tiles, queries, *state)
+
+
+def stage_kernel(*refs):
+    *refs, sems = refs
+    half = len(refs) // 2
+    copies = []
+    for source_ref, out_ref in zip(refs[:half], refs[half:]):
+        rows = source_ref.shape[0] // STAGES
+        for at in range(STAGES):
+            block = pl.ds(at * rows, rows)
+            copies.append(
+                pltpu.make_async_copy(
+                    source_ref.at[block, :], out_ref.at[block, :], sems.at[len(copies)]
+                )
+            )
+    for copy in copies:
+        copy.start()
+    for copy in copies:
+        copy.wait()
+
+
+def stage(*arrays):
+    return pl.pallas_call(
+        stage_kernel,
+        in_specs=[pl.BlockSpec(memory_space=pltpu.HBM)] * len(arrays),
+        out_specs=[pl.BlockSpec(memory_space=pltpu.VMEM)] * len(arrays),
+        out_shape=[pltpu.VMEM(array.shape, array.dtype) for array in arrays],
+        scratch_shapes=[pltpu.SemaphoreType.DMA((STAGES * len(arrays),))],
+        compiler_params=pltpu.CompilerParams(vmem_limit_bytes=8 << 20),
+        cost_estimate=pl.CostEstimate(
+            flops=0, transcendentals=0, bytes_accessed=4 * sum(array.size for array in arrays)
+        ),
+        name="stage",
+    )(*(pltpu.with_memory_space_constraint(array, pltpu.HBM) for array in arrays))
+
+
+def shards_rows(queries, latent_cache, tile_lists):
+    size = lax.axis_size("ctx")
+    span = size - ROW
+    me = lax.axis_index("ctx")
+    z, r = me // ROW, me % ROW
+
+    def beside(array, m):
+        return lax.ppermute(array, "ctx", [(i, i ^ m) for i in range(size)])
+
+    def further(array, rows, sources):
+        return lax.ppermute(array, "ctx", [(i, i + ROW * rows) for i in sources])
+
+    def named_tiles(listing, holders):
+        hit = (listing >= 0) & (listing // TILES_DEV == holders[:, None])
+        return jnp.sum(jnp.where(hit, listing % TILES_DEV, 0), axis=1)
+
+    shape = queries.shape
+    cache = latent_cache.T
+    cache1 = further(cache, 1, range(span))
+    across = beside(cache, 2)
+    far_list = lax.ppermute(tile_lists, "ctx", [(i + span, i) for i in range(ROW)])
+    (cache,) = stage(cache)
+    cache, across = lax.optimization_barrier((cache, across))
+    row0 = [cache, beside(cache, 1), across, beside(across, 1)]
+
+    slot = jnp.arange((DEPTH - 1) * ROW, dtype=jnp.int32)
+    sel = named_tiles(tile_lists, ROW * (z - slot // ROW) + (r ^ slot % ROW))
+
+    far_sel = named_tiles(far_list, me ^ jnp.arange(ROW, dtype=jnp.int32))
+    far, keys0 = pick_tiles(far_sel, sel, row0)
+    cache2 = further(cache1, 1, range(ROW, span))
+    across = beside(cache1, 2)
+    queries = queries.reshape(-1, shape[2])
+    far, queries = lax.optimization_barrier((far, queries))
+    (queries,) = stage(queries)
+    cache1, queries = lax.optimization_barrier((cache1, queries))
+    beside1 = beside(cache1, 1)
+    across, far, queries = lax.optimization_barrier((across, far, queries))
+    far = further(far, DEPTH - 1, range(ROW))
+    row1 = [cache1, beside1, across, beside(across, 1)]
+
+    slot = jnp.arange(ROW * TILE, dtype=jnp.int32)
+    m, offset = slot // TILE, slot % TILE
+    query = jnp.arange(shape[0], dtype=jnp.int32)[:, None]
+    seen = ((r ^ m) <= r) & ((m > 0) | (offset <= query))
+    bias = jnp.where(seen, 0.0, MASKED).astype(jnp.float32)
+
+    *row1, cache2 = lax.optimization_barrier((*row1, cache2))
+    across, beside2 = beside(cache2, 2), beside(cache2, 1)
+    state = attend(functools.partial(near_kernel, shape[1]), queries, sel, [*row1, keys0, bias])
+    across, *state = lax.optimization_barrier((across, *state))
+    row2 = [cache2, beside2, across, beside(across, 1)]
+    out = attend(rest_kernel, queries, sel, [*row2, far], state)
+    return out.reshape(*shape[:2], LAT)
+
+
 def solution(mesh):
     placed = (
         P(("groups", "ctx"), None, None),
         P(("groups", "ctx"), None),
         P(("groups", "ctx"), None),
     )
+    size = mesh.shape["ctx"]
+    shards = shards_rows if size == ROW * DEPTH else shards_general
     return jax.shard_map(
         shards,
         mesh=mesh,

time: 140 us -> 43.5 us (0.31); the launches traced: 137 us -> 43.3 us
  other arithmetic: 36.2 us -> 1.76 us
  matrix products: 33.4 us -> 0 us
  Pallas kernels: 0 us -> 21.8 us
  waiting for transfers between devices: 24.1 us -> 3.49 us
  local copies, waits for them, and re-layouts: 17.6 us -> 0 us
  blocking collectives: 17.3 us -> 0 us
  starting transfers between devices: 8.47 us -> 15.8 us
    dot_general x2 -> x0, matrix products: 33.4 us -> none  [the longest x1 19.6 us: shards(): jnp.einsum('qhc,kc->qhk', queries, keys, preferred_element_type=jnp.float32)]
    sub x1 -> x0, other arithmetic: 32.5 us -> none  [shards(): expo = jnp.where(allowed, jnp.exp(scores - top), 0.0)]
    all_to_all x1 -> x0, waiting for transfers between devices: 24.1 us -> none  [shards(): lax.all_to_all(outgoing, 'ctx', split_axis=0, concat_axis=0, tiled=True)]
    pallas_call x0 -> x5, Pallas kernels: none -> 21.8 us  [the longest x2 17.3 us: attend(): pl.pallas_call(kernel, in_specs=[pl.BlockSpec(memory_space=pltpu.SMEM)] +...]
    all_gather x1 -> x0, blocking collectives: 17.3 us -> none  [shards(): lists_all = lax.all_gather(tile_lists, 'ctx', axis=0, tiled=True)]
    ppermute x0 -> x13, starting transfers between devices: none -> 15.8 us  [the longest x9 8.19 us: beside(): return lax.ppermute(array, 'ctx', [(i, i ^ m) for i in range(size)])]
    gather x3 -> x0, local copies, waits for them, and re-layouts: 9.38 us -> none  [the longest x2 8.04 us: shards(): keys = jnp.take(incoming, position, axis=0)]
    all_to_all x1 -> x0, starting transfers between devices: 8.47 us -> none  [shards(): lax.all_to_all(outgoing, 'ctx', split_axis=0, concat_axis=0, tiled=True)]
  transfers between devices with their start and end apart: 1 -> 13, of which waited for: 1 -> 5; matrix products, arithmetic and copies ran while one was open for 1% -> 4% of each run, Pallas kernels for 0% -> 28%
where the time goes in v4:
time: 43.5 us; the launch traced here: 43.3 us
  Pallas kernels  21.8 us (50%)
  starting transfers between devices  15.8 us (36%)
  waiting for transfers between devices  3.49 us (8%)
  other arithmetic  1.76 us (4%)
    pallas_call x2, Pallas kernels, attend(): pl.pallas_call(kernel, in_specs=[pl.BlockSpec(memory_space=pltpu.SMEM)] +...  17.3 us
    ppermute x9, starting transfers between devices, beside(): return lax.ppermute(array, 'ctx', [(i, i ^ m) for i in range(size)])  8.19 us
    ppermute x3, starting transfers between devices, further(): return lax.ppermute(array, 'ctx', [(i, i + ROW * rows) for i in sources])  3.86 us
    ppermute x1, starting transfers between devices, shards_rows(): lax.ppermute(tile_lists, 'ctx', [(i + span, i) for i in range(ROW)])  3.78 us
    pallas_call x2, Pallas kernels, stage(): pl.pallas_call(stage_kernel, in_specs=[pl.BlockSpec(memory_space=pltpu.HB...  3.57 us
    ppermute x9, waiting for transfers between devices, beside(): return lax.ppermute(array, 'ctx', [(i, i ^ m) for i in range(size)])  2.75 us
    pallas_call x1, Pallas kernels, pick_tiles(): pl.pallas_call(pick_kernel, in_specs=[pl.BlockSpec(memory_space=pltpu.SME...  1.01 us
  transfers between devices with their start and end apart: 13, of which 5 were waited for; matrix products, arithmetic and copies ran while one was open for 4% of the time, Pallas kernels for 28%

profile of v4, /device:TPU:25, one launch (start us, length us, event | category | flops | bytes accessed | tf_op | source)
XLA Modules:
  0.0 43.3 jit_solution(9143744402742067887)
XLA Ops:
  0.0 1.2 %collective-permute-start.2 = (bf16[576,256]{1,0:T(8,128)(2,1)}, bf16[576,256]{1,0:T(8,128)(2,1)S(1)}, u32[]{:S(2)}, u32[]{:S(2)}) collective-permute-start(bf16[576,256]{1,0:T(8,128)(2,1)} %bitcast.16), channel_id=1, source_target_pairs={{0,2},{1,3},{2,0},{3,1},{4,6},{5,7},{6,4},{7,5},{8,10},{9,11},{10,... | collective-permute-start | bytes 884744 | tf_op jit(solution)/shard_map/ppermute | solution.py:284
  1.2 1.3 %collective-permute-start = (bf16[576,256]{1,0:T(8,128)(2,1)}, bf16[576,256]{1,0:T(8,128)(2,1)S(1)}, u32[]{:S(2)}, u32[]{:S(2)}) collective-permute-start(bf16[576,256]{1,0:T(8,128)(2,1)} %bitcast.17), channel_id=1, source_target_pairs={{0,4},{1,5},{2,6},{3,7},{4,8},{5,9},{6,10},{7,11},{8,12},{9,13},{1... | collective-permute-start | bytes 884744 | tf_op jit(solution)/shard_map/ppermute | solution.py:287
  2.5 3.8 %collective-permute-start.1 = (s32[1,32]{1,0:T(1,128)}, s32[1,32]{1,0:T(1,128)S(1)}, u32[]{:S(2)}, u32[]{:S(2)}) collective-permute-start(s32[1,32]{1,0:T(1,128)} %param.5), channel_id=1, source_target_pairs={{12,0},{13,1},{14,2},{15,3},{28,16},{29,17},{30,18},{31,19}} | collective-permute-start | bytes 392 | tf_op jit(solution)/shard_map/ppermute | solution.py:297
  6.3 0.7 %compare_bitcast_fusion.1 = pred[32]{0:T(512)(128)(4,1)S(1)} fusion(s32[1,32]{1,0:T(1,128)} %param.5), kind=kLoop, calls=%fused_computation.18 | loop fusion | flops 32 | bytes 160 | tf_op jit(solution)/shard_map/and | solution.py:290
  7.0 0.7 %fusion.11 = (s32[32]{0:T(128)S(1)}, s32[32]{0:T(128)S(1)}) fusion(s32[1,32]{1,0:T(1,128)} %param.5), kind=kLoop, calls=%fused_computation.39 | loop fusion | flops 608 | bytes 384 | tf_op jit(solution)/shard_map/eq | solution.py:290
  7.7 0.2 select_reduce_fusion.own_ref.sel_ref
  7.9 1.0 %stage.2.refs_0_ = bf16[576,256]{1,0:T(8,128)(2,1)S(1)} custom-call(bf16[576,256]{1,0:T(8,128)(2,1)} %bitcast.18), custom_call_target="tpu_custom_call" | custom-call | bytes 589824 | tf_op jit(solution)/shard_map/stage/pallas_call | solution.py:263
  8.9 1.6 %collective-permute-start.3 = (bf16[576,256]{1,0:T(8,128)(2,1)S(1)}, bf16[576,256]{1,0:T(8,128)(2,1)S(1)}, u32[]{:S(2)}, u32[]{:S(2)}) collective-permute-start(bf16[576,256]{1,0:T(8,128)(2,1)S(1)} %stage.2.refs_0_), channel_id=1, source_target_pairs={{0,1},{1,0},{2,3},{3,2},{4,5},{5,4},{6,7},{7,6},{8,9},{9,8},{10,11... | collective-permute-start | bytes 884744 | tf_op jit(solution)/shard_map/ppermute | solution.py:284
  10.6 0.3 collective-permute-done.refs_0_
  10.9 0.2 collective-permute-start.6
  11.1 0.2 select_reduce_fusion.1.sel_ref
  11.3 1.3 %collective-permute-start.8 = (bf16[576,256]{1,0:T(8,128)(2,1)S(1)}, bf16[576,256]{1,0:T(8,128)(2,1)S(1)}, u32[]{:S(2)}, u32[]{:S(2)}) collective-permute-start(bf16[576,256]{1,0:T(8,128)(2,1)S(1)} %collective-permute-done.refs_0_), channel_id=1, source_target_pairs={{4,8},{5,9},{6,10},{7,11},{8,12},{9,13},{10,14},{11,15},{20,24},{2... | collective-permute-start | bytes 884744 | tf_op jit(solution)/shard_map/ppermute | solution.py:287
  12.6 1.0 %pick_tiles.1 = (bf16[576,256]{1,0:T(8,128)(2,1)S(1)}, bf16[576,256]{1,0:T(8,128)(2,1)S(1)}) custom-call(s32[4]{0:T(128)S(1)} %select_reduce_fusion.1.sel_ref, s32[12]{0:T(128)S(1)} %select_reduce_fusion.own_ref.sel_ref, bf16[576,256]{1,0:T(8,128)(2,1)S(1)} %stage.2.refs_0_, bf16[576,256]{1,0:T(8,128)(2,1)S(1)} %collective-permute-done.3.refs_1_, ...), custom_call_target="tpu_custom_call" | custom-call | bytes 1179648 | tf_op jit(solution)/shard_map/pick_tiles/pallas_call | solution.py:106
  13.6 2.5 %stage.3.refs_6_.refs_5_ = bf16[4096,576]{1,0:T(8,128)(2,1)S(1)} custom-call(bf16[4096,576]{1,0:T(8,128)(2,1)} %bitcast.15), custom_call_target="tpu_custom_call" | custom-call | bytes 9437184 | tf_op jit(solution)/shard_map/stage/pallas_call | solution.py:263
  16.2 1.3 %collective-permute-done.6.refs_2_ = bf16[576,256]{1,0:T(8,128)(2,1)S(1)} collective-permute-done((bf16[576,256]{1,0:T(8,128)(2,1)S(1)}, bf16[576,256]{1,0:T(8,128)(2,1)S(1)}, u32[]{:S(2)}, u32[]{:S(2)}) %collective-permute-start.6) | collective-permute-done | bytes 294944 | tf_op jit(solution)/shard_map/ppermute | solution.py:284
  17.5 2.8 %collective-permute-start.7 = (bf16[576,256]{1,0:T(8,128)(2,1)S(1)}, bf16[576,256]{1,0:T(8,128)(2,1)S(1)}, u32[]{:S(2)}, u32[]{:S(2)}) collective-permute-start(bf16[576,256]{1,0:T(8,128)(2,1)S(1)} %collective-permute-done.6.refs_2_), channel_id=1, source_target_pairs={{0,1},{1,0},{2,3},{3,2},{4,5},{5,4},{6,7},{7,6},{8,9},{9,8},{10,11... | collective-permute-start | bytes 884744 | tf_op jit(solution)/shard_map/ppermute | solution.py:284
  20.4 1.3 %collective-permute-start.12 = (bf16[576,256]{1,0:T(8,128)(2,1)S(1)}, bf16[576,256]{1,0:T(8,128)(2,1)S(1)}, u32[]{:S(2)}, u32[]{:S(2)}) collective-permute-start(bf16[576,256]{1,0:T(8,128)(2,1)S(1)} %get-tuple-element.47), channel_id=1, source_target_pairs={{0,12},{1,13},{2,14},{3,15},{16,28},{17,29},{18,30},{19,31}} | collective-permute-start | bytes 884744 | tf_op jit(solution)/shard_map/ppermute | solution.py:287
  21.7 0.3 collective-permute-done.5.refs_1_
  21.9 0.2 collective-permute-start.10
  22.2 2.0 %collective-permute-start.9 = (bf16[576,256]{1,0:T(8,128)(2,1)S(1)}, bf16[576,256]{1,0:T(8,128)(2,1)S(1)}, u32[]{:S(2)}, u32[]{:S(2)}) collective-permute-start(bf16[576,256]{1,0:T(8,128)(2,1)S(1)} %collective-permute-done.8.refs_0_), channel_id=1, source_target_pairs={{0,1},{1,0},{2,3},{3,2},{4,5},{5,4},{6,7},{7,6},{8,9},{9,8},{10,11... | collective-permute-start | bytes 884744 | tf_op jit(solution)/shard_map/ppermute | solution.py:284
  24.2 7.4 %attend_near.1 = (bf16[4096,512]{1,0:T(8,128)(2,1)S(1)}, f32[4096,128]{1,0:T(8,128)S(1)}, f32[4096,128]{1,0:T(8,128)S(1)}) custom-call(s32[12]{0:T(128)S(1)} %select_reduce_fusion.own_ref.sel_ref, bf16[576,256]{1,0:T(8,128)(2,1)S(1)} %collective-permute-done.refs_0_, bf16[576,256]{1,0:T(8,128)(2,1)S(1)} %collective-permute-done.5.refs_1_, ...), custom_call_target="tpu_custom_call" | custom-call | flops 4563402752 | bytes 8912896 | tf_op jit(solution)/shard_map/attend_near/pallas_call | solution.py:227
  31.7 0.5 %collective-permute-done.12.refs_4_ = bf16[576,256]{1,0:T(8,128)(2,1)S(1)} collective-permute-done((bf16[576,256]{1,0:T(8,128)(2,1)S(1)}, bf16[576,256]{1,0:T(8,128)(2,1)S(1)}, u32[]{:S(2)}, u32[]{:S(2)}) %collective-permute-start.12) | collective-permute-done | bytes 294944 | tf_op jit(solution)/shard_map/ppermute | solution.py:287
  32.1 1.1 %collective-permute-done.11.refs_3_ = bf16[576,256]{1,0:T(8,128)(2,1)S(1)} collective-permute-done((bf16[576,256]{1,0:T(8,128)(2,1)S(1)}, bf16[576,256]{1,0:T(8,128)(2,1)S(1)}, u32[]{:S(2)}, u32[]{:S(2)}) %collective-permute-start.11) | collective-permute-done | bytes 294944 | tf_op jit(solution)/shard_map/ppermute | solution.py:284
  33.2 9.9 %attend_rest.1 = bf16[4096,512]{1,0:T(8,128)(2,1)} custom-call(s32[12]{0:T(128)S(1)} %select_reduce_fusion.own_ref.sel_ref, bf16[576,256]{1,0:T(8,128)(2,1)S(1)} %collective-permute-done.8.refs_0_, bf16[576,256]{1,0:T(8,128)(2,1)S(1)} %collective-permute-done.9.refs_1_, bf16[576,256]{1,0:T(8,128)(2,1)S(1)} %collective-permute-done.10.refs_2_, ...), custom_call_target="tpu_custom_call" | custom-call | flops 4563402752 | bytes 8912896 | tf_op jit(solution)/shard_map/attend_rest/pallas_call | solution.py:227
  (18 shorter events, 0.2 us)
Async XLA Ops:
  0.0 8.9 %collective-permute-start.2 = (bf16[576,256]{1,0:T(8,128)(2,1)}, bf16[576,256]{1,0:T(8,128)(2,1)S(1)}, u32[]{:S(2)}, u32[]{:S(2)}) collective-permute-start(bf16[576,256]{1,0:T(8,128)(2,1)} %bitcast.16), channel_id=1, source_target_pairs={{0,2},{1,3},{2,0},{3,1},{4,6},{5,7},{6,4},{7,5},{8,10},{9,11},{10,... | collective-permute-start | bytes 884744 | tf_op jit(solution)/shard_map/ppermute | solution.py:284
  1.2 9.7 %collective-permute-start = (bf16[576,256]{1,0:T(8,128)(2,1)}, bf16[576,256]{1,0:T(8,128)(2,1)S(1)}, u32[]{:S(2)}, u32[]{:S(2)}) collective-permute-start(bf16[576,256]{1,0:T(8,128)(2,1)} %bitcast.17), channel_id=1, source_target_pairs={{0,4},{1,5},{2,6},{3,7},{4,8},{5,9},{6,10},{7,11},{8,12},{9,13},{1... | collective-permute-start | bytes 884744 | tf_op jit(solution)/shard_map/ppermute | solution.py:287
  2.5 6.4 %collective-permute-start.1 = (s32[1,32]{1,0:T(1,128)}, s32[1,32]{1,0:T(1,128)S(1)}, u32[]{:S(2)}, u32[]{:S(2)}) collective-permute-start(s32[1,32]{1,0:T(1,128)} %param.5), channel_id=1, source_target_pairs={{12,0},{13,1},{14,2},{15,3},{28,16},{29,17},{30,18},{31,19}} | collective-permute-start | bytes 392 | tf_op jit(solution)/shard_map/ppermute | solution.py:297
  8.9 3.7 %collective-permute-start.3 = (bf16[576,256]{1,0:T(8,128)(2,1)S(1)}, bf16[576,256]{1,0:T(8,128)(2,1)S(1)}, u32[]{:S(2)}, u32[]{:S(2)}) collective-permute-start(bf16[576,256]{1,0:T(8,128)(2,1)S(1)} %stage.2.refs_0_), channel_id=1, source_target_pairs={{0,1},{1,0},{2,3},{3,2},{4,5},{5,4},{6,7},{7,6},{8,9},{9,8},{10,11... | collective-permute-start | bytes 884744 | tf_op jit(solution)/shard_map/ppermute | solution.py:284
  10.5 2.1 %collective-permute-start.4 = (bf16[576,256]{1,0:T(8,128)(2,1)S(1)}, bf16[576,256]{1,0:T(8,128)(2,1)S(1)}, u32[]{:S(2)}, u32[]{:S(2)}) collective-permute-start(bf16[576,256]{1,0:T(8,128)(2,1)S(1)} %collective-permute-done.2.refs_2_), channel_id=1, source_target_pairs={{0,1},{1,0},{2,3},{3,2},{4,5},{5,4},{6,7},{7,6},{8,9},{9,8},{10,11... | collective-permute-start | bytes 884744 | tf_op jit(solution)/shard_map/ppermute | solution.py:284
  10.9 6.6 %collective-permute-start.6 = (bf16[576,256]{1,0:T(8,128)(2,1)S(1)}, bf16[576,256]{1,0:T(8,128)(2,1)S(1)}, u32[]{:S(2)}, u32[]{:S(2)}) collective-permute-start(bf16[576,256]{1,0:T(8,128)(2,1)S(1)} %collective-permute-done.refs_0_), channel_id=1, source_target_pairs={{0,2},{1,3},{2,0},{3,1},{4,6},{5,7},{6,4},{7,5},{8,10},{9,11},{10,... | collective-permute-start | bytes 884744 | tf_op jit(solution)/shard_map/ppermute | solution.py:284
  11.3 10.3 %collective-permute-start.8 = (bf16[576,256]{1,0:T(8,128)(2,1)S(1)}, bf16[576,256]{1,0:T(8,128)(2,1)S(1)}, u32[]{:S(2)}, u32[]{:S(2)}) collective-permute-start(bf16[576,256]{1,0:T(8,128)(2,1)S(1)} %collective-permute-done.refs_0_), channel_id=1, source_target_pairs={{4,8},{5,9},{6,10},{7,11},{8,12},{9,13},{10,14},{11,15},{20,24},{2... | collective-permute-start | bytes 884744 | tf_op jit(solution)/shard_map/ppermute | solution.py:287
  17.5 4.1 %collective-permute-start.7 = (bf16[576,256]{1,0:T(8,128)(2,1)S(1)}, bf16[576,256]{1,0:T(8,128)(2,1)S(1)}, u32[]{:S(2)}, u32[]{:S(2)}) collective-permute-start(bf16[576,256]{1,0:T(8,128)(2,1)S(1)} %collective-permute-done.6.refs_2_), channel_id=1, source_target_pairs={{0,1},{1,0},{2,3},{3,2},{4,5},{5,4},{6,7},{7,6},{8,9},{9,8},{10,11... | collective-permute-start | bytes 884744 | tf_op jit(solution)/shard_map/ppermute | solution.py:284
  20.3 1.6 %collective-permute-start.5 = (bf16[576,256]{1,0:T(8,128)(2,1)S(1)}, bf16[576,256]{1,0:T(8,128)(2,1)S(1)}, u32[]{:S(2)}, u32[]{:S(2)}) collective-permute-start(bf16[576,256]{1,0:T(8,128)(2,1)S(1)} %collective-permute-done.refs_0_), channel_id=1, source_target_pairs={{0,1},{1,0},{2,3},{3,2},{4,5},{5,4},{6,7},{7,6},{8,9},{9,8},{10,11... | collective-permute-start | bytes 884744 | tf_op jit(solution)/shard_map/ppermute | solution.py:284
  20.4 11.8 %collective-permute-start.12 = (bf16[576,256]{1,0:T(8,128)(2,1)S(1)}, bf16[576,256]{1,0:T(8,128)(2,1)S(1)}, u32[]{:S(2)}, u32[]{:S(2)}) collective-permute-start(bf16[576,256]{1,0:T(8,128)(2,1)S(1)} %get-tuple-element.47), channel_id=1, source_target_pairs={{0,12},{1,13},{2,14},{3,15},{16,28},{17,29},{18,30},{19,31}} | collective-permute-start | bytes 884744 | tf_op jit(solution)/shard_map/ppermute | solution.py:287
  21.9 9.6 %collective-permute-start.10 = (bf16[576,256]{1,0:T(8,128)(2,1)S(1)}, bf16[576,256]{1,0:T(8,128)(2,1)S(1)}, u32[]{:S(2)}, u32[]{:S(2)}) collective-permute-start(bf16[576,256]{1,0:T(8,128)(2,1)S(1)} %collective-permute-done.8.refs_0_), channel_id=1, source_target_pairs={{0,2},{1,3},{2,0},{3,1},{4,6},{5,7},{6,4},{7,5},{8,10},{9,11},{10,... | collective-permute-start | bytes 884744 | tf_op jit(solution)/shard_map/ppermute | solution.py:284
  22.2 9.9 %collective-permute-start.9 = (bf16[576,256]{1,0:T(8,128)(2,1)S(1)}, bf16[576,256]{1,0:T(8,128)(2,1)S(1)}, u32[]{:S(2)}, u32[]{:S(2)}) collective-permute-start(bf16[576,256]{1,0:T(8,128)(2,1)S(1)} %collective-permute-done.8.refs_0_), channel_id=1, source_target_pairs={{0,1},{1,0},{2,3},{3,2},{4,5},{5,4},{6,7},{7,6},{8,9},{9,8},{10,11... | collective-permute-start | bytes 884744 | tf_op jit(solution)/shard_map/ppermute | solution.py:284
  31.6 1.6 %collective-permute-start.11 = (bf16[576,256]{1,0:T(8,128)(2,1)S(1)}, bf16[576,256]{1,0:T(8,128)(2,1)S(1)}, u32[]{:S(2)}, u32[]{:S(2)}) collective-permute-start(bf16[576,256]{1,0:T(8,128)(2,1)S(1)} %collective-permute-done.10.refs_2_), channel_id=1, source_target_pairs={{0,1},{1,0},{2,3},{3,2},{4,5},{5,4},{6,7},{7,6},{8,9},{9,8},{10,11... | collective-permute-start | bytes 884744 | tf_op jit(solution)/shard_map/ppermute | solution.py:284

commit v5 on v4

--- a/solution.py
+++ b/solution.py
@@ -93,6 +93,24 @@
         )
 
 
+def mixed(factor, without, with_it):
+    return without * (1 - factor) + with_it * factor
+
+
+def lay_out(factors_ref, entry, caches, out_ref):
+    for at in range(0, len(caches), 2):
+        pair = []
+        for one in (at, at + 1):
+            row = 2 * (entry + one)
+            lower, upper = caches[one][:, : 2 * TILE], caches[one][:, 2 * TILE :]
+            block = mixed(factors_ref[row : row + 1, :], lower, upper)
+            swapped = jnp.concatenate([block[:, TILE:], block[:, :TILE]], axis=1)
+            pair.append(mixed(factors_ref[row + 1 : row + 2, :], block, swapped))
+        out_ref[:, at * TILE : (at + 2) * TILE] = jnp.concatenate(
+            [pair[0][:, :TILE], pair[1][:, TILE:]], axis=1
+        )
+
+
 def pick_kernel(sel_ref, own_ref, *refs):
     *caches, sent_ref, kept_ref = refs
     side_by_side(sel_ref, 0, caches, sent_ref)
@@ -144,11 +162,11 @@
     return pieces(summed)
 
 
-def near_kernel(heads, sel_ref, *refs):
+def near_kernel(heads, factors_ref, *refs):
     caches, refs = refs[:ROW], refs[ROW:]
     own_ref, bias_ref, q_ref, mean_ref, top_ref, total_ref, keys_ref = refs
     half = ROW * TILE
-    side_by_side(sel_ref, ROW, caches, keys_ref)
+    lay_out(factors_ref, ROW, caches, keys_ref)
     keys_ref[:, half:] = own_ref[...]
     hidden = jnp.where(lax.axis_index("ctx") >= ROW, 0.0, MASKED)
     rows = q_ref.shape[0] // BLOCKS
@@ -169,7 +187,7 @@
         total_ref[block, :] = total
 
 
-def rest_kernel(sel_ref, *refs):
+def rest_kernel(factors_ref, *refs):
     caches, refs = refs[:ROW], refs[ROW:]
     far_ref, q_ref, mean_ref, top_ref, total_ref, out_hbm, keys_ref, out_ref, sems = refs
     z = lax.axis_index("ctx") // ROW
@@ -182,7 +200,7 @@
     @pl.when(z >= DEPTH - 2)
     def _():
         half = ROW * TILE
-        side_by_side(sel_ref, 2 * ROW, caches, keys_ref)
+        lay_out(factors_ref, 2 * ROW, caches, keys_ref)
         keys_ref[:, half:] = far_ref[...]
         hidden = jnp.where(z >= DEPTH - 1, 0.0, MASKED)
         for at in range(BLOCKS):
@@ -212,7 +230,7 @@
         put(at).wait()
 
 
-def attend(kernel, queries, sel, tiles, state=()):
+def attend(kernel, queries, factors, tiles, state=()):
     count, width = queries.shape
     keys = 2 * ROW * TILE
     vmem = pl.BlockSpec(memory_space=pltpu.VMEM)
@@ -226,7 +244,7 @@
         scratch += [pltpu.VMEM((count, LAT), queries.dtype), pltpu.SemaphoreType.DMA((BLOCKS,))]
     return pl.pallas_call(
         kernel,
-        in_specs=[pl.BlockSpec(memory_space=pltpu.SMEM)] + [vmem] * (len(tiles) + 1 + len(state)),
+        in_specs=[vmem] * (len(tiles) + 2 + len(state)),
         out_specs=[vmem] * 3 if near else pl.BlockSpec(memory_space=pl.ANY),
         out_shape=out_shape,
         scratch_shapes=scratch,
@@ -237,7 +255,7 @@
             bytes_accessed=2 * count * (width + LAT),
         ),
         name="attend_near" if near else "attend_rest",
-    )(sel, *tiles, queries, *state)
+    )(factors, *tiles, queries, *state)
 
 
 def stage_kernel(*refs):
@@ -302,6 +320,12 @@
     slot = jnp.arange((DEPTH - 1) * ROW, dtype=jnp.int32)
     sel = named_tiles(tile_lists, ROW * (z - slot // ROW) + (r ^ slot % ROW))
 
+    entry = jnp.arange(2 * (DEPTH - 1) * ROW, dtype=jnp.int32) // 2
+    tile = jnp.repeat(sel, 2)
+    part = jnp.arange(2 * (DEPTH - 1) * ROW, dtype=jnp.int32) % 2
+    factors = jnp.where(part == 0, tile // 2, (tile + entry) % 2).astype(cache.dtype)
+    factors = jnp.broadcast_to(factors[:, None], (factors.shape[0], 2 * TILE))
+
     far_sel = named_tiles(far_list, me ^ jnp.arange(ROW, dtype=jnp.int32))
     far, keys0 = pick_tiles(far_sel, sel, row0)
     cache2 = further(cache1, 1, range(ROW, span))
@@ -323,10 +347,10 @@
 
     *row1, cache2 = lax.optimization_barrier((*row1, cache2))
     across, beside2 = beside(cache2, 2), beside(cache2, 1)
-    state = attend(functools.partial(near_kernel, shape[1]), queries, sel, [*row1, keys0, bias])
+    state = attend(functools.partial(near_kernel, shape[1]), queries, factors, [*row1, keys0, bias])
     across, *state = lax.optimization_barrier((across, *state))
     row2 = [cache2, beside2, across, beside(across, 1)]
-    out = attend(rest_kernel, queries, sel, [*row2, far], state)
+    out = attend(rest_kernel, queries, factors, [*row2, far], state)
     return out.reshape(*shape[:2], LAT)
 
 

time: 43.5 us -> 42.3 us (0.972)
  Pallas kernels: 21.8 us -> 20.4 us
    pallas_call x2, Pallas kernels: 17.3 us -> 15.8 us  [attend(): pl.pallas_call(kernel, in_specs=[vmem] * (len(tiles) + 2 + len(state)), o...]
    ppermute x9, waiting for transfers between devices: 2.75 us -> 2.25 us  [beside(): return lax.ppermute(array, 'ctx', [(i, i ^ m) for i in range(size)])]
  transfers between devices with their start and end apart: 13 -> 13, of which waited for: 5 -> 5; matrix products, arithmetic and copies ran while one was open for 4% -> 5% of each run, Pallas kernels for 28% -> 27%
where the time goes in v5:
time: 42.3 us; the launch traced here: 41.9 us
  Pallas kernels  20.4 us (48%)
  starting transfers between devices  16.1 us (38%)
  waiting for transfers between devices  3.08 us (7%)
  other arithmetic  1.77 us (4%)
    pallas_call x2, Pallas kernels, attend(): pl.pallas_call(kernel, in_specs=[vmem] * (len(tiles) + 2 + len(state)), o...  15.8 us
    ppermute x9, starting transfers between devices, beside(): return lax.ppermute(array, 'ctx', [(i, i ^ m) for i in range(size)])  8.42 us
    ppermute x3, starting transfers between devices, further(): return lax.ppermute(array, 'ctx', [(i, i + ROW * rows) for i in sources])  3.86 us
    ppermute x1, starting transfers between devices, shards_rows(): lax.ppermute(tile_lists, 'ctx', [(i + span, i) for i in range(ROW)])  3.78 us
    pallas_call x2, Pallas kernels, stage(): pl.pallas_call(stage_kernel, in_specs=[pl.BlockSpec(memory_space=pltpu.HB...  3.57 us
    ppermute x9, waiting for transfers between devices, beside(): return lax.ppermute(array, 'ctx', [(i, i ^ m) for i in range(size)])  2.25 us
    pallas_call x1, Pallas kernels, pick_tiles(): pl.pallas_call(pick_kernel, in_specs=[pl.BlockSpec(memory_space=pltpu.SME...  1 us
  transfers between devices with their start and end apart: 13, of which 5 were waited for; matrix products, arithmetic and copies ran while one was open for 5% of the time, Pallas kernels for 27%

profile of v5, /device:TPU:25, one launch (start us, length us, event | category | flops | bytes accessed | tf_op | source)
XLA Modules:
  0.0 41.9 jit_solution(5856765249132099739)
XLA Ops:
  0.0 1.2 %collective-permute-start.2 = (bf16[576,256]{1,0:T(8,128)(2,1)}, bf16[576,256]{1,0:T(8,128)(2,1)S(1)}, u32[]{:S(2)}, u32[]{:S(2)}) collective-permute-start(bf16[576,256]{1,0:T(8,128)(2,1)} %bitcast.16), channel_id=1, source_target_pairs={{0,2},{1,3},{2,0},{3,1},{4,6},{5,7},{6,4},{7,5},{8,10},{9,11},{10,... | collective-permute-start | bytes 884744 | tf_op jit(solution)/shard_map/ppermute | solution.py:302
  1.2 1.3 %collective-permute-start = (bf16[576,256]{1,0:T(8,128)(2,1)}, bf16[576,256]{1,0:T(8,128)(2,1)S(1)}, u32[]{:S(2)}, u32[]{:S(2)}) collective-permute-start(bf16[576,256]{1,0:T(8,128)(2,1)} %bitcast.17), channel_id=1, source_target_pairs={{0,4},{1,5},{2,6},{3,7},{4,8},{5,9},{6,10},{7,11},{8,12},{9,13},{1... | collective-permute-start | bytes 884744 | tf_op jit(solution)/shard_map/ppermute | solution.py:305
  2.5 3.8 %collective-permute-start.1 = (s32[1,32]{1,0:T(1,128)}, s32[1,32]{1,0:T(1,128)S(1)}, u32[]{:S(2)}, u32[]{:S(2)}) collective-permute-start(s32[1,32]{1,0:T(1,128)} %param.5), channel_id=1, source_target_pairs={{12,0},{13,1},{14,2},{15,3},{28,16},{29,17},{30,18},{31,19}} | collective-permute-start | bytes 392 | tf_op jit(solution)/shard_map/ppermute | solution.py:315
  6.3 0.7 %compare_bitcast_fusion.1 = pred[32]{0:T(512)(128)(4,1)S(1)} fusion(s32[1,32]{1,0:T(1,128)} %param.5), kind=kLoop, calls=%fused_computation.23 | loop fusion | flops 32 | bytes 160 | tf_op jit(solution)/shard_map/and | solution.py:308
  7.0 0.7 %fusion.14 = (s32[32]{0:T(128)S(1)}, s32[32]{0:T(128)S(1)}) fusion(s32[1,32]{1,0:T(1,128)} %param.5), kind=kLoop, calls=%fused_computation.55 | loop fusion | flops 608 | bytes 384 | tf_op jit(solution)/shard_map/eq | solution.py:308
  7.7 0.2 select_reduce_fusion.own_ref
  8.1 1.0 %stage.2.refs_0_ = bf16[576,256]{1,0:T(8,128)(2,1)S(1)} custom-call(bf16[576,256]{1,0:T(8,128)(2,1)} %bitcast.18), custom_call_target="tpu_custom_call" | custom-call | bytes 589824 | tf_op jit(solution)/shard_map/stage/pallas_call | solution.py:281
  9.1 1.6 %collective-permute-start.3 = (bf16[576,256]{1,0:T(8,128)(2,1)S(1)}, bf16[576,256]{1,0:T(8,128)(2,1)S(1)}, u32[]{:S(2)}, u32[]{:S(2)}) collective-permute-start(bf16[576,256]{1,0:T(8,128)(2,1)S(1)} %stage.2.refs_0_), channel_id=1, source_target_pairs={{0,1},{1,0},{2,3},{3,2},{4,5},{5,4},{6,7},{7,6},{8,9},{9,8},{10,11... | collective-permute-start | bytes 884744 | tf_op jit(solution)/shard_map/ppermute | solution.py:302
  10.9 0.2 collective-permute-start.6
  11.1 0.2 select_reduce_fusion.1.sel_ref
  11.3 1.3 %collective-permute-start.8 = (bf16[576,256]{1,0:T(8,128)(2,1)S(1)}, bf16[576,256]{1,0:T(8,128)(2,1)S(1)}, u32[]{:S(2)}, u32[]{:S(2)}) collective-permute-start(bf16[576,256]{1,0:T(8,128)(2,1)S(1)} %collective-permute-done.refs_0_), channel_id=1, source_target_pairs={{4,8},{5,9},{6,10},{7,11},{8,12},{9,13},{10,14},{11,15},{20,24},{2... | collective-permute-start | bytes 884744 | tf_op jit(solution)/shard_map/ppermute | solution.py:305
  12.6 1.0 %pick_tiles.1 = (bf16[576,256]{1,0:T(8,128)(2,1)S(1)}, bf16[576,256]{1,0:T(8,128)(2,1)S(1)}) custom-call(s32[4]{0:T(128)S(1)} %select_reduce_fusion.1.sel_ref, s32[12]{0:T(128)S(1)} %select_reduce_fusion.own_ref, bf16[576,256]{1,0:T(8,128)(2,1)S(1)} %stage.2.refs_0_, bf16[576,256]{1,0:T(8,128)(2,1)S(1)} %collective-permute-done.3.refs_1_, ...), custom_call_target="tpu_custom_call" | custom-call | bytes 1179648 | tf_op jit(solution)/shard_map/pick_tiles/pallas_call | solution.py:124
  13.6 2.5 %stage.3.refs_6_.refs_5_ = bf16[4096,576]{1,0:T(8,128)(2,1)S(1)} custom-call(bf16[4096,576]{1,0:T(8,128)(2,1)} %bitcast.15), custom_call_target="tpu_custom_call" | custom-call | bytes 9437184 | tf_op jit(solution)/shard_map/stage/pallas_call | solution.py:281
  16.2 1.3 %collective-permute-done.6.refs_2_ = bf16[576,256]{1,0:T(8,128)(2,1)S(1)} collective-permute-done((bf16[576,256]{1,0:T(8,128)(2,1)S(1)}, bf16[576,256]{1,0:T(8,128)(2,1)S(1)}, u32[]{:S(2)}, u32[]{:S(2)}) %collective-permute-start.6) | collective-permute-done | bytes 294944 | tf_op jit(solution)/shard_map/ppermute | solution.py:302
  17.5 2.8 %collective-permute-start.7 = (bf16[576,256]{1,0:T(8,128)(2,1)S(1)}, bf16[576,256]{1,0:T(8,128)(2,1)S(1)}, u32[]{:S(2)}, u32[]{:S(2)}) collective-permute-start(bf16[576,256]{1,0:T(8,128)(2,1)S(1)} %collective-permute-done.6.refs_2_), channel_id=1, source_target_pairs={{0,1},{1,0},{2,3},{3,2},{4,5},{5,4},{6,7},{7,6},{8,9},{9,8},{10,11... | collective-permute-start | bytes 884744 | tf_op jit(solution)/shard_map/ppermute | solution.py:302
  20.4 1.3 %collective-permute-start.12 = (bf16[576,256]{1,0:T(8,128)(2,1)S(1)}, bf16[576,256]{1,0:T(8,128)(2,1)S(1)}, u32[]{:S(2)}, u32[]{:S(2)}) collective-permute-start(bf16[576,256]{1,0:T(8,128)(2,1)S(1)} %get-tuple-element.47), channel_id=1, source_target_pairs={{0,12},{1,13},{2,14},{3,15},{16,28},{17,29},{18,30},{19,31}} | collective-permute-start | bytes 884744 | tf_op jit(solution)/shard_map/ppermute | solution.py:305
  21.7 0.3 collective-permute-done.5.refs_1_
  21.9 0.2 collective-permute-start.10
  22.2 2.0 %collective-permute-start.9 = (bf16[576,256]{1,0:T(8,128)(2,1)S(1)}, bf16[576,256]{1,0:T(8,128)(2,1)S(1)}, u32[]{:S(2)}, u32[]{:S(2)}) collective-permute-start(bf16[576,256]{1,0:T(8,128)(2,1)S(1)} %collective-permute-done.8.refs_0_), channel_id=1, source_target_pairs={{0,1},{1,0},{2,3},{3,2},{4,5},{5,4},{6,7},{7,6},{8,9},{9,8},{10,11... | collective-permute-start | bytes 884744 | tf_op jit(solution)/shard_map/ppermute | solution.py:302
  24.2 6.8 %attend_near.1 = (bf16[4096,512]{1,0:T(8,128)(2,1)S(1)}, f32[4096,128]{1,0:T(8,128)S(1)}, f32[4096,128]{1,0:T(8,128)S(1)}) custom-call(bf16[24,128]{1,0:T(8,128)(2,1)S(1)} %broadcast_in_dim.55.factors_ref, bf16[576,256]{1,0:T(8,128)(2,1)S(1)} %collective-permute-done.refs_0_, bf16[576,256]{1,0:T(8,128)(2,1)S(1)} %collective-permute-done.5.refs_1_, ...), custom_call_target="tpu_custom_call" | custom-call | flops 4563402752 | bytes 8912896 | tf_op jit(solution)/shard_map/attend_near/pallas_call | solution.py:245
  31.1 0.3 collective-permute-start.11
  31.4 0.7 %collective-permute-done.12.refs_4_ = bf16[576,256]{1,0:T(8,128)(2,1)S(1)} collective-permute-done((bf16[576,256]{1,0:T(8,128)(2,1)S(1)}, bf16[576,256]{1,0:T(8,128)(2,1)S(1)}, u32[]{:S(2)}, u32[]{:S(2)}) %collective-permute-start.12) | collective-permute-done | bytes 294944 | tf_op jit(solution)/shard_map/ppermute | solution.py:305
  32.1 0.6 %collective-permute-done.11.refs_3_ = bf16[576,256]{1,0:T(8,128)(2,1)S(1)} collective-permute-done((bf16[576,256]{1,0:T(8,128)(2,1)S(1)}, bf16[576,256]{1,0:T(8,128)(2,1)S(1)}, u32[]{:S(2)}, u32[]{:S(2)}) %collective-permute-start.11) | collective-permute-done | bytes 294944 | tf_op jit(solution)/shard_map/ppermute | solution.py:302
  32.7 9.0 %attend_rest.1 = bf16[4096,512]{1,0:T(8,128)(2,1)} custom-call(bf16[24,128]{1,0:T(8,128)(2,1)S(1)} %broadcast_in_dim.55.factors_ref, bf16[576,256]{1,0:T(8,128)(2,1)S(1)} %collective-permute-done.8.refs_0_, bf16[576,256]{1,0:T(8,128)(2,1)S(1)} %collective-permute-done.9.refs_1_, bf16[576,256]{1,0:T(8,128)(2,1)S(1)} %collective-permute-done.10.refs_2_, ...), custom_call_target="tpu_custom_call" | custom-call | flops 4563402752 | bytes 8912896 | tf_op jit(solution)/shard_map/attend_rest/pallas_call | solution.py:245
  (22 shorter events, 0.5 us)
Async XLA Ops:
  0.0 9.1 %collective-permute-start.2 = (bf16[576,256]{1,0:T(8,128)(2,1)}, bf16[576,256]{1,0:T(8,128)(2,1)S(1)}, u32[]{:S(2)}, u32[]{:S(2)}) collective-permute-start(bf16[576,256]{1,0:T(8,128)(2,1)} %bitcast.16), channel_id=1, source_target_pairs={{0,2},{1,3},{2,0},{3,1},{4,6},{5,7},{6,4},{7,5},{8,10},{9,11},{10,... | collective-permute-start | bytes 884744 | tf_op jit(solution)/shard_map/ppermute | solution.py:302
  1.2 9.7 %collective-permute-start = (bf16[576,256]{1,0:T(8,128)(2,1)}, bf16[576,256]{1,0:T(8,128)(2,1)S(1)}, u32[]{:S(2)}, u32[]{:S(2)}) collective-permute-start(bf16[576,256]{1,0:T(8,128)(2,1)} %bitcast.17), channel_id=1, source_target_pairs={{0,4},{1,5},{2,6},{3,7},{4,8},{5,9},{6,10},{7,11},{8,12},{9,13},{1... | collective-permute-start | bytes 884744 | tf_op jit(solution)/shard_map/ppermute | solution.py:305
  2.5 6.6 %collective-permute-start.1 = (s32[1,32]{1,0:T(1,128)}, s32[1,32]{1,0:T(1,128)S(1)}, u32[]{:S(2)}, u32[]{:S(2)}) collective-permute-start(s32[1,32]{1,0:T(1,128)} %param.5), channel_id=1, source_target_pairs={{12,0},{13,1},{14,2},{15,3},{28,16},{29,17},{30,18},{31,19}} | collective-permute-start | bytes 392 | tf_op jit(solution)/shard_map/ppermute | solution.py:315
  9.1 3.5 %collective-permute-start.3 = (bf16[576,256]{1,0:T(8,128)(2,1)S(1)}, bf16[576,256]{1,0:T(8,128)(2,1)S(1)}, u32[]{:S(2)}, u32[]{:S(2)}) collective-permute-start(bf16[576,256]{1,0:T(8,128)(2,1)S(1)} %stage.2.refs_0_), channel_id=1, source_target_pairs={{0,1},{1,0},{2,3},{3,2},{4,5},{5,4},{6,7},{7,6},{8,9},{9,8},{10,11... | collective-permute-start | bytes 884744 | tf_op jit(solution)/shard_map/ppermute | solution.py:302
  10.7 1.9 %collective-permute-start.4 = (bf16[576,256]{1,0:T(8,128)(2,1)S(1)}, bf16[576,256]{1,0:T(8,128)(2,1)S(1)}, u32[]{:S(2)}, u32[]{:S(2)}) collective-permute-start(bf16[576,256]{1,0:T(8,128)(2,1)S(1)} %collective-permute-done.2.refs_2_), channel_id=1, source_target_pairs={{0,1},{1,0},{2,3},{3,2},{4,5},{5,4},{6,7},{7,6},{8,9},{9,8},{10,11... | collective-permute-start | bytes 884744 | tf_op jit(solution)/shard_map/ppermute | solution.py:302
  10.9 6.6 %collective-permute-start.6 = (bf16[576,256]{1,0:T(8,128)(2,1)S(1)}, bf16[576,256]{1,0:T(8,128)(2,1)S(1)}, u32[]{:S(2)}, u32[]{:S(2)}) collective-permute-start(bf16[576,256]{1,0:T(8,128)(2,1)S(1)} %collective-permute-done.refs_0_), channel_id=1, source_target_pairs={{0,2},{1,3},{2,0},{3,1},{4,6},{5,7},{6,4},{7,5},{8,10},{9,11},{10,... | collective-permute-start | bytes 884744 | tf_op jit(solution)/shard_map/ppermute | solution.py:302
  11.3 10.3 %collective-permute-start.8 = (bf16[576,256]{1,0:T(8,128)(2,1)S(1)}, bf16[576,256]{1,0:T(8,128)(2,1)S(1)}, u32[]{:S(2)}, u32[]{:S(2)}) collective-permute-start(bf16[576,256]{1,0:T(8,128)(2,1)S(1)} %collective-permute-done.refs_0_), channel_id=1, source_target_pairs={{4,8},{5,9},{6,10},{7,11},{8,12},{9,13},{10,14},{11,15},{20,24},{2... | collective-permute-start | bytes 884744 | tf_op jit(solution)/shard_map/ppermute | solution.py:305
  17.5 4.1 %collective-permute-start.7 = (bf16[576,256]{1,0:T(8,128)(2,1)S(1)}, bf16[576,256]{1,0:T(8,128)(2,1)S(1)}, u32[]{:S(2)}, u32[]{:S(2)}) collective-permute-start(bf16[576,256]{1,0:T(8,128)(2,1)S(1)} %collective-permute-done.6.refs_2_), channel_id=1, source_target_pairs={{0,1},{1,0},{2,3},{3,2},{4,5},{5,4},{6,7},{7,6},{8,9},{9,8},{10,11... | collective-permute-start | bytes 884744 | tf_op jit(solution)/shard_map/ppermute | solution.py:302
  20.3 1.6 %collective-permute-start.5 = (bf16[576,256]{1,0:T(8,128)(2,1)S(1)}, bf16[576,256]{1,0:T(8,128)(2,1)S(1)}, u32[]{:S(2)}, u32[]{:S(2)}) collective-permute-start(bf16[576,256]{1,0:T(8,128)(2,1)S(1)} %collective-permute-done.refs_0_), channel_id=1, source_target_pairs={{0,1},{1,0},{2,3},{3,2},{4,5},{5,4},{6,7},{7,6},{8,9},{9,8},{10,11... | collective-permute-start | bytes 884744 | tf_op jit(solution)/shard_map/ppermute | solution.py:302
  20.4 11.8 %collective-permute-start.12 = (bf16[576,256]{1,0:T(8,128)(2,1)S(1)}, bf16[576,256]{1,0:T(8,128)(2,1)S(1)}, u32[]{:S(2)}, u32[]{:S(2)}) collective-permute-start(bf16[576,256]{1,0:T(8,128)(2,1)S(1)} %get-tuple-element.47), channel_id=1, source_target_pairs={{0,12},{1,13},{2,14},{3,15},{16,28},{17,29},{18,30},{19,31}} | collective-permute-start | bytes 884744 | tf_op jit(solution)/shard_map/ppermute | solution.py:305
  21.9 9.1 %collective-permute-start.10 = (bf16[576,256]{1,0:T(8,128)(2,1)S(1)}, bf16[576,256]{1,0:T(8,128)(2,1)S(1)}, u32[]{:S(2)}, u32[]{:S(2)}) collective-permute-start(bf16[576,256]{1,0:T(8,128)(2,1)S(1)} %collective-permute-done.8.refs_0_), channel_id=1, source_target_pairs={{0,2},{1,3},{2,0},{3,1},{4,6},{5,7},{6,4},{7,5},{8,10},{9,11},{10,... | collective-permute-start | bytes 884744 | tf_op jit(solution)/shard_map/ppermute | solution.py:302
  22.2 9.9 %collective-permute-start.9 = (bf16[576,256]{1,0:T(8,128)(2,1)S(1)}, bf16[576,256]{1,0:T(8,128)(2,1)S(1)}, u32[]{:S(2)}, u32[]{:S(2)}) collective-permute-start(bf16[576,256]{1,0:T(8,128)(2,1)S(1)} %collective-permute-done.8.refs_0_), channel_id=1, source_target_pairs={{0,1},{1,0},{2,3},{3,2},{4,5},{5,4},{6,7},{7,6},{8,9},{9,8},{10,11... | collective-permute-start | bytes 884744 | tf_op jit(solution)/shard_map/ppermute | solution.py:302
  31.1 1.6 %collective-permute-start.11 = (bf16[576,256]{1,0:T(8,128)(2,1)S(1)}, bf16[576,256]{1,0:T(8,128)(2,1)S(1)}, u32[]{:S(2)}, u32[]{:S(2)}) collective-permute-start(bf16[576,256]{1,0:T(8,128)(2,1)S(1)} %collective-permute-done.10.refs_2_), channel_id=1, source_target_pairs={{0,1},{1,0},{2,3},{3,2},{4,5},{5,4},{6,7},{7,6},{8,9},{9,8},{10,11... | collective-permute-start | bytes 884744 | tf_op jit(solution)/shard_map/ppermute | solution.py:302

commit v6 on v5

--- a/solution.py
+++ b/solution.py
@@ -305,8 +305,9 @@
         return lax.ppermute(array, "ctx", [(i, i + ROW * rows) for i in sources])
 
     def named_tiles(listing, holders):
-        hit = (listing >= 0) & (listing // TILES_DEV == holders[:, None])
-        return jnp.sum(jnp.where(hit, listing % TILES_DEV, 0), axis=1)
+        tile = listing - TILES_DEV * holders[:, None]
+        hit = (listing >= 0) & (tile >= 0) & (tile < TILES_DEV)
+        return jnp.sum(jnp.where(hit, tile, 0), axis=1)
 
     shape = queries.shape
     cache = latent_cache.T

time: 42.3 us -> 42.3 us (level)
    eq x2 -> x0, other arithmetic: 0.67 us -> none  [named_tiles(): hit = (listing >= 0) & (listing // TILES_DEV == holders[:, None])]
    reduce_sum x2, other arithmetic: 0.37 us -> 1.03 us  [named_tiles(): return jnp.sum(jnp.where(hit, tile, 0), axis=1)]
where the time goes in v6:
time: 42.3 us; the launch traced here: 41.9 us
  Pallas kernels  20.4 us (48%)
  starting transfers between devices  16.1 us (38%)
  waiting for transfers between devices  3.09 us (7%)
  other arithmetic  1.76 us (4%)
    pallas_call x2, Pallas kernels, attend(): pl.pallas_call(kernel, in_specs=[vmem] * (len(tiles) + 2 + len(state)), o...  15.8 us
    ppermute x9, starting transfers between devices, beside(): return lax.ppermute(array, 'ctx', [(i, i ^ m) for i in range(size)])  8.42 us
    ppermute x3, starting transfers between devices, further(): return lax.ppermute(array, 'ctx', [(i, i + ROW * rows) for i in sources])  3.86 us
    ppermute x1, starting transfers between devices, shards_rows(): lax.ppermute(tile_lists, 'ctx', [(i + span, i) for i in range(ROW)])  3.78 us
    pallas_call x2, Pallas kernels, stage(): pl.pallas_call(stage_kernel, in_specs=[pl.BlockSpec(memory_space=pltpu.HB...  3.56 us
    ppermute x9, waiting for transfers between devices, beside(): return lax.ppermute(array, 'ctx', [(i, i ^ m) for i in range(size)])  2.24 us
    reduce_sum x2, other arithmetic, named_tiles(): return jnp.sum(jnp.where(hit, tile, 0), axis=1)  1.03 us
    pallas_call x1, Pallas kernels, pick_tiles(): pl.pallas_call(pick_kernel, in_specs=[pl.BlockSpec(memory_space=pltpu.SME...  1.01 us
  transfers between devices with their start and end apart: 13, of which 5 were waited for; matrix products, arithmetic and copies ran while one was open for 5% of the time, Pallas kernels for 27%

profile of v6, /device:TPU:25, one launch (start us, length us, event | category | flops | bytes accessed | tf_op | source)
XLA Modules:
  0.0 41.9 jit_solution(7473033583019271802)
XLA Ops:
  0.0 1.2 %collective-permute-start.2 = (bf16[576,256]{1,0:T(8,128)(2,1)}, bf16[576,256]{1,0:T(8,128)(2,1)S(1)}, u32[]{:S(2)}, u32[]{:S(2)}) collective-permute-start(bf16[576,256]{1,0:T(8,128)(2,1)} %bitcast.10), channel_id=1, source_target_pairs={{0,2},{1,3},{2,0},{3,1},{4,6},{5,7},{6,4},{7,5},{8,10},{9,11},{10,... | collective-permute-start | bytes 884744 | tf_op jit(solution)/shard_map/ppermute | solution.py:302
  1.2 1.3 %collective-permute-start = (bf16[576,256]{1,0:T(8,128)(2,1)}, bf16[576,256]{1,0:T(8,128)(2,1)S(1)}, u32[]{:S(2)}, u32[]{:S(2)}) collective-permute-start(bf16[576,256]{1,0:T(8,128)(2,1)} %bitcast.11), channel_id=1, source_target_pairs={{0,4},{1,5},{2,6},{3,7},{4,8},{5,9},{6,10},{7,11},{8,12},{9,13},{1... | collective-permute-start | bytes 884744 | tf_op jit(solution)/shard_map/ppermute | solution.py:305
  2.5 3.8 %collective-permute-start.1 = (s32[1,32]{1,0:T(1,128)}, s32[1,32]{1,0:T(1,128)S(1)}, u32[]{:S(2)}, u32[]{:S(2)}) collective-permute-start(s32[1,32]{1,0:T(1,128)} %param.5), channel_id=1, source_target_pairs={{12,0},{13,1},{14,2},{15,3},{28,16},{29,17},{30,18},{31,19}} | collective-permute-start | bytes 392 | tf_op jit(solution)/shard_map/ppermute | solution.py:316
  6.3 0.7 %compare_bitcast_fusion.1 = pred[32]{0:T(512)(128)(4,1)S(1)} fusion(s32[1,32]{1,0:T(1,128)} %param.5), kind=kLoop, calls=%fused_computation.29 | loop fusion | flops 32 | bytes 160 | tf_op jit(solution)/shard_map/and | solution.py:309
  7.0 1.0 %stage.2.refs_0_ = bf16[576,256]{1,0:T(8,128)(2,1)S(1)} custom-call(bf16[576,256]{1,0:T(8,128)(2,1)} %bitcast.12), custom_call_target="tpu_custom_call" | custom-call | bytes 589824 | tf_op jit(solution)/shard_map/stage/pallas_call | solution.py:281
  8.1 0.8 %fusion.3.own_ref = s32[12]{0:T(128)S(1)} fusion(s32[12]{0:T(128)S(1)} %fusion.13, s32[32]{0:T(128)} %bitcast.13, pred[32]{0:T(512)(128)(4,1)S(1)} %compare_bitcast_fusion.1), kind=kLoop, calls=%fused_computation.7 | loop fusion | flops 2676 | bytes 256 | tf_op jit(solution)/shard_map/reduce_sum | solution.py:310
  9.1 1.6 %collective-permute-start.3 = (bf16[576,256]{1,0:T(8,128)(2,1)S(1)}, bf16[576,256]{1,0:T(8,128)(2,1)S(1)}, u32[]{:S(2)}, u32[]{:S(2)}) collective-permute-start(bf16[576,256]{1,0:T(8,128)(2,1)S(1)} %stage.2.refs_0_), channel_id=1, source_target_pairs={{0,1},{1,0},{2,3},{3,2},{4,5},{5,4},{6,7},{7,6},{8,9},{9,8},{10,11... | collective-permute-start | bytes 884744 | tf_op jit(solution)/shard_map/ppermute | solution.py:302
  10.8 0.1 collective-permute-done.refs_0_
  10.9 0.2 collective-permute-start.6
  11.1 0.2 fusion.6.sel_ref
  11.3 1.3 %collective-permute-start.8 = (bf16[576,256]{1,0:T(8,128)(2,1)S(1)}, bf16[576,256]{1,0:T(8,128)(2,1)S(1)}, u32[]{:S(2)}, u32[]{:S(2)}) collective-permute-start(bf16[576,256]{1,0:T(8,128)(2,1)S(1)} %collective-permute-done.refs_0_), channel_id=1, source_target_pairs={{4,8},{5,9},{6,10},{7,11},{8,12},{9,13},{10,14},{11,15},{20,24},{2... | collective-permute-start | bytes 884744 | tf_op jit(solution)/shard_map/ppermute | solution.py:305
  12.6 1.0 %pick_tiles.1 = (bf16[576,256]{1,0:T(8,128)(2,1)S(1)}, bf16[576,256]{1,0:T(8,128)(2,1)S(1)}) custom-call(s32[4]{0:T(128)S(1)} %fusion.6.sel_ref, s32[12]{0:T(128)S(1)} %fusion.3.own_ref, bf16[576,256]{1,0:T(8,128)(2,1)S(1)} %stage.2.refs_0_, bf16[576,256]{1,0:T(8,128)(2,1)S(1)} %collective-permute-done.3.refs_1_, ...), custom_call_target="tpu_custom_call" | custom-call | bytes 1179648 | tf_op jit(solution)/shard_map/pick_tiles/pallas_call | solution.py:124
  13.6 2.5 %stage.3.refs_6_.refs_5_ = bf16[4096,576]{1,0:T(8,128)(2,1)S(1)} custom-call(bf16[4096,576]{1,0:T(8,128)(2,1)} %bitcast.9), custom_call_target="tpu_custom_call" | custom-call | bytes 9437184 | tf_op jit(solution)/shard_map/stage/pallas_call | solution.py:281
  16.2 1.3 %collective-permute-done.6.refs_2_ = bf16[576,256]{1,0:T(8,128)(2,1)S(1)} collective-permute-done((bf16[576,256]{1,0:T(8,128)(2,1)S(1)}, bf16[576,256]{1,0:T(8,128)(2,1)S(1)}, u32[]{:S(2)}, u32[]{:S(2)}) %collective-permute-start.6) | collective-permute-done | bytes 294944 | tf_op jit(solution)/shard_map/ppermute | solution.py:302
  17.5 2.8 %collective-permute-start.7 = (bf16[576,256]{1,0:T(8,128)(2,1)S(1)}, bf16[576,256]{1,0:T(8,128)(2,1)S(1)}, u32[]{:S(2)}, u32[]{:S(2)}) collective-permute-start(bf16[576,256]{1,0:T(8,128)(2,1)S(1)} %collective-permute-done.6.refs_2_), channel_id=1, source_target_pairs={{0,1},{1,0},{2,3},{3,2},{4,5},{5,4},{6,7},{7,6},{8,9},{9,8},{10,11... | collective-permute-start | bytes 884744 | tf_op jit(solution)/shard_map/ppermute | solution.py:302
  20.4 1.3 %collective-permute-start.12 = (bf16[576,256]{1,0:T(8,128)(2,1)S(1)}, bf16[576,256]{1,0:T(8,128)(2,1)S(1)}, u32[]{:S(2)}, u32[]{:S(2)}) collective-permute-start(bf16[576,256]{1,0:T(8,128)(2,1)S(1)} %get-tuple-element.47), channel_id=1, source_target_pairs={{0,12},{1,13},{2,14},{3,15},{16,28},{17,29},{18,30},{19,31}} | collective-permute-start | bytes 884744 | tf_op jit(solution)/shard_map/ppermute | solution.py:305
  21.7 0.3 collective-permute-done.5.refs_1_
  21.9 0.2 collective-permute-start.10
  22.2 2.0 %collective-permute-start.9 = (bf16[576,256]{1,0:T(8,128)(2,1)S(1)}, bf16[576,256]{1,0:T(8,128)(2,1)S(1)}, u32[]{:S(2)}, u32[]{:S(2)}) collective-permute-start(bf16[576,256]{1,0:T(8,128)(2,1)S(1)} %collective-permute-done.8.refs_0_), channel_id=1, source_target_pairs={{0,1},{1,0},{2,3},{3,2},{4,5},{5,4},{6,7},{7,6},{8,9},{9,8},{10,11... | collective-permute-start | bytes 884744 | tf_op jit(solution)/shard_map/ppermute | solution.py:302
  24.2 6.8 %attend_near.1 = (bf16[4096,512]{1,0:T(8,128)(2,1)S(1)}, f32[4096,128]{1,0:T(8,128)S(1)}, f32[4096,128]{1,0:T(8,128)S(1)}) custom-call(bf16[24,128]{1,0:T(8,128)(2,1)S(1)} %broadcast_in_dim.15.factors_ref, bf16[576,256]{1,0:T(8,128)(2,1)S(1)} %collective-permute-done.refs_0_, bf16[576,256]{1,0:T(8,128)(2,1)S(1)} %collective-permute-done.5.refs_1_, ...), custom_call_target="tpu_custom_call" | custom-call | flops 4563402752 | bytes 8912896 | tf_op jit(solution)/shard_map/attend_near/pallas_call | solution.py:245
  31.1 0.3 collective-permute-start.11
  31.4 0.7 %collective-permute-done.12.refs_4_ = bf16[576,256]{1,0:T(8,128)(2,1)S(1)} collective-permute-done((bf16[576,256]{1,0:T(8,128)(2,1)S(1)}, bf16[576,256]{1,0:T(8,128)(2,1)S(1)}, u32[]{:S(2)}, u32[]{:S(2)}) %collective-permute-start.12) | collective-permute-done | bytes 294944 | tf_op jit(solution)/shard_map/ppermute | solution.py:305
  32.1 0.6 %collective-permute-done.11.refs_3_ = bf16[576,256]{1,0:T(8,128)(2,1)S(1)} collective-permute-done((bf16[576,256]{1,0:T(8,128)(2,1)S(1)}, bf16[576,256]{1,0:T(8,128)(2,1)S(1)}, u32[]{:S(2)}, u32[]{:S(2)}) %collective-permute-start.11) | collective-permute-done | bytes 294944 | tf_op jit(solution)/shard_map/ppermute | solution.py:302
  32.7 9.0 %attend_rest.1 = bf16[4096,512]{1,0:T(8,128)(2,1)} custom-call(bf16[24,128]{1,0:T(8,128)(2,1)S(1)} %broadcast_in_dim.15.factors_ref, bf16[576,256]{1,0:T(8,128)(2,1)S(1)} %collective-permute-done.8.refs_0_, bf16[576,256]{1,0:T(8,128)(2,1)S(1)} %collective-permute-done.9.refs_1_, bf16[576,256]{1,0:T(8,128)(2,1)S(1)} %collective-permute-done.10.refs_2_, ...), custom_call_target="tpu_custom_call" | custom-call | flops 4563402752 | bytes 8912896 | tf_op jit(solution)/shard_map/attend_rest/pallas_call | solution.py:245
  (20 shorter events, 0.4 us)
Async XLA Ops:
  0.0 9.1 %collective-permute-start.2 = (bf16[576,256]{1,0:T(8,128)(2,1)}, bf16[576,256]{1,0:T(8,128)(2,1)S(1)}, u32[]{:S(2)}, u32[]{:S(2)}) collective-permute-start(bf16[576,256]{1,0:T(8,128)(2,1)} %bitcast.10), channel_id=1, source_target_pairs={{0,2},{1,3},{2,0},{3,1},{4,6},{5,7},{6,4},{7,5},{8,10},{9,11},{10,... | collective-permute-start | bytes 884744 | tf_op jit(solution)/shard_map/ppermute | solution.py:302
  1.2 9.7 %collective-permute-start = (bf16[576,256]{1,0:T(8,128)(2,1)}, bf16[576,256]{1,0:T(8,128)(2,1)S(1)}, u32[]{:S(2)}, u32[]{:S(2)}) collective-permute-start(bf16[576,256]{1,0:T(8,128)(2,1)} %bitcast.11), channel_id=1, source_target_pairs={{0,4},{1,5},{2,6},{3,7},{4,8},{5,9},{6,10},{7,11},{8,12},{9,13},{1... | collective-permute-start | bytes 884744 | tf_op jit(solution)/shard_map/ppermute | solution.py:305
  2.5 8.6 %collective-permute-start.1 = (s32[1,32]{1,0:T(1,128)}, s32[1,32]{1,0:T(1,128)S(1)}, u32[]{:S(2)}, u32[]{:S(2)}) collective-permute-start(s32[1,32]{1,0:T(1,128)} %param.5), channel_id=1, source_target_pairs={{12,0},{13,1},{14,2},{15,3},{28,16},{29,17},{30,18},{31,19}} | collective-permute-start | bytes 392 | tf_op jit(solution)/shard_map/ppermute | solution.py:316
  9.1 3.5 %collective-permute-start.3 = (bf16[576,256]{1,0:T(8,128)(2,1)S(1)}, bf16[576,256]{1,0:T(8,128)(2,1)S(1)}, u32[]{:S(2)}, u32[]{:S(2)}) collective-permute-start(bf16[576,256]{1,0:T(8,128)(2,1)S(1)} %stage.2.refs_0_), channel_id=1, source_target_pairs={{0,1},{1,0},{2,3},{3,2},{4,5},{5,4},{6,7},{7,6},{8,9},{9,8},{10,11... | collective-permute-start | bytes 884744 | tf_op jit(solution)/shard_map/ppermute | solution.py:302
  10.7 1.9 %collective-permute-start.4 = (bf16[576,256]{1,0:T(8,128)(2,1)S(1)}, bf16[576,256]{1,0:T(8,128)(2,1)S(1)}, u32[]{:S(2)}, u32[]{:S(2)}) collective-permute-start(bf16[576,256]{1,0:T(8,128)(2,1)S(1)} %collective-permute-done.2.refs_2_), channel_id=1, source_target_pairs={{0,1},{1,0},{2,3},{3,2},{4,5},{5,4},{6,7},{7,6},{8,9},{9,8},{10,11... | collective-permute-start | bytes 884744 | tf_op jit(solution)/shard_map/ppermute | solution.py:302
  10.9 6.6 %collective-permute-start.6 = (bf16[576,256]{1,0:T(8,128)(2,1)S(1)}, bf16[576,256]{1,0:T(8,128)(2,1)S(1)}, u32[]{:S(2)}, u32[]{:S(2)}) collective-permute-start(bf16[576,256]{1,0:T(8,128)(2,1)S(1)} %collective-permute-done.refs_0_), channel_id=1, source_target_pairs={{0,2},{1,3},{2,0},{3,1},{4,6},{5,7},{6,4},{7,5},{8,10},{9,11},{10,... | collective-permute-start | bytes 884744 | tf_op jit(solution)/shard_map/ppermute | solution.py:302
  11.3 10.3 %collective-permute-start.8 = (bf16[576,256]{1,0:T(8,128)(2,1)S(1)}, bf16[576,256]{1,0:T(8,128)(2,1)S(1)}, u32[]{:S(2)}, u32[]{:S(2)}) collective-permute-start(bf16[576,256]{1,0:T(8,128)(2,1)S(1)} %collective-permute-done.refs_0_), channel_id=1, source_target_pairs={{4,8},{5,9},{6,10},{7,11},{8,12},{9,13},{10,14},{11,15},{20,24},{2... | collective-permute-start | bytes 884744 | tf_op jit(solution)/shard_map/ppermute | solution.py:305
  17.5 4.1 %collective-permute-start.7 = (bf16[576,256]{1,0:T(8,128)(2,1)S(1)}, bf16[576,256]{1,0:T(8,128)(2,1)S(1)}, u32[]{:S(2)}, u32[]{:S(2)}) collective-permute-start(bf16[576,256]{1,0:T(8,128)(2,1)S(1)} %collective-permute-done.6.refs_2_), channel_id=1, source_target_pairs={{0,1},{1,0},{2,3},{3,2},{4,5},{5,4},{6,7},{7,6},{8,9},{9,8},{10,11... | collective-permute-start | bytes 884744 | tf_op jit(solution)/shard_map/ppermute | solution.py:302
  20.3 1.6 %collective-permute-start.5 = (bf16[576,256]{1,0:T(8,128)(2,1)S(1)}, bf16[576,256]{1,0:T(8,128)(2,1)S(1)}, u32[]{:S(2)}, u32[]{:S(2)}) collective-permute-start(bf16[576,256]{1,0:T(8,128)(2,1)S(1)} %collective-permute-done.refs_0_), channel_id=1, source_target_pairs={{0,1},{1,0},{2,3},{3,2},{4,5},{5,4},{6,7},{7,6},{8,9},{9,8},{10,11... | collective-permute-start | bytes 884744 | tf_op jit(solution)/shard_map/ppermute | solution.py:302
  20.4 11.8 %collective-permute-start.12 = (bf16[576,256]{1,0:T(8,128)(2,1)S(1)}, bf16[576,256]{1,0:T(8,128)(2,1)S(1)}, u32[]{:S(2)}, u32[]{:S(2)}) collective-permute-start(bf16[576,256]{1,0:T(8,128)(2,1)S(1)} %get-tuple-element.47), channel_id=1, source_target_pairs={{0,12},{1,13},{2,14},{3,15},{16,28},{17,29},{18,30},{19,31}} | collective-permute-start | bytes 884744 | tf_op jit(solution)/shard_map/ppermute | solution.py:305
  21.9 9.1 %collective-permute-start.10 = (bf16[576,256]{1,0:T(8,128)(2,1)S(1)}, bf16[576,256]{1,0:T(8,128)(2,1)S(1)}, u32[]{:S(2)}, u32[]{:S(2)}) collective-permute-start(bf16[576,256]{1,0:T(8,128)(2,1)S(1)} %collective-permute-done.8.refs_0_), channel_id=1, source_target_pairs={{0,2},{1,3},{2,0},{3,1},{4,6},{5,7},{6,4},{7,5},{8,10},{9,11},{10,... | collective-permute-start | bytes 884744 | tf_op jit(solution)/shard_map/ppermute | solution.py:302
  22.2 9.9 %collective-permute-start.9 = (bf16[576,256]{1,0:T(8,128)(2,1)S(1)}, bf16[576,256]{1,0:T(8,128)(2,1)S(1)}, u32[]{:S(2)}, u32[]{:S(2)}) collective-permute-start(bf16[576,256]{1,0:T(8,128)(2,1)S(1)} %collective-permute-done.8.refs_0_), channel_id=1, source_target_pairs={{0,1},{1,0},{2,3},{3,2},{4,5},{5,4},{6,7},{7,6},{8,9},{9,8},{10,11... | collective-permute-start | bytes 884744 | tf_op jit(solution)/shard_map/ppermute | solution.py:302
  31.1 1.6 %collective-permute-start.11 = (bf16[576,256]{1,0:T(8,128)(2,1)S(1)}, bf16[576,256]{1,0:T(8,128)(2,1)S(1)}, u32[]{:S(2)}, u32[]{:S(2)}) collective-permute-start(bf16[576,256]{1,0:T(8,128)(2,1)S(1)} %collective-permute-done.10.refs_2_), channel_id=1, source_target_pairs={{0,1},{1,0},{2,3},{3,2},{4,5},{5,4},{6,7},{7,6},{8,9},{9,8},{10,11... | collective-permute-start | bytes 884744 | tf_op jit(solution)/shard_map/ppermute | solution.py:302

commit v7 on v6

--- a/solution.py
+++ b/solution.py
@@ -347,8 +347,10 @@
     bias = jnp.where(seen, 0.0, MASKED).astype(jnp.float32)
 
     *row1, cache2 = lax.optimization_barrier((*row1, cache2))
-    across, beside2 = beside(cache2, 2), beside(cache2, 1)
+    across = beside(cache2, 2)
     state = attend(functools.partial(near_kernel, shape[1]), queries, factors, [*row1, keys0, bias])
+    cache2, *state = lax.optimization_barrier((cache2, *state))
+    beside2 = beside(cache2, 1)
     across, *state = lax.optimization_barrier((across, *state))
     row2 = [cache2, beside2, across, beside(across, 1)]
     out = attend(rest_kernel, queries, factors, [*row2, far], state)

time: 42.3 us -> 42.3 us (level)
  transfers between devices with their start and end apart: 13 -> 13, of which waited for: 5 -> 6; matrix products, arithmetic and copies ran while one was open for 5% -> 5% of each run, Pallas kernels for 27% -> 27%
where the time goes in v7:
time: 42.3 us; the launch traced here: 41.9 us
  Pallas kernels  20.4 us (48%)
  starting transfers between devices  16.1 us (38%)
  waiting for transfers between devices  3.13 us (7%)
  other arithmetic  1.76 us (4%)
    pallas_call x2, Pallas kernels, attend(): pl.pallas_call(kernel, in_specs=[vmem] * (len(tiles) + 2 + len(state)), o...  15.8 us
    ppermute x9, starting transfers between devices, beside(): return lax.ppermute(array, 'ctx', [(i, i ^ m) for i in range(size)])  8.42 us
    ppermute x3, starting transfers between devices, further(): return lax.ppermute(array, 'ctx', [(i, i + ROW * rows) for i in sources])  3.86 us
    ppermute x1, starting transfers between devices, shards_rows(): lax.ppermute(tile_lists, 'ctx', [(i + span, i) for i in range(ROW)])  3.78 us
    pallas_call x2, Pallas kernels, stage(): pl.pallas_call(stage_kernel, in_specs=[pl.BlockSpec(memory_space=pltpu.HB...  3.56 us
    ppermute x9, waiting for transfers between devices, beside(): return lax.ppermute(array, 'ctx', [(i, i ^ m) for i in range(size)])  2.28 us
    reduce_sum x2, other arithmetic, named_tiles(): return jnp.sum(jnp.where(hit, tile, 0), axis=1)  1.03 us
    pallas_call x1, Pallas kernels, pick_tiles(): pl.pallas_call(pick_kernel, in_specs=[pl.BlockSpec(memory_space=pltpu.SME...  1.01 us
  transfers between devices with their start and end apart: 13, of which 6 were waited for; matrix products, arithmetic and copies ran while one was open for 5% of the time, Pallas kernels for 27%

profile of v7, /device:TPU:25, one launch (start us, length us, event | category | flops | bytes accessed | tf_op | source)
XLA Modules:
  0.0 41.9 jit_solution(9625388962735227593)
XLA Ops:
  0.0 1.2 %collective-permute-start.2 = (bf16[576,256]{1,0:T(8,128)(2,1)}, bf16[576,256]{1,0:T(8,128)(2,1)S(1)}, u32[]{:S(2)}, u32[]{:S(2)}) collective-permute-start(bf16[576,256]{1,0:T(8,128)(2,1)} %bitcast.10), channel_id=1, source_target_pairs={{0,2},{1,3},{2,0},{3,1},{4,6},{5,7},{6,4},{7,5},{8,10},{9,11},{10,... | collective-permute-start | bytes 884744 | tf_op jit(solution)/shard_map/ppermute | solution.py:302
  1.2 1.3 %collective-permute-start = (bf16[576,256]{1,0:T(8,128)(2,1)}, bf16[576,256]{1,0:T(8,128)(2,1)S(1)}, u32[]{:S(2)}, u32[]{:S(2)}) collective-permute-start(bf16[576,256]{1,0:T(8,128)(2,1)} %bitcast.11), channel_id=1, source_target_pairs={{0,4},{1,5},{2,6},{3,7},{4,8},{5,9},{6,10},{7,11},{8,12},{9,13},{1... | collective-permute-start | bytes 884744 | tf_op jit(solution)/shard_map/ppermute | solution.py:305
  2.5 3.8 %collective-permute-start.1 = (s32[1,32]{1,0:T(1,128)}, s32[1,32]{1,0:T(1,128)S(1)}, u32[]{:S(2)}, u32[]{:S(2)}) collective-permute-start(s32[1,32]{1,0:T(1,128)} %param.5), channel_id=1, source_target_pairs={{12,0},{13,1},{14,2},{15,3},{28,16},{29,17},{30,18},{31,19}} | collective-permute-start | bytes 392 | tf_op jit(solution)/shard_map/ppermute | solution.py:316
  6.3 0.7 %compare_bitcast_fusion.1 = pred[32]{0:T(512)(128)(4,1)S(1)} fusion(s32[1,32]{1,0:T(1,128)} %param.5), kind=kLoop, calls=%fused_computation.29 | loop fusion | flops 32 | bytes 160 | tf_op jit(solution)/shard_map/and | solution.py:309
  7.0 1.0 %stage.2.refs_0_ = bf16[576,256]{1,0:T(8,128)(2,1)S(1)} custom-call(bf16[576,256]{1,0:T(8,128)(2,1)} %bitcast.12), custom_call_target="tpu_custom_call" | custom-call | bytes 589824 | tf_op jit(solution)/shard_map/stage/pallas_call | solution.py:281
  8.1 0.8 %fusion.3.own_ref = s32[12]{0:T(128)S(1)} fusion(s32[12]{0:T(128)S(1)} %fusion.13, s32[32]{0:T(128)} %bitcast.13, pred[32]{0:T(512)(128)(4,1)S(1)} %compare_bitcast_fusion.1), kind=kLoop, calls=%fused_computation.7 | loop fusion | flops 2676 | bytes 256 | tf_op jit(solution)/shard_map/reduce_sum | solution.py:310
  9.1 1.6 %collective-permute-start.3 = (bf16[576,256]{1,0:T(8,128)(2,1)S(1)}, bf16[576,256]{1,0:T(8,128)(2,1)S(1)}, u32[]{:S(2)}, u32[]{:S(2)}) collective-permute-start(bf16[576,256]{1,0:T(8,128)(2,1)S(1)} %stage.2.refs_0_), channel_id=1, source_target_pairs={{0,1},{1,0},{2,3},{3,2},{4,5},{5,4},{6,7},{7,6},{8,9},{9,8},{10,11... | collective-permute-start | bytes 884744 | tf_op jit(solution)/shard_map/ppermute | solution.py:302
  10.9 0.2 collective-permute-start.6
  11.1 0.2 fusion.6.sel_ref
  11.3 1.3 %collective-permute-start.8 = (bf16[576,256]{1,0:T(8,128)(2,1)S(1)}, bf16[576,256]{1,0:T(8,128)(2,1)S(1)}, u32[]{:S(2)}, u32[]{:S(2)}) collective-permute-start(bf16[576,256]{1,0:T(8,128)(2,1)S(1)} %collective-permute-done.refs_0_), channel_id=1, source_target_pairs={{4,8},{5,9},{6,10},{7,11},{8,12},{9,13},{10,14},{11,15},{20,24},{2... | collective-permute-start | bytes 884744 | tf_op jit(solution)/shard_map/ppermute | solution.py:305
  12.6 1.0 %pick_tiles.1 = (bf16[576,256]{1,0:T(8,128)(2,1)S(1)}, bf16[576,256]{1,0:T(8,128)(2,1)S(1)}) custom-call(s32[4]{0:T(128)S(1)} %fusion.6.sel_ref, s32[12]{0:T(128)S(1)} %fusion.3.own_ref, bf16[576,256]{1,0:T(8,128)(2,1)S(1)} %stage.2.refs_0_, bf16[576,256]{1,0:T(8,128)(2,1)S(1)} %collective-permute-done.3.refs_1_, ...), custom_call_target="tpu_custom_call" | custom-call | bytes 1179648 | tf_op jit(solution)/shard_map/pick_tiles/pallas_call | solution.py:124
  13.6 2.5 %stage.3.refs_6_.refs_5_ = bf16[4096,576]{1,0:T(8,128)(2,1)S(1)} custom-call(bf16[4096,576]{1,0:T(8,128)(2,1)} %bitcast.9), custom_call_target="tpu_custom_call" | custom-call | bytes 9437184 | tf_op jit(solution)/shard_map/stage/pallas_call | solution.py:281
  16.2 1.3 %collective-permute-done.6.refs_2_ = bf16[576,256]{1,0:T(8,128)(2,1)S(1)} collective-permute-done((bf16[576,256]{1,0:T(8,128)(2,1)S(1)}, bf16[576,256]{1,0:T(8,128)(2,1)S(1)}, u32[]{:S(2)}, u32[]{:S(2)}) %collective-permute-start.6) | collective-permute-done | bytes 294944 | tf_op jit(solution)/shard_map/ppermute | solution.py:302
  17.5 2.8 %collective-permute-start.7 = (bf16[576,256]{1,0:T(8,128)(2,1)S(1)}, bf16[576,256]{1,0:T(8,128)(2,1)S(1)}, u32[]{:S(2)}, u32[]{:S(2)}) collective-permute-start(bf16[576,256]{1,0:T(8,128)(2,1)S(1)} %collective-permute-done.6.refs_2_), channel_id=1, source_target_pairs={{0,1},{1,0},{2,3},{3,2},{4,5},{5,4},{6,7},{7,6},{8,9},{9,8},{10,11... | collective-permute-start | bytes 884744 | tf_op jit(solution)/shard_map/ppermute | solution.py:302
  20.4 1.3 %collective-permute-start.12 = (bf16[576,256]{1,0:T(8,128)(2,1)S(1)}, bf16[576,256]{1,0:T(8,128)(2,1)S(1)}, u32[]{:S(2)}, u32[]{:S(2)}) collective-permute-start(bf16[576,256]{1,0:T(8,128)(2,1)S(1)} %get-tuple-element.55), channel_id=1, source_target_pairs={{0,12},{1,13},{2,14},{3,15},{16,28},{17,29},{18,30},{19,31}} | collective-permute-start | bytes 884744 | tf_op jit(solution)/shard_map/ppermute | solution.py:305
  21.7 0.3 collective-permute-done.5.refs_1_
  21.9 0.2 collective-permute-start.10
  22.2 6.8 %attend_near.1 = (bf16[4096,512]{1,0:T(8,128)(2,1)S(1)}, f32[4096,128]{1,0:T(8,128)S(1)}, f32[4096,128]{1,0:T(8,128)S(1)}) custom-call(bf16[24,128]{1,0:T(8,128)(2,1)S(1)} %broadcast_in_dim.15.factors_ref, bf16[576,256]{1,0:T(8,128)(2,1)S(1)} %collective-permute-done.refs_0_, bf16[576,256]{1,0:T(8,128)(2,1)S(1)} %collective-permute-done.5.refs_1_, ...), custom_call_target="tpu_custom_call" | custom-call | flops 4563402752 | bytes 8912896 | tf_op jit(solution)/shard_map/attend_near/pallas_call | solution.py:245
  29.1 2.0 %collective-permute-start.9 = (bf16[576,256]{1,0:T(8,128)(2,1)S(1)}, bf16[576,256]{1,0:T(8,128)(2,1)S(1)}, u32[]{:S(2)}, u32[]{:S(2)}) collective-permute-start(bf16[576,256]{1,0:T(8,128)(2,1)S(1)} %collective-permute-done.8.refs_0_), channel_id=1, source_target_pairs={{0,1},{1,0},{2,3},{3,2},{4,5},{5,4},{6,7},{7,6},{8,9},{9,8},{10,11... | collective-permute-start | bytes 884744 | tf_op jit(solution)/shard_map/ppermute | solution.py:302
  31.1 0.2 collective-permute-start.11
  31.4 0.7 %collective-permute-done.12.refs_4_ = bf16[576,256]{1,0:T(8,128)(2,1)S(1)} collective-permute-done((bf16[576,256]{1,0:T(8,128)(2,1)S(1)}, bf16[576,256]{1,0:T(8,128)(2,1)S(1)}, u32[]{:S(2)}, u32[]{:S(2)}) %collective-permute-start.12) | collective-permute-done | bytes 294944 | tf_op jit(solution)/shard_map/ppermute | solution.py:305
  32.1 0.2 collective-permute-done.9.refs_1_
  32.3 0.4 %collective-permute-done.11.refs_3_ = bf16[576,256]{1,0:T(8,128)(2,1)S(1)} collective-permute-done((bf16[576,256]{1,0:T(8,128)(2,1)S(1)}, bf16[576,256]{1,0:T(8,128)(2,1)S(1)}, u32[]{:S(2)}, u32[]{:S(2)}) %collective-permute-start.11) | collective-permute-done | bytes 294944 | tf_op jit(solution)/shard_map/ppermute | solution.py:302
  32.8 9.0 %attend_rest.1 = bf16[4096,512]{1,0:T(8,128)(2,1)} custom-call(bf16[24,128]{1,0:T(8,128)(2,1)S(1)} %broadcast_in_dim.15.factors_ref, bf16[576,256]{1,0:T(8,128)(2,1)S(1)} %collective-permute-done.8.refs_0_, bf16[576,256]{1,0:T(8,128)(2,1)S(1)} %collective-permute-done.9.refs_1_, bf16[576,256]{1,0:T(8,128)(2,1)S(1)} %collective-permute-done.10.refs_2_, ...), custom_call_target="tpu_custom_call" | custom-call | flops 4563402752 | bytes 8912896 | tf_op jit(solution)/shard_map/attend_rest/pallas_call | solution.py:245
  (20 shorter events, 0.5 us)
Async XLA Ops:
  0.0 9.1 %collective-permute-start.2 = (bf16[576,256]{1,0:T(8,128)(2,1)}, bf16[576,256]{1,0:T(8,128)(2,1)S(1)}, u32[]{:S(2)}, u32[]{:S(2)}) collective-permute-start(bf16[576,256]{1,0:T(8,128)(2,1)} %bitcast.10), channel_id=1, source_target_pairs={{0,2},{1,3},{2,0},{3,1},{4,6},{5,7},{6,4},{7,5},{8,10},{9,11},{10,... | collective-permute-start | bytes 884744 | tf_op jit(solution)/shard_map/ppermute | solution.py:302
  1.2 9.7 %collective-permute-start = (bf16[576,256]{1,0:T(8,128)(2,1)}, bf16[576,256]{1,0:T(8,128)(2,1)S(1)}, u32[]{:S(2)}, u32[]{:S(2)}) collective-permute-start(bf16[576,256]{1,0:T(8,128)(2,1)} %bitcast.11), channel_id=1, source_target_pairs={{0,4},{1,5},{2,6},{3,7},{4,8},{5,9},{6,10},{7,11},{8,12},{9,13},{1... | collective-permute-start | bytes 884744 | tf_op jit(solution)/shard_map/ppermute | solution.py:305
  2.5 8.6 %collective-permute-start.1 = (s32[1,32]{1,0:T(1,128)}, s32[1,32]{1,0:T(1,128)S(1)}, u32[]{:S(2)}, u32[]{:S(2)}) collective-permute-start(s32[1,32]{1,0:T(1,128)} %param.5), channel_id=1, source_target_pairs={{12,0},{13,1},{14,2},{15,3},{28,16},{29,17},{30,18},{31,19}} | collective-permute-start | bytes 392 | tf_op jit(solution)/shard_map/ppermute | solution.py:316
  9.1 3.5 %collective-permute-start.3 = (bf16[576,256]{1,0:T(8,128)(2,1)S(1)}, bf16[576,256]{1,0:T(8,128)(2,1)S(1)}, u32[]{:S(2)}, u32[]{:S(2)}) collective-permute-start(bf16[576,256]{1,0:T(8,128)(2,1)S(1)} %stage.2.refs_0_), channel_id=1, source_target_pairs={{0,1},{1,0},{2,3},{3,2},{4,5},{5,4},{6,7},{7,6},{8,9},{9,8},{10,11... | collective-permute-start | bytes 884744 | tf_op jit(solution)/shard_map/ppermute | solution.py:302
  10.7 1.9 %collective-permute-start.4 = (bf16[576,256]{1,0:T(8,128)(2,1)S(1)}, bf16[576,256]{1,0:T(8,128)(2,1)S(1)}, u32[]{:S(2)}, u32[]{:S(2)}) collective-permute-start(bf16[576,256]{1,0:T(8,128)(2,1)S(1)} %collective-permute-done.2.refs_2_), channel_id=1, source_target_pairs={{0,1},{1,0},{2,3},{3,2},{4,5},{5,4},{6,7},{7,6},{8,9},{9,8},{10,11... | collective-permute-start | bytes 884744 | tf_op jit(solution)/shard_map/ppermute | solution.py:302
  10.9 6.6 %collective-permute-start.6 = (bf16[576,256]{1,0:T(8,128)(2,1)S(1)}, bf16[576,256]{1,0:T(8,128)(2,1)S(1)}, u32[]{:S(2)}, u32[]{:S(2)}) collective-permute-start(bf16[576,256]{1,0:T(8,128)(2,1)S(1)} %collective-permute-done.refs_0_), channel_id=1, source_target_pairs={{0,2},{1,3},{2,0},{3,1},{4,6},{5,7},{6,4},{7,5},{8,10},{9,11},{10,... | collective-permute-start | bytes 884744 | tf_op jit(solution)/shard_map/ppermute | solution.py:302
  11.3 10.3 %collective-permute-start.8 = (bf16[576,256]{1,0:T(8,128)(2,1)S(1)}, bf16[576,256]{1,0:T(8,128)(2,1)S(1)}, u32[]{:S(2)}, u32[]{:S(2)}) collective-permute-start(bf16[576,256]{1,0:T(8,128)(2,1)S(1)} %collective-permute-done.refs_0_), channel_id=1, source_target_pairs={{4,8},{5,9},{6,10},{7,11},{8,12},{9,13},{10,14},{11,15},{20,24},{2... | collective-permute-start | bytes 884744 | tf_op jit(solution)/shard_map/ppermute | solution.py:305
  17.5 4.1 %collective-permute-start.7 = (bf16[576,256]{1,0:T(8,128)(2,1)S(1)}, bf16[576,256]{1,0:T(8,128)(2,1)S(1)}, u32[]{:S(2)}, u32[]{:S(2)}) collective-permute-start(bf16[576,256]{1,0:T(8,128)(2,1)S(1)} %collective-permute-done.6.refs_2_), channel_id=1, source_target_pairs={{0,1},{1,0},{2,3},{3,2},{4,5},{5,4},{6,7},{7,6},{8,9},{9,8},{10,11... | collective-permute-start | bytes 884744 | tf_op jit(solution)/shard_map/ppermute | solution.py:302
  20.3 1.6 %collective-permute-start.5 = (bf16[576,256]{1,0:T(8,128)(2,1)S(1)}, bf16[576,256]{1,0:T(8,128)(2,1)S(1)}, u32[]{:S(2)}, u32[]{:S(2)}) collective-permute-start(bf16[576,256]{1,0:T(8,128)(2,1)S(1)} %collective-permute-done.refs_0_), channel_id=1, source_target_pairs={{0,1},{1,0},{2,3},{3,2},{4,5},{5,4},{6,7},{7,6},{8,9},{9,8},{10,11... | collective-permute-start | bytes 884744 | tf_op jit(solution)/shard_map/ppermute | solution.py:302
  20.4 11.8 %collective-permute-start.12 = (bf16[576,256]{1,0:T(8,128)(2,1)S(1)}, bf16[576,256]{1,0:T(8,128)(2,1)S(1)}, u32[]{:S(2)}, u32[]{:S(2)}) collective-permute-start(bf16[576,256]{1,0:T(8,128)(2,1)S(1)} %get-tuple-element.55), channel_id=1, source_target_pairs={{0,12},{1,13},{2,14},{3,15},{16,28},{17,29},{18,30},{19,31}} | collective-permute-start | bytes 884744 | tf_op jit(solution)/shard_map/ppermute | solution.py:305
  21.9 9.2 %collective-permute-start.10 = (bf16[576,256]{1,0:T(8,128)(2,1)S(1)}, bf16[576,256]{1,0:T(8,128)(2,1)S(1)}, u32[]{:S(2)}, u32[]{:S(2)}) collective-permute-start(bf16[576,256]{1,0:T(8,128)(2,1)S(1)} %collective-permute-done.8.refs_0_), channel_id=1, source_target_pairs={{0,2},{1,3},{2,0},{3,1},{4,6},{5,7},{6,4},{7,5},{8,10},{9,11},{10,... | collective-permute-start | bytes 884744 | tf_op jit(solution)/shard_map/ppermute | solution.py:302
  29.1 3.3 %collective-permute-start.9 = (bf16[576,256]{1,0:T(8,128)(2,1)S(1)}, bf16[576,256]{1,0:T(8,128)(2,1)S(1)}, u32[]{:S(2)}, u32[]{:S(2)}) collective-permute-start(bf16[576,256]{1,0:T(8,128)(2,1)S(1)} %collective-permute-done.8.refs_0_), channel_id=1, source_target_pairs={{0,1},{1,0},{2,3},{3,2},{4,5},{5,4},{6,7},{7,6},{8,9},{9,8},{10,11... | collective-permute-start | bytes 884744 | tf_op jit(solution)/shard_map/ppermute | solution.py:302
  31.1 1.6 %collective-permute-start.11 = (bf16[576,256]{1,0:T(8,128)(2,1)S(1)}, bf16[576,256]{1,0:T(8,128)(2,1)S(1)}, u32[]{:S(2)}, u32[]{:S(2)}) collective-permute-start(bf16[576,256]{1,0:T(8,128)(2,1)S(1)} %collective-permute-done.10.refs_2_), channel_id=1, source_target_pairs={{0,1},{1,0},{2,3},{3,2},{4,5},{5,4},{6,7},{7,6},{8,9},{9,8},{10,11... | collective-permute-start | bytes 884744 | tf_op jit(solution)/shard_map/ppermute | solution.py:302

commit v8 on v6

--- a/solution.py
+++ b/solution.py
@@ -333,9 +333,8 @@
     across = beside(cache1, 2)
     queries = queries.reshape(-1, shape[2])
     far, queries = lax.optimization_barrier((far, queries))
+    beside1 = beside(cache1, 1)
     (queries,) = stage(queries)
-    cache1, queries = lax.optimization_barrier((cache1, queries))
-    beside1 = beside(cache1, 1)
     across, far, queries = lax.optimization_barrier((across, far, queries))
     far = further(far, DEPTH - 1, range(ROW))
     row1 = [cache1, beside1, across, beside(across, 1)]

time: 42.3 us -> 42.3 us (level)
  waiting for transfers between devices: 3.09 us -> 1.68 us
  starting transfers between devices: 16.1 us -> 17.5 us
    ppermute x9, waiting for transfers between devices: 2.24 us -> 0.06 us  [beside(): return lax.ppermute(array, 'ctx', [(i, i ^ m) for i in range(size)])]
    ppermute x9, starting transfers between devices: 8.42 us -> 9.83 us  [beside(): return lax.ppermute(array, 'ctx', [(i, i ^ m) for i in range(size)])]
    ppermute x3, waiting for transfers between devices: 0.84 us -> 1.62 us  [further(): return lax.ppermute(array, 'ctx', [(i, i + ROW * rows) for i in sources])]
  transfers between devices with their start and end apart: 13 -> 13, of which waited for: 5 -> 2; matrix products, arithmetic and copies ran while one was open for 5% -> 5% of each run, Pallas kernels for 27% -> 27%
where the time goes in v8:
time: 42.3 us; the launch traced here: 41.9 us
  Pallas kernels  20.4 us (48%)
  starting transfers between devices  17.5 us (41%)
  other arithmetic  1.76 us (4%)
  waiting for transfers between devices  1.68 us (4%)
    pallas_call x2, Pallas kernels, attend(): pl.pallas_call(kernel, in_specs=[vmem] * (len(tiles) + 2 + len(state)), o...  15.8 us
    ppermute x9, starting transfers between devices, beside(): return lax.ppermute(array, 'ctx', [(i, i ^ m) for i in range(size)])  9.83 us
    ppermute x3, starting transfers between devices, further(): return lax.ppermute(array, 'ctx', [(i, i + ROW * rows) for i in sources])  3.86 us
    ppermute x1, starting transfers between devices, shards_rows(): lax.ppermute(tile_lists, 'ctx', [(i + span, i) for i in range(ROW)])  3.78 us
    pallas_call x2, Pallas kernels, stage(): pl.pallas_call(stage_kernel, in_specs=[pl.BlockSpec(memory_space=pltpu.HB...  3.56 us
    ppermute x3, waiting for transfers between devices, further(): return lax.ppermute(array, 'ctx', [(i, i + ROW * rows) for i in sources])  1.62 us
    reduce_sum x2, other arithmetic, named_tiles(): return jnp.sum(jnp.where(hit, tile, 0), axis=1)  1.03 us
    pallas_call x1, Pallas kernels, pick_tiles(): pl.pallas_call(pick_kernel, in_specs=[pl.BlockSpec(memory_space=pltpu.SME...  1.01 us
  transfers between devices with their start and end apart: 13, of which 2 were waited for; matrix products, arithmetic and copies ran while one was open for 5% of the time, Pallas kernels for 27%

profile of v8, /device:TPU:25, one launch (start us, length us, event | category | flops | bytes accessed | tf_op | source)
XLA Modules:
  0.0 41.9 jit_solution(12026312054316527822)
XLA Ops:
  0.0 1.2 %collective-permute-start.4 = (bf16[576,256]{1,0:T(8,128)(2,1)}, bf16[576,256]{1,0:T(8,128)(2,1)S(1)}, u32[]{:S(2)}, u32[]{:S(2)}) collective-permute-start(bf16[576,256]{1,0:T(8,128)(2,1)} %bitcast.10), channel_id=1, source_target_pairs={{0,2},{1,3},{2,0},{3,1},{4,6},{5,7},{6,4},{7,5},{8,10},{9,11},{10,... | collective-permute-start | bytes 884744 | tf_op jit(solution)/shard_map/ppermute | solution.py:302
  1.2 1.3 %collective-permute-start = (bf16[576,256]{1,0:T(8,128)(2,1)}, bf16[576,256]{1,0:T(8,128)(2,1)S(1)}, u32[]{:S(2)}, u32[]{:S(2)}) collective-permute-start(bf16[576,256]{1,0:T(8,128)(2,1)} %bitcast.11), channel_id=1, source_target_pairs={{0,4},{1,5},{2,6},{3,7},{4,8},{5,9},{6,10},{7,11},{8,12},{9,13},{1... | collective-permute-start | bytes 884744 | tf_op jit(solution)/shard_map/ppermute | solution.py:305
  2.5 3.8 %collective-permute-start.3 = (s32[1,32]{1,0:T(1,128)}, s32[1,32]{1,0:T(1,128)S(1)}, u32[]{:S(2)}, u32[]{:S(2)}) collective-permute-start(s32[1,32]{1,0:T(1,128)} %param.5), channel_id=1, source_target_pairs={{12,0},{13,1},{14,2},{15,3},{28,16},{29,17},{30,18},{31,19}} | collective-permute-start | bytes 392 | tf_op jit(solution)/shard_map/ppermute | solution.py:316
  6.3 0.7 %compare_bitcast_fusion.1 = pred[32]{0:T(512)(128)(4,1)S(1)} fusion(s32[1,32]{1,0:T(1,128)} %param.5), kind=kLoop, calls=%fused_computation.29 | loop fusion | flops 32 | bytes 160 | tf_op jit(solution)/shard_map/and | solution.py:309
  7.0 1.0 %stage.2.refs_0_ = bf16[576,256]{1,0:T(8,128)(2,1)S(1)} custom-call(bf16[576,256]{1,0:T(8,128)(2,1)} %bitcast.12), custom_call_target="tpu_custom_call" | custom-call | bytes 589824 | tf_op jit(solution)/shard_map/stage/pallas_call | solution.py:281
  8.1 0.8 %fusion.3.own_ref = s32[12]{0:T(128)S(1)} fusion(s32[12]{0:T(128)S(1)} %fusion.13, s32[32]{0:T(128)} %bitcast.13, pred[32]{0:T(512)(128)(4,1)S(1)} %compare_bitcast_fusion.1), kind=kLoop, calls=%fused_computation.7 | loop fusion | flops 2676 | bytes 256 | tf_op jit(solution)/shard_map/reduce_sum | solution.py:310
  9.0 0.1 reshape.136
  9.1 1.6 %collective-permute-start.5 = (bf16[576,256]{1,0:T(8,128)(2,1)S(1)}, bf16[576,256]{1,0:T(8,128)(2,1)S(1)}, u32[]{:S(2)}, u32[]{:S(2)}) collective-permute-start(bf16[576,256]{1,0:T(8,128)(2,1)S(1)} %stage.2.refs_0_), channel_id=1, source_target_pairs={{0,1},{1,0},{2,3},{3,2},{4,5},{5,4},{6,7},{7,6},{8,9},{9,8},{10,11... | collective-permute-start | bytes 884744 | tf_op jit(solution)/shard_map/ppermute | solution.py:302
  10.7 0.1 collective-permute-start.6
  10.8 0.1 collective-permute-done.refs_0_
  10.9 0.2 collective-permute-start.2
  11.1 0.2 fusion.6.sel_ref
  11.3 1.3 %collective-permute-start.8 = (bf16[576,256]{1,0:T(8,128)(2,1)S(1)}, bf16[576,256]{1,0:T(8,128)(2,1)S(1)}, u32[]{:S(2)}, u32[]{:S(2)}) collective-permute-start(bf16[576,256]{1,0:T(8,128)(2,1)S(1)} %collective-permute-done.refs_0_), channel_id=1, source_target_pairs={{4,8},{5,9},{6,10},{7,11},{8,12},{9,13},{10,14},{11,15},{20,24},{2... | collective-permute-start | bytes 884744 | tf_op jit(solution)/shard_map/ppermute | solution.py:305
  12.6 2.2 %collective-permute-start.1 = (bf16[576,256]{1,0:T(8,128)(2,1)S(1)}, bf16[576,256]{1,0:T(8,128)(2,1)S(1)}, u32[]{:S(2)}, u32[]{:S(2)}) collective-permute-start(bf16[576,256]{1,0:T(8,128)(2,1)S(1)} %collective-permute-done.refs_0_), channel_id=1, source_target_pairs={{0,1},{1,0},{2,3},{3,2},{4,5},{5,4},{6,7},{7,6},{8,9},{9,8},{10,11... | collective-permute-start | bytes 884744 | tf_op jit(solution)/shard_map/ppermute | solution.py:302
  14.8 1.0 %pick_tiles.1 = (bf16[576,256]{1,0:T(8,128)(2,1)S(1)}, bf16[576,256]{1,0:T(8,128)(2,1)S(1)}) custom-call(s32[4]{0:T(128)S(1)} %fusion.6.sel_ref, s32[12]{0:T(128)S(1)} %fusion.3.own_ref, bf16[576,256]{1,0:T(8,128)(2,1)S(1)} %stage.2.refs_0_, bf16[576,256]{1,0:T(8,128)(2,1)S(1)} %collective-permute-done.5.refs_1_, ...), custom_call_target="tpu_custom_call" | custom-call | bytes 1179648 | tf_op jit(solution)/shard_map/pick_tiles/pallas_call | solution.py:124
  15.8 2.5 %stage.3.refs_6_.refs_5_ = bf16[4096,576]{1,0:T(8,128)(2,1)S(1)} custom-call(bf16[4096,576]{1,0:T(8,128)(2,1)} %bitcast.9), custom_call_target="tpu_custom_call" | custom-call | bytes 9437184 | tf_op jit(solution)/shard_map/stage/pallas_call | solution.py:281
  18.4 1.9 %collective-permute-start.7 = (bf16[576,256]{1,0:T(8,128)(2,1)S(1)}, bf16[576,256]{1,0:T(8,128)(2,1)S(1)}, u32[]{:S(2)}, u32[]{:S(2)}) collective-permute-start(bf16[576,256]{1,0:T(8,128)(2,1)S(1)} %collective-permute-done.2.refs_2_), channel_id=1, source_target_pairs={{0,1},{1,0},{2,3},{3,2},{4,5},{5,4},{6,7},{7,6},{8,9},{9,8},{10,11... | collective-permute-start | bytes 884744 | tf_op jit(solution)/shard_map/ppermute | solution.py:302
  20.3 1.3 %collective-permute-start.12 = (bf16[576,256]{1,0:T(8,128)(2,1)S(1)}, bf16[576,256]{1,0:T(8,128)(2,1)S(1)}, u32[]{:S(2)}, u32[]{:S(2)}) collective-permute-start(bf16[576,256]{1,0:T(8,128)(2,1)S(1)} %get-tuple-element.43), channel_id=1, source_target_pairs={{0,12},{1,13},{2,14},{3,15},{16,28},{17,29},{18,30},{19,31}} | collective-permute-start | bytes 884744 | tf_op jit(solution)/shard_map/ppermute | solution.py:305
  21.7 0.3 collective-permute-start.10
  22.0 2.2 %collective-permute-start.9 = (bf16[576,256]{1,0:T(8,128)(2,1)S(1)}, bf16[576,256]{1,0:T(8,128)(2,1)S(1)}, u32[]{:S(2)}, u32[]{:S(2)}) collective-permute-start(bf16[576,256]{1,0:T(8,128)(2,1)S(1)} %collective-permute-done.8.refs_0_), channel_id=1, source_target_pairs={{0,1},{1,0},{2,3},{3,2},{4,5},{5,4},{6,7},{7,6},{8,9},{9,8},{10,11... | collective-permute-start | bytes 884744 | tf_op jit(solution)/shard_map/ppermute | solution.py:302
  24.2 6.8 %attend_near.1 = (bf16[4096,512]{1,0:T(8,128)(2,1)S(1)}, f32[4096,128]{1,0:T(8,128)S(1)}, f32[4096,128]{1,0:T(8,128)S(1)}) custom-call(bf16[24,128]{1,0:T(8,128)(2,1)S(1)} %broadcast_in_dim.15.factors_ref, bf16[576,256]{1,0:T(8,128)(2,1)S(1)} %collective-permute-done.refs_0_, bf16[576,256]{1,0:T(8,128)(2,1)S(1)} %collective-permute-done.1.refs_1_, ...), custom_call_target="tpu_custom_call" | custom-call | flops 4563402752 | bytes 8912896 | tf_op jit(solution)/shard_map/attend_near/pallas_call | solution.py:245
  31.1 0.1 collective-permute-start.11
  31.2 1.5 %collective-permute-done.12.refs_4_ = bf16[576,256]{1,0:T(8,128)(2,1)S(1)} collective-permute-done((bf16[576,256]{1,0:T(8,128)(2,1)S(1)}, bf16[576,256]{1,0:T(8,128)(2,1)S(1)}, u32[]{:S(2)}, u32[]{:S(2)}) %collective-permute-start.12) | collective-permute-done | bytes 294944 | tf_op jit(solution)/shard_map/ppermute | solution.py:305
  32.7 9.0 %attend_rest.1 = bf16[4096,512]{1,0:T(8,128)(2,1)} custom-call(bf16[24,128]{1,0:T(8,128)(2,1)S(1)} %broadcast_in_dim.15.factors_ref, bf16[576,256]{1,0:T(8,128)(2,1)S(1)} %collective-permute-done.8.refs_0_, bf16[576,256]{1,0:T(8,128)(2,1)S(1)} %collective-permute-done.9.refs_1_, bf16[576,256]{1,0:T(8,128)(2,1)S(1)} %collective-permute-done.10.refs_2_, ...), custom_call_target="tpu_custom_call" | custom-call | flops 4563402752 | bytes 8912896 | tf_op jit(solution)/shard_map/attend_rest/pallas_call | solution.py:245
  (20 shorter events, 0.3 us)
Async XLA Ops:
  0.0 9.1 %collective-permute-start.4 = (bf16[576,256]{1,0:T(8,128)(2,1)}, bf16[576,256]{1,0:T(8,128)(2,1)S(1)}, u32[]{:S(2)}, u32[]{:S(2)}) collective-permute-start(bf16[576,256]{1,0:T(8,128)(2,1)} %bitcast.10), channel_id=1, source_target_pairs={{0,2},{1,3},{2,0},{3,1},{4,6},{5,7},{6,4},{7,5},{8,10},{9,11},{10,... | collective-permute-start | bytes 884744 | tf_op jit(solution)/shard_map/ppermute | solution.py:302
  1.2 9.7 %collective-permute-start = (bf16[576,256]{1,0:T(8,128)(2,1)}, bf16[576,256]{1,0:T(8,128)(2,1)S(1)}, u32[]{:S(2)}, u32[]{:S(2)}) collective-permute-start(bf16[576,256]{1,0:T(8,128)(2,1)} %bitcast.11), channel_id=1, source_target_pairs={{0,4},{1,5},{2,6},{3,7},{4,8},{5,9},{6,10},{7,11},{8,12},{9,13},{1... | collective-permute-start | bytes 884744 | tf_op jit(solution)/shard_map/ppermute | solution.py:305
  2.5 8.6 %collective-permute-start.3 = (s32[1,32]{1,0:T(1,128)}, s32[1,32]{1,0:T(1,128)S(1)}, u32[]{:S(2)}, u32[]{:S(2)}) collective-permute-start(s32[1,32]{1,0:T(1,128)} %param.5), channel_id=1, source_target_pairs={{12,0},{13,1},{14,2},{15,3},{28,16},{29,17},{30,18},{31,19}} | collective-permute-start | bytes 392 | tf_op jit(solution)/shard_map/ppermute | solution.py:316
  9.1 5.7 %collective-permute-start.5 = (bf16[576,256]{1,0:T(8,128)(2,1)S(1)}, bf16[576,256]{1,0:T(8,128)(2,1)S(1)}, u32[]{:S(2)}, u32[]{:S(2)}) collective-permute-start(bf16[576,256]{1,0:T(8,128)(2,1)S(1)} %stage.2.refs_0_), channel_id=1, source_target_pairs={{0,1},{1,0},{2,3},{3,2},{4,5},{5,4},{6,7},{7,6},{8,9},{9,8},{10,11... | collective-permute-start | bytes 884744 | tf_op jit(solution)/shard_map/ppermute | solution.py:302
  10.7 4.1 %collective-permute-start.6 = (bf16[576,256]{1,0:T(8,128)(2,1)S(1)}, bf16[576,256]{1,0:T(8,128)(2,1)S(1)}, u32[]{:S(2)}, u32[]{:S(2)}) collective-permute-start(bf16[576,256]{1,0:T(8,128)(2,1)S(1)} %collective-permute-done.4.refs_2_), channel_id=1, source_target_pairs={{0,1},{1,0},{2,3},{3,2},{4,5},{5,4},{6,7},{7,6},{8,9},{9,8},{10,11... | collective-permute-start | bytes 884744 | tf_op jit(solution)/shard_map/ppermute | solution.py:302
  10.9 7.5 %collective-permute-start.2 = (bf16[576,256]{1,0:T(8,128)(2,1)S(1)}, bf16[576,256]{1,0:T(8,128)(2,1)S(1)}, u32[]{:S(2)}, u32[]{:S(2)}) collective-permute-start(bf16[576,256]{1,0:T(8,128)(2,1)S(1)} %collective-permute-done.refs_0_), channel_id=1, source_target_pairs={{0,2},{1,3},{2,0},{3,1},{4,6},{5,7},{6,4},{7,5},{8,10},{9,11},{10,... | collective-permute-start | bytes 884744 | tf_op jit(solution)/shard_map/ppermute | solution.py:302
  11.3 10.3 %collective-permute-start.8 = (bf16[576,256]{1,0:T(8,128)(2,1)S(1)}, bf16[576,256]{1,0:T(8,128)(2,1)S(1)}, u32[]{:S(2)}, u32[]{:S(2)}) collective-permute-start(bf16[576,256]{1,0:T(8,128)(2,1)S(1)} %collective-permute-done.refs_0_), channel_id=1, source_target_pairs={{4,8},{5,9},{6,10},{7,11},{8,12},{9,13},{10,14},{11,15},{20,24},{2... | collective-permute-start | bytes 884744 | tf_op jit(solution)/shard_map/ppermute | solution.py:305
  12.6 9.1 %collective-permute-start.1 = (bf16[576,256]{1,0:T(8,128)(2,1)S(1)}, bf16[576,256]{1,0:T(8,128)(2,1)S(1)}, u32[]{:S(2)}, u32[]{:S(2)}) collective-permute-start(bf16[576,256]{1,0:T(8,128)(2,1)S(1)} %collective-permute-done.refs_0_), channel_id=1, source_target_pairs={{0,1},{1,0},{2,3},{3,2},{4,5},{5,4},{6,7},{7,6},{8,9},{9,8},{10,11... | collective-permute-start | bytes 884744 | tf_op jit(solution)/shard_map/ppermute | solution.py:302
  18.4 3.3 %collective-permute-start.7 = (bf16[576,256]{1,0:T(8,128)(2,1)S(1)}, bf16[576,256]{1,0:T(8,128)(2,1)S(1)}, u32[]{:S(2)}, u32[]{:S(2)}) collective-permute-start(bf16[576,256]{1,0:T(8,128)(2,1)S(1)} %collective-permute-done.2.refs_2_), channel_id=1, source_target_pairs={{0,1},{1,0},{2,3},{3,2},{4,5},{5,4},{6,7},{7,6},{8,9},{9,8},{10,11... | collective-permute-start | bytes 884744 | tf_op jit(solution)/shard_map/ppermute | solution.py:302
  20.3 12.3 %collective-permute-start.12 = (bf16[576,256]{1,0:T(8,128)(2,1)S(1)}, bf16[576,256]{1,0:T(8,128)(2,1)S(1)}, u32[]{:S(2)}, u32[]{:S(2)}) collective-permute-start(bf16[576,256]{1,0:T(8,128)(2,1)S(1)} %get-tuple-element.43), channel_id=1, source_target_pairs={{0,12},{1,13},{2,14},{3,15},{16,28},{17,29},{18,30},{19,31}} | collective-permute-start | bytes 884744 | tf_op jit(solution)/shard_map/ppermute | solution.py:305
  21.7 9.4 %collective-permute-start.10 = (bf16[576,256]{1,0:T(8,128)(2,1)S(1)}, bf16[576,256]{1,0:T(8,128)(2,1)S(1)}, u32[]{:S(2)}, u32[]{:S(2)}) collective-permute-start(bf16[576,256]{1,0:T(8,128)(2,1)S(1)} %collective-permute-done.8.refs_0_), channel_id=1, source_target_pairs={{0,2},{1,3},{2,0},{3,1},{4,6},{5,7},{6,4},{7,5},{8,10},{9,11},{10,... | collective-permute-start | bytes 884744 | tf_op jit(solution)/shard_map/ppermute | solution.py:302
  22.0 10.7 %collective-permute-start.9 = (bf16[576,256]{1,0:T(8,128)(2,1)S(1)}, bf16[576,256]{1,0:T(8,128)(2,1)S(1)}, u32[]{:S(2)}, u32[]{:S(2)}) collective-permute-start(bf16[576,256]{1,0:T(8,128)(2,1)S(1)} %collective-permute-done.8.refs_0_), channel_id=1, source_target_pairs={{0,1},{1,0},{2,3},{3,2},{4,5},{5,4},{6,7},{7,6},{8,9},{9,8},{10,11... | collective-permute-start | bytes 884744 | tf_op jit(solution)/shard_map/ppermute | solution.py:302
  31.1 1.6 %collective-permute-start.11 = (bf16[576,256]{1,0:T(8,128)(2,1)S(1)}, bf16[576,256]{1,0:T(8,128)(2,1)S(1)}, u32[]{:S(2)}, u32[]{:S(2)}) collective-permute-start(bf16[576,256]{1,0:T(8,128)(2,1)S(1)} %collective-permute-done.10.refs_2_), channel_id=1, source_target_pairs={{0,1},{1,0},{2,3},{3,2},{4,5},{5,4},{6,7},{7,6},{8,9},{9,8},{10,11... | collective-permute-start | bytes 884744 | tf_op jit(solution)/shard_map/ppermute | solution.py:302
